TPU v7x, 32 devices: a whole 2x2x4 slice. The times are simulated.
32 devices in a mesh: ctx: 8 (over y, x, core), wa: 4 (over z).
Axes of the slice: x: 2, y: 2, z: 4, core: 2. Of those that a mesh axis runs over, the one named last changes fastest.
Arguments:
- hidden: bfloat16 [4, 2048, 512], P('wa', 'ctx'), may hold values from -6 to 6
- stream: bfloat16 [4, 2048, 512], P('wa', 'ctx'), may hold values from -6 to 6
- encoder: bfloat16 [4, 2048, 512], P('wa', 'ctx'), may hold values from -6 to 6
- lengths: int32 [4, 4], P('wa'), may hold values from 1 to 1024, 2048 in all within a row
- order: int32 [4, 2048], P('wa'), may hold values from 0 to 2047, each once within a row
- ranks: int32 [4, 2048], P('wa'), may hold values from 0 to 1023
- thresholds: int32 [4, 2048], P('wa'), may hold values from 1 to 1024
- self_query: bfloat16 [512, 512], P('wa'), may hold values from -0.25 to 0.25
- self_key_value: bfloat16 [512, 1024], P('wa'), may hold values from -0.25 to 0.25
- self_output: bfloat16 [512, 512], P('wa'), may hold values from -1 to 1
- cross_query: bfloat16 [512, 512], P('wa'), may hold values from -0.25 to 0.25
- cross_key_value: bfloat16 [512, 1024], P('wa'), may hold values from -0.25 to 0.25
- cross_output: bfloat16 [512, 512], P('wa'), may hold values from -1 to 1
- ffn_in: bfloat16 [512, 2048], P('wa'), may hold values from -0.25 to 0.25
- ffn_out: bfloat16 [2048, 512], P('wa'), may hold values from -0.1875 to 0.1875
- norm_gain: bfloat16 [3, 512], P(None, 'wa'), may hold values from 0.5 to 1.5
- norm_shift: bfloat16 [3, 512], P(None, 'wa'), may hold values from -2 to 2
- cotangent: bfloat16 [4, 2048, 512], P('wa', 'ctx'), may hold values from -6 to 6
Outputs:
- layer_out: bfloat16 [4, 2048, 512], P('wa', 'ctx')
- hidden_grad: float32 [4, 2048, 512], P('wa', 'ctx')
- stream_grad: float32 [4, 2048, 512], P('wa', 'ctx')
- encoder_grad: float32 [4, 2048, 512], P('wa', 'ctx')
- self_query_grad: float32 [512, 512], P('wa')
- self_key_value_grad: float32 [512, 1024], P('wa')
- self_output_grad: float32 [512, 512], P('wa')
- cross_query_grad: float32 [512, 512], P('wa')
- cross_key_value_grad: float32 [512, 1024], P('wa')
- cross_output_grad: float32 [512, 512], P('wa')
- ffn_in_grad: float32 [512, 2048], P('wa')
- ffn_out_grad: float32 [2048, 512], P('wa')
- norm_gain_grad: float32 [3, 512], P(None, 'wa')
- norm_shift_grad: float32 [3, 512], P(None, 'wa')
All inputs are finite; a program needn't handle non-finite values.
Results may differ from a plain program's by a relative error of at most 0.022.
Values may be sent and summed in bfloat16 or wider, within the bound.
No kernel may reach another device: no remote copies, remote signals or barrier semaphores. Data moves between devices by JAX's collectives and lax.ppermute only.
A program may use at most 384 MiB of HBM per device.

v0:
```python
import jax
import jax.numpy as jnp
from jax import lax
from jax.sharding import PartitionSpec as P

D = 512
HEADS = 8
HEAD = 64
KEYBLK = 1024


layer_eps = 1e-05
neg_fill = -1e30


def sequence_ids(positions, seq_ends):
    return jnp.sum((positions[:, None] >= seq_ends[None, :]).astype(jnp.int32), axis=1)


def head_split(matrix):
    return matrix.reshape(matrix.shape[0], HEADS, HEAD)


def block_scores(query_heads, key_heads):
    raw_scores = jnp.einsum(
        "lhd,khd->hlk", query_heads, key_heads, preferred_element_type=jnp.float32
    )
    return raw_scores * float(HEAD) ** (-0.5)


def softmax_totals(queries, key_rows, allowed_fn):
    query_heads = head_split(queries)
    count_rows = queries.shape[0]

    def visit(state_pair, block_index):
        running_top, running_sum = state_pair
        block_start = block_index * KEYBLK
        key_piece = lax.dynamic_slice_in_dim(key_rows, block_start, KEYBLK, 0)
        allowed = allowed_fn(block_start)[None]
        scores = jnp.where(
            allowed, block_scores(query_heads, head_split(key_piece[:, :D])), neg_fill
        )
        new_top = jnp.maximum(running_top, jnp.max(scores, axis=2))
        weights = jnp.where(allowed, jnp.exp(scores - new_top[:, :, None]), 0.0)
        running_sum = running_sum * jnp.exp(running_top - new_top) + jnp.sum(weights, axis=2)
        return ((new_top, running_sum), None)

    initial = (
        jnp.full((HEADS, count_rows), neg_fill, jnp.float32),
        jnp.zeros((HEADS, count_rows), jnp.float32),
    )
    (final_top, final_sum), unused = lax.scan(
        visit, initial, jnp.arange(key_rows.shape[0] // KEYBLK)
    )
    return final_top + jnp.log(final_sum)


def attend_values(queries, key_rows, log_totals, allowed_fn):
    query_heads = head_split(queries)

    def visit(running, block_index):
        block_start = block_index * KEYBLK
        key_piece = lax.dynamic_slice_in_dim(key_rows, block_start, KEYBLK, 0)
        allowed = allowed_fn(block_start)[None]
        scores = block_scores(query_heads, head_split(key_piece[:, :D]))
        weights = jnp.where(allowed, jnp.exp(scores - log_totals[:, :, None]), 0.0)
        value_heads = head_split(key_piece[:, D:])
        return (
            running
            + jnp.einsum(
                "hlk,khd->lhd",
                weights.astype(jnp.bfloat16),
                value_heads,
                preferred_element_type=jnp.float32,
            ),
            None,
        )

    mixed, unused = lax.scan(
        visit, jnp.zeros(query_heads.shape, jnp.float32), jnp.arange(key_rows.shape[0] // KEYBLK)
    )
    return mixed.reshape(queries.shape[0], D)


def head_offsets(grad_low, attended):
    return jnp.sum(head_split(grad_low.astype(jnp.float32) * attended), axis=2).T


def attend_back(queries, key_rows, log_totals, attended, grad_low, allowed_fn):
    query_heads = head_split(queries)
    grad_heads = head_split(grad_low)
    offsets = head_offsets(grad_low, attended)
    scale_value = float(HEAD) ** (-0.5)

    def visit(query_grad, block_index):
        block_start = block_index * KEYBLK
        key_piece = lax.dynamic_slice_in_dim(key_rows, block_start, KEYBLK, 0)
        allowed = allowed_fn(block_start)[None]
        key_heads = head_split(key_piece[:, :D])
        value_heads = head_split(key_piece[:, D:])
        weights = jnp.where(
            allowed, jnp.exp(block_scores(query_heads, key_heads) - log_totals[:, :, None]), 0.0
        )
        value_grad = jnp.einsum(
            "hlk,lhd->khd",
            weights.astype(jnp.bfloat16),
            grad_heads,
            preferred_element_type=jnp.float32,
        )
        weight_grad = jnp.einsum(
            "lhd,khd->hlk", grad_heads, value_heads, preferred_element_type=jnp.float32
        )
        score_grad = (weights * (weight_grad - offsets[:, :, None]) * scale_value).astype(
            jnp.bfloat16
        )
        query_grad = query_grad + jnp.einsum(
            "hlk,khd->lhd", score_grad, key_heads, preferred_element_type=jnp.float32
        )
        key_grad = jnp.einsum(
            "hlk,lhd->khd", score_grad, query_heads, preferred_element_type=jnp.float32
        )
        return (
            query_grad,
            jnp.concatenate((key_grad.reshape(KEYBLK, D), value_grad.reshape(KEYBLK, D)), axis=1),
        )

    query_grad, grad_pieces = lax.scan(
        visit, jnp.zeros(query_heads.shape, jnp.float32), jnp.arange(key_rows.shape[0] // KEYBLK)
    )
    return (query_grad.reshape(queries.shape[0], D), grad_pieces.reshape(key_rows.shape[0], 2 * D))


def normalize(values, gain_row, shift_row):
    row_mean = jnp.mean(values, axis=1, keepdims=True)
    centred = values - row_mean
    scale_inv = lax.rsqrt(jnp.mean(centred * centred, axis=1, keepdims=True) + layer_eps)
    normed = centred * scale_inv
    return (normed * gain_row + shift_row, normed, scale_inv)


def normalize_back(grad_out, normed, scale_inv, gain_row):
    gain_term = jnp.sum(grad_out * normed, axis=0)
    shift_term = jnp.sum(grad_out, axis=0)
    scaled = grad_out * gain_row
    grad_in = scale_inv * (
        scaled
        - jnp.mean(scaled, axis=1, keepdims=True)
        - normed * jnp.mean(scaled * normed, axis=1, keepdims=True)
    )
    return (grad_in, gain_term, shift_term)


def matmul(left, right):
    return jnp.dot(left, right, preferred_element_type=jnp.float32)


def shards(
    hidden,
    stream,
    encoder,
    lengths,
    order,
    ranks,
    thresholds,
    self_query,
    self_key_value,
    self_output,
    cross_query,
    cross_key_value,
    cross_output,
    ffn_in,
    ffn_out,
    norm_gain,
    norm_shift,
    cotangent,
):
    (
        full_query,
        full_pair,
        full_output,
        full_cross_query,
        full_cross_pair,
        full_cross_output,
        full_in,
        full_out,
        gain_rows,
        shift_rows,
    ) = (
        lax.all_gather(self_query, "wa", axis=0, tiled=True),
        lax.all_gather(self_key_value, "wa", axis=0, tiled=True),
        lax.all_gather(self_output, "wa", axis=0, tiled=True),
        lax.all_gather(cross_query, "wa", axis=0, tiled=True),
        lax.all_gather(cross_key_value, "wa", axis=0, tiled=True),
        lax.all_gather(cross_output, "wa", axis=0, tiled=True),
        lax.all_gather(ffn_in, "wa", axis=0, tiled=True),
        lax.all_gather(ffn_out, "wa", axis=0, tiled=True),
        lax.all_gather(norm_gain, "wa", axis=1, tiled=True),
        lax.all_gather(norm_shift, "wa", axis=1, tiled=True),
    )
    gains = gain_rows.astype(jnp.float32)
    shifts = shift_rows.astype(jnp.float32)
    local_rows = hidden.shape[1]
    total_rows = order.shape[1]
    row_start = lax.axis_index("ctx") * local_rows
    seq_ends = jnp.cumsum(lengths[0])
    token_seq = sequence_ids(order[0], seq_ends)
    source_seq = sequence_ids(jnp.arange(total_rows, dtype=jnp.int32), seq_ends)
    query_seq = lax.dynamic_slice_in_dim(token_seq, row_start, local_rows)
    query_rows = row_start + jnp.arange(local_rows, dtype=jnp.int32)
    all_limits = thresholds[0]
    limits = lax.dynamic_slice_in_dim(all_limits, row_start, local_rows)
    key_ranks = ranks[0]

    def self_allowed(block_start):
        block_seq = lax.dynamic_slice_in_dim(token_seq, block_start, KEYBLK)
        block_rank = lax.dynamic_slice_in_dim(key_ranks, block_start, KEYBLK)
        block_rows = block_start + jnp.arange(KEYBLK, dtype=jnp.int32)
        return (query_seq[:, None] == block_seq[None, :]) & (
            (block_rank[None, :] < limits[:, None]) | (query_rows[:, None] == block_rows[None, :])
        )

    def cross_allowed(block_start):
        return (
            query_seq[:, None] == lax.dynamic_slice_in_dim(source_seq, block_start, KEYBLK)[None, :]
        )

    inputs = hidden[0]
    stream_rows = stream[0]
    source_rows = encoder[0]
    queries = matmul(inputs, full_query).astype(jnp.bfloat16)
    self_local = matmul(stream_rows, full_pair).astype(jnp.bfloat16)
    cross_local = matmul(source_rows, full_cross_pair).astype(jnp.bfloat16)
    self_keys, cross_keys = (
        lax.all_gather(self_local, "ctx", axis=0, tiled=True),
        lax.all_gather(cross_local, "ctx", axis=0, tiled=True),
    )
    self_totals = softmax_totals(queries, self_keys, self_allowed)
    self_mixed = attend_values(queries, self_keys, self_totals, self_allowed)
    self_low = self_mixed.astype(jnp.bfloat16)
    first, first_normed, first_scale = normalize(
        inputs.astype(jnp.float32) + matmul(self_low, full_output), gains[0], shifts[0]
    )
    first_low = first.astype(jnp.bfloat16)
    cross_queries = matmul(first_low, full_cross_query).astype(jnp.bfloat16)
    cross_totals = softmax_totals(cross_queries, cross_keys, cross_allowed)
    cross_mixed = attend_values(cross_queries, cross_keys, cross_totals, cross_allowed)
    cross_low = cross_mixed.astype(jnp.bfloat16)
    second, second_normed, second_scale = normalize(
        first + matmul(cross_low, full_cross_output), gains[1], shifts[1]
    )
    second_low = second.astype(jnp.bfloat16)
    hidden_pre = matmul(second_low, full_in)
    sigmoid_pre = jax.nn.sigmoid(hidden_pre)
    activated = (hidden_pre * sigmoid_pre).astype(jnp.bfloat16)
    result, third_normed, third_scale = normalize(
        second + matmul(activated, full_out), gains[2], shifts[2]
    )
    third_grad, gain_grad_c, shift_grad_c = normalize_back(
        cotangent[0].astype(jnp.float32), third_normed, third_scale, gains[2]
    )
    branch_grad = third_grad.astype(jnp.bfloat16)
    grad_ffn_out = matmul(activated.T, branch_grad)
    slope = sigmoid_pre * (1.0 + hidden_pre * (1.0 - sigmoid_pre))
    pre_grad = (matmul(branch_grad, full_out.T) * slope).astype(jnp.bfloat16)
    grad_ffn_in = matmul(second_low.T, pre_grad)
    second_total = third_grad + matmul(pre_grad, full_in.T)
    second_grad, gain_grad_b, shift_grad_b = normalize_back(
        second_total, second_normed, second_scale, gains[1]
    )
    cross_branch = second_grad.astype(jnp.bfloat16)
    grad_cross_output = matmul(cross_low.T, cross_branch)
    cross_mixed_grad = matmul(cross_branch, full_cross_output.T).astype(jnp.bfloat16)
    cross_query_term, cross_terms = attend_back(
        cross_queries, cross_keys, cross_totals, cross_mixed, cross_mixed_grad, cross_allowed
    )
    cross_query_low = cross_query_term.astype(jnp.bfloat16)
    grad_cross_query = matmul(first_low.T, cross_query_low)
    first_total = second_grad + matmul(cross_query_low, full_cross_query.T)
    first_grad, gain_grad_a, shift_grad_a = normalize_back(
        first_total, first_normed, first_scale, gains[0]
    )
    self_branch = first_grad.astype(jnp.bfloat16)
    grad_self_output = matmul(self_low.T, self_branch)
    self_mixed_grad = matmul(self_branch, full_output.T).astype(jnp.bfloat16)
    self_query_term, self_terms = attend_back(
        queries, self_keys, self_totals, self_mixed, self_mixed_grad, self_allowed
    )
    self_sum, cross_sum = (
        lax.psum_scatter(self_terms, "ctx", scatter_dimension=0, tiled=True),
        lax.psum_scatter(cross_terms, "ctx", scatter_dimension=0, tiled=True),
    )
    self_query_low = self_query_term.astype(jnp.bfloat16)
    grad_self_query = matmul(inputs.T, self_query_low)
    input_grad = first_grad + matmul(self_query_low, full_query.T)
    self_sum_low = self_sum.astype(jnp.bfloat16)
    grad_self_pair = matmul(stream_rows.T, self_sum_low)
    stream_grad = matmul(self_sum_low, full_pair.T)
    cross_sum_low = cross_sum.astype(jnp.bfloat16)
    grad_cross_pair = matmul(source_rows.T, cross_sum_low)
    source_grad = matmul(cross_sum_low, full_cross_pair.T)
    gain_grads = jnp.stack((gain_grad_a, gain_grad_b, gain_grad_c))
    shift_grads = jnp.stack((shift_grad_a, shift_grad_b, shift_grad_c))
    (
        share_query,
        share_pair,
        share_output,
        share_cross_query,
        share_cross_pair,
        share_cross_output,
        share_in,
        share_out,
        share_gain,
        share_shift,
    ) = (
        lax.psum_scatter(
            grad_self_query.astype(jnp.bfloat16), "wa", scatter_dimension=0, tiled=True
        ).astype(jnp.float32),
        lax.psum_scatter(
            grad_self_pair.astype(jnp.bfloat16), "wa", scatter_dimension=0, tiled=True
        ).astype(jnp.float32),
        lax.psum_scatter(
            grad_self_output.astype(jnp.bfloat16), "wa", scatter_dimension=0, tiled=True
        ).astype(jnp.float32),
        lax.psum_scatter(
            grad_cross_query.astype(jnp.bfloat16), "wa", scatter_dimension=0, tiled=True
        ).astype(jnp.float32),
        lax.psum_scatter(
            grad_cross_pair.astype(jnp.bfloat16), "wa", scatter_dimension=0, tiled=True
        ).astype(jnp.float32),
        lax.psum_scatter(
            grad_cross_output.astype(jnp.bfloat16), "wa", scatter_dimension=0, tiled=True
        ).astype(jnp.float32),
        lax.psum_scatter(
            grad_ffn_in.astype(jnp.bfloat16), "wa", scatter_dimension=0, tiled=True
        ).astype(jnp.float32),
        lax.psum_scatter(
            grad_ffn_out.astype(jnp.bfloat16), "wa", scatter_dimension=0, tiled=True
        ).astype(jnp.float32),
        lax.psum_scatter(
            gain_grads.astype(jnp.bfloat16), "wa", scatter_dimension=1, tiled=True
        ).astype(jnp.float32),
        lax.psum_scatter(
            shift_grads.astype(jnp.bfloat16), "wa", scatter_dimension=1, tiled=True
        ).astype(jnp.float32),
    )
    (
        total_query,
        total_pair,
        total_output,
        total_cross_query,
        total_cross_pair,
        total_cross_output,
        total_in,
        total_out,
        total_gain,
        total_shift,
    ) = lax.psum(
        (
            share_query,
            share_pair,
            share_output,
            share_cross_query,
            share_cross_pair,
            share_cross_output,
            share_in,
            share_out,
            share_gain,
            share_shift,
        ),
        "ctx",
    )
    return (
        result.astype(jnp.bfloat16)[None],
        input_grad[None],
        stream_grad[None],
        source_grad[None],
        total_query,
        total_pair,
        total_output,
        total_cross_query,
        total_cross_pair,
        total_cross_output,
        total_in,
        total_out,
        total_gain,
        total_shift,
    )


def solution(mesh):
    in_specs = (
        P("wa", "ctx", None),
        P("wa", "ctx", None),
        P("wa", "ctx", None),
        P("wa", None),
        P("wa", None),
        P("wa", None),
        P("wa", None),
        P("wa", None),
        P("wa", None),
        P("wa", None),
        P("wa", None),
        P("wa", None),
        P("wa", None),
        P("wa", None),
        P("wa", None),
        P(None, "wa"),
        P(None, "wa"),
        P("wa", "ctx", None),
    )
    out_specs = (
        P("wa", "ctx", None),
        P("wa", "ctx", None),
        P("wa", "ctx", None),
        P("wa", "ctx", None),
        P("wa", None),
        P("wa", None),
        P("wa", None),
        P("wa", None),
        P("wa", None),
        P("wa", None),
        P("wa", None),
        P("wa", None),
        P(None, "wa"),
        P(None, "wa"),
    )
    return jax.shard_map(shards, mesh=mesh, in_specs=in_specs, out_specs=out_specs, check_vma=False)
```

profile of v0, /device:TPU:0, one launch (start us, length us, event | category | flops | bytes accessed | tf_op | source)
XLA Modules:
  0.0 829.5 jit_solution(3917390262233746699)
XLA Ops:
  8.8 31.5 %all-gather.7.cloned.1.call-done = bf16[512,1024]{1,0:T(8,128)(2,1)} async-done(((bf16[128,1024]{1,0:T(8,128)(2,1)}), bf16[512,1024]{1,0:T(8,128)(2,1)}) %all-gather.7.cloned.1.call-update) | async-done | bytes 1048592 | tf_op jit(solution)/shard_map/all_gather | solution.py:190
  43.0 26.4 %all-gather.11.cloned.1.call-done = bf16[512,1024]{1,0:T(8,128)(2,1)} async-done(((bf16[128,1024]{1,0:T(8,128)(2,1)}), bf16[512,1024]{1,0:T(8,128)(2,1)}) %all-gather.11.cloned.1.call-update) | async-done | bytes 1048592 | tf_op jit(solution)/shard_map/all_gather | solution.py:193
  91.4 15.2 %all_gather.38 = bf16[512,512]{1,0:T(8,128)(2,1)S(1)} all-gather(bf16[128,512]{1,0:T(8,128)(2,1)S(1)} %copy-done.35), channel_id=1, replica_groups=mesh['ctx'=8,'wa'=4] {'wa'}, dimensions={0}, use_global_device_ids=true | all-gather | bytes 655360 | tf_op jit(solution)/shard_map/all_gather | solution.py:189
  107.8 16.5 %all_gather.39 = bf16[512,512]{1,0:T(8,128)(2,1)} all-gather(bf16[128,512]{1,0:T(8,128)(2,1)S(1)} %copy-done.36), channel_id=1, replica_groups=mesh['ctx'=8,'wa'=4] {'wa'}, dimensions={0}, use_global_device_ids=true | all-gather | bytes 655360 | tf_op jit(solution)/shard_map/all_gather | solution.py:191
  124.3 16.1 %all_gather.44 = bf16[512,512]{1,0:T(8,128)(2,1)} all-gather(bf16[128,512]{1,0:T(8,128)(2,1)S(1)} %copy-done.37), channel_id=1, replica_groups=mesh['ctx'=8,'wa'=4] {'wa'}, dimensions={0}, use_global_device_ids=true | all-gather | bytes 655360 | tf_op jit(solution)/shard_map/all_gather | solution.py:192
  140.4 15.4 %all_gather.45 = bf16[512,512]{1,0:T(8,128)(2,1)} all-gather(bf16[128,512]{1,0:T(8,128)(2,1)S(1)} %copy-done.38), channel_id=1, replica_groups=mesh['ctx'=8,'wa'=4] {'wa'}, dimensions={0}, use_global_device_ids=true | all-gather | bytes 655360 | tf_op jit(solution)/shard_map/all_gather | solution.py:194
  162.4 14.1 %while.74 = (s32[]{:T(128)}, f32[8,256]{1,0:T(8,128)S(1)}, f32[8,256]{1,0:T(8,128)S(1)}, s32[256]{0:T(256)S(1)}, s32[2]{0:T(128)S(1)}, /*index=5*/s32[2048]{0:T(...) while((s32[]{:T(128)}, f32[8,256]{1,0:T(8,128)S(1)}, ...), condition=%wide.region_5.6_spmd.clone, body=%wide.region_2.0_spmd.clone.sunk | while | flops 286534912 | bytes 21115116 | solution.py:52
  176.5 12.9 %while.75 = (s32[]{:T(128)}, f32[256,8,64]{0,2,1:T(8,128)S(1)}, s32[2]{0:T(128)S(1)}, bf16[2048,1024]{0,1:T(8,128)(2,1)}, s32[256]{0:T(256)S(1)}, /*index=5*/s32...) while((s32[]{:T(128)}, f32[256,8,64]{0,2,1:T(8,128)S(1)}, ...), condition=%wide.region_7.8_spmd.clone, body=%wide.region_6.7_spmd.clone.sunk | while | flops 546833664 | bytes 8171781 | solution.py:79
  200.3 12.9 %while.76 = (s32[]{:T(128)}, f32[8,256]{1,0:T(8,128)S(1)}, f32[8,256]{1,0:T(8,128)S(1)}, s32[256]{0:T(256)S(1)}, s32[2]{0:T(128)S(1)}, /*index=5*/s32[2048]{0:T(...) while((s32[]{:T(128)}, f32[8,256]{1,0:T(8,128)S(1)}, ...), condition=%wide.region_14.15_spmd.clone, body=%wide.region_11.14_spmd.clone.sunk | while | flops 285485056 | bytes 21091528 | solution.py:52
  213.3 14.4 %while.77 = (s32[]{:T(128)}, f32[256,8,64]{0,2,1:T(8,128)}, s32[2]{0:T(128)S(1)}, bf16[2048,1024]{0,1:T(8,128)(2,1)}, s32[256]{0:T(256)S(1)}, /*index=5*/s32[204...) while((s32[]{:T(128)}, f32[256,8,64]{0,2,1:T(8,128)}, ...), condition=%wide.region_16.17_spmd.clone, body=%wide.region_15.16_spmd.clone.sunk | while | flops 545783808 | bytes 8148193 | solution.py:79
  254.0 49.5 %while.78 = (s32[]{:T(128)}, f32[256,8,64]{0,2,1:T(8,128)S(1)}, f32[2,1024,1024]{2,1,0:T(8,128)}, s32[2]{0:T(128)S(1)}, bf16[2048,1024]{0,1:T(8,128)(2,1)}, /*in...) while((s32[]{:T(128)}, f32[256,8,64]{0,2,1:T(8,128)S(1)}, ...), condition=%wide.region_27.28_spmd.clone, body=%wide.region_26.27_spmd.clone.sunk | while | flops 1366818816 | bytes 77370616 | solution.py:127
  317.5 51.4 %while.79 = (s32[]{:T(128)}, f32[256,8,64]{0,2,1:T(8,128)S(1)}, f32[2,1024,1024]{2,1,0:T(8,128)}, s32[2]{0:T(128)S(1)}, bf16[2048,1024]{0,1:T(8,128)(2,1)}, /*in...) while((s32[]{:T(128)}, f32[256,8,64]{0,2,1:T(8,128)S(1)}, ...), condition=%wide.region_32.33_spmd.clone, body=%wide.region_31.32_spmd.clone.sunk | while | flops 1367868672 | bytes 78442816 | solution.py:127
  390.8 58.0 %reduce-scatter.23.cloned.1.call-done = f32[256,1024]{1,0:T(8,128)} async-done(((f32[2048,1024]{1,0:T(8,128)}), f32[256,1024]{1,0:T(8,128)}) %reduce-scatter.23.cloned.1.call-update) | async-done | bytes 1048592 | tf_op jit(solution)/shard_map/reduce_scatter | solution.py:289
  456.1 14.8 %reduce-scatter.45.cloned.1.call-done = bf16[128,3]{1,0:T(8,128)(2,1)} async-done(((bf16[512,3]{1,0:T(8,128)(2,1)}), bf16[128,3]{1,0:T(8,128)(2,1)}) %reduce-scatter.45.cloned.1.call-update) | async-done | bytes 784
  471.7 19.3 %reduce-scatter.43.cloned.1.call-done = bf16[128,3]{1,0:T(8,128)(2,1)} async-done(((bf16[512,3]{1,0:T(8,128)(2,1)}), bf16[128,3]{1,0:T(8,128)(2,1)}) %reduce-scatter.43.cloned.1.call-update) | async-done | bytes 784
  491.8 21.8 %reduce-scatter.37.cloned.1.call-done = bf16[128,512]{1,0:T(8,128)(2,1)} async-done(((bf16[512,512]{1,0:T(8,128)(2,1)}), bf16[128,512]{1,0:T(8,128)(2,1)}) %reduce-scatter.37.cloned.1.call-update) | async-done | bytes 131088
  514.6 21.7 %reduce-scatter.31.cloned.1.call-done = bf16[128,512]{1,0:T(8,128)(2,1)} async-done(((bf16[512,512]{1,0:T(8,128)(2,1)}), bf16[128,512]{1,0:T(8,128)(2,1)}) %reduce-scatter.31.cloned.1.call-update) | async-done | bytes 131088 | tf_op jit(solution)/shard_map/reduce_scatter | solution.py:330
  536.3 22.8 %reduce-scatter.27.cloned.1.call-done = bf16[128,512]{1,0:T(8,128)(2,1)} async-done(((bf16[512,512]{1,0:T(8,128)(2,1)}), bf16[128,512]{1,0:T(8,128)(2,1)}) %reduce-scatter.27.cloned.1.call-update) | async-done | bytes 131088 | tf_op jit(solution)/shard_map/reduce_scatter | solution.py:321
  559.1 22.7 %reduce-scatter.29.cloned.1.call-done = bf16[128,512]{1,0:T(8,128)(2,1)} async-done(((bf16[512,512]{1,0:T(8,128)(2,1)}), bf16[128,512]{1,0:T(8,128)(2,1)}) %reduce-scatter.29.cloned.1.call-update) | async-done | bytes 131088 | tf_op jit(solution)/shard_map/reduce_scatter | solution.py:324
  581.8 44.3 %reduce-scatter.35.cloned.1.call-done = bf16[512,512]{1,0:T(8,128)(2,1)} async-done(((bf16[2048,512]{1,0:T(8,128)(2,1)}), bf16[512,512]{1,0:T(8,128)(2,1)}) %reduce-scatter.35.cloned.1.call-update) | async-done | bytes 524304 | tf_op jit(solution)/shard_map/reduce_scatter | solution.py:336
  626.2 45.5 %reduce-scatter.33.cloned.1.call-done = bf16[128,2048]{1,0:T(8,128)(2,1)} async-done(((bf16[512,2048]{1,0:T(8,128)(2,1)}), bf16[128,2048]{1,0:T(8,128)(2,1)}) %reduce-scatter.33.cloned.1.call-update) | async-done | bytes 524304 | tf_op jit(solution)/shard_map/reduce_scatter | solution.py:333
  676.6 23.7 %reduce-scatter.41.cloned.1.call-done = bf16[128,1024]{1,0:T(8,128)(2,1)} async-done(((bf16[512,1024]{1,0:T(8,128)(2,1)}), bf16[128,1024]{1,0:T(8,128)(2,1)}) %reduce-scatter.41.cloned.1.call-update) | async-done | bytes 262160
  701.4 27.5 %reduce-scatter.39.cloned.1.call-done = bf16[128,1024]{1,0:T(8,128)(2,1)} async-done(((bf16[512,1024]{1,0:T(8,128)(2,1)}), bf16[128,1024]{1,0:T(8,128)(2,1)}) %reduce-scatter.39.cloned.1.call-update) | async-done | bytes 262160
  730.1 89.6 %all-reduce.2 = (f32[128,512]{0,1:T(8,128)S(1)}, f32[128,1024]{0,1:T(8,128)S(1)}, f32[128,512]{1,0:T(8,128)}, f32[128,512]{1,0:T(8,128)}, f32[128,1024]{0,1:T(8,...) all-reduce(bf16[128,512]{0,1:T(8,128)(2,1)S(1)} %copy.145, ...), channel_id=1, replica_groups=mesh['ctx'=8,'wa'=4] {'ctx'}, use_global_device_ids=true, to_apply=%region_36.37 | all-reduce | flops 1049344 | bytes 6296064 | tf_op jit(solution)/shard_map/psum | solution.py:357
  (406 shorter events, 271.6 us)
Async XLA Ops:
  7.3 33.1 %all-gather.7.cloned.1.call-start = ((), (), s32[]{:S(2)}) async-start(), calls=%async_computation.12 | async-start | bytes 1310720 | tf_op jit(solution)/shard_map/all_gather | solution.py:190
  8.0 61.3 %all-gather.11.cloned.1.call-start = ((), (), s32[]{:S(2)}) async-start(), calls=%async_computation.14 | async-start | bytes 1310720 | tf_op jit(solution)/shard_map/all_gather | solution.py:193
  8.8 147.1 %all-gather.9.cloned.1.call-start = ((), (), s32[]{:S(2)}) async-start(), calls=%async_computation.13 | async-start | bytes 4718592 | tf_op jit(solution)/shard_map/all_gather | solution.py:234
  42.9 150.8 %all-gather.13.cloned.1.call-start = ((), (), s32[]{:S(2)}) async-start(), calls=%async_computation.15 | async-start | bytes 4718592 | tf_op jit(solution)/shard_map/all_gather | solution.py:235
  71.8 159.0 %all-gather.15.cloned.1.call-start = ((), (), s32[]{:S(2)}) async-start(), calls=%async_computation.16 | async-start | bytes 2621440 | tf_op jit(solution)/shard_map/all_gather | solution.py:195
  72.4 168.1 %all-gather.17.cloned.1.call-start = ((), (), s32[]{:S(2)}) async-start(), calls=%async_computation.17 | async-start | bytes 2621440 | tf_op jit(solution)/shard_map/all_gather | solution.py:196
  73.0 314.3 %reduce-scatter.25.cloned.1.call-start = ((), (), s32[]{:S(2)}) async-start(), calls=%async_computation.19 | async-start | bytes 9437184 | tf_op jit(solution)/shard_map/reduce_scatter | solution.py:290
  82.8 164.0 %copy-start.51 = (f32[1,512]{1,0:T(1,128)}, f32[1,512]{1,0:T(1,128)S(1)}, u32[]{:S(2)}) copy-start(f32[1,512]{1,0:T(1,128)S(1)} %get-tuple-element.1041) | copy-start | bytes 6148
  82.8 165.9 %copy-start.41 = (f32[1,512]{1,0:T(1,128)}, f32[1,512]{1,0:T(1,128)S(1)}, u32[]{:S(2)}) copy-start(f32[1,512]{1,0:T(1,128)S(1)} %get-tuple-element.1042) | copy-start | bytes 6148
  90.5 138.4 %copy-start.47 = (f32[1,512]{1,0:T(1,128)}, f32[1,512]{1,0:T(1,128)S(1)}, u32[]{:S(2)}) copy-start(f32[1,512]{1,0:T(1,128)S(1)} %get-tuple-element.1046) | copy-start | bytes 6148
  90.5 150.1 %copy-start.45 = (f32[1,512]{1,0:T(1,128)}, f32[1,512]{1,0:T(1,128)S(1)}, u32[]{:S(2)}) copy-start(f32[1,512]{1,0:T(1,128)S(1)} %get-tuple-element.1045) | copy-start | bytes 6148
  303.5 145.3 %reduce-scatter.23.cloned.1.call-start = ((), (), s32[]{:S(2)}) async-start(), calls=%async_computation.18 | async-start | bytes 9437184 | tf_op jit(solution)/shard_map/reduce_scatter | solution.py:289
  368.9 102.0 %reduce-scatter.45.cloned.1.call-start = ((), (), s32[]{:S(2)}) async-start(), calls=%async_computation.29 | async-start | bytes 163840
  371.0 120.0 %reduce-scatter.43.cloned.1.call-start = ((), (), s32[]{:S(2)}) async-start(), calls=%async_computation.28 | async-start | bytes 163840
  372.6 141.0 %reduce-scatter.37.cloned.1.call-start = ((), (), s32[]{:S(2)}) async-start(), calls=%async_computation.25 | async-start | bytes 655360
  376.9 159.4 %reduce-scatter.31.cloned.1.call-start = ((), (), s32[]{:S(2)}) async-start(), calls=%async_computation.22 | async-start | bytes 655360 | tf_op jit(solution)/shard_map/reduce_scatter | solution.py:330
  378.1 181.0 %reduce-scatter.27.cloned.1.call-start = ((), (), s32[]{:S(2)}) async-start(), calls=%async_computation.20 | async-start | bytes 655360 | tf_op jit(solution)/shard_map/reduce_scatter | solution.py:321
  379.3 202.5 %reduce-scatter.29.cloned.1.call-start = ((), (), s32[]{:S(2)}) async-start(), calls=%async_computation.21 | async-start | bytes 655360 | tf_op jit(solution)/shard_map/reduce_scatter | solution.py:324
  380.7 245.4 %reduce-scatter.35.cloned.1.call-start = ((), (), s32[]{:S(2)}) async-start(), calls=%async_computation.24 | async-start | bytes 2621440 | tf_op jit(solution)/shard_map/reduce_scatter | solution.py:336
  384.9 286.7 %reduce-scatter.33.cloned.1.call-start = ((), (), s32[]{:S(2)}) async-start(), calls=%async_computation.23 | async-start | bytes 2621440 | tf_op jit(solution)/shard_map/reduce_scatter | solution.py:333
  387.2 313.1 %reduce-scatter.41.cloned.1.call-start = ((), (), s32[]{:S(2)}) async-start(), calls=%async_computation.27 | async-start | bytes 1310720
  390.6 281.1 %copy-start.14 = (bf16[512,1024]{1,0:T(8,128)(2,1)S(1)}, bf16[512,1024]{1,0:T(8,128)(2,1)}, u32[]{:S(2)}) copy-start(bf16[512,1024]{1,0:T(8,128)(2,1)} %all-gather.11.cloned.1.call-done) | copy-start | bytes 3145732
  390.6 338.4 %reduce-scatter.39.cloned.1.call-start = ((), (), s32[]{:S(2)}) async-start(), calls=%async_computation.26 | async-start | bytes 1310720
  451.6 222.5 %copy-start.13 = (bf16[512,1024]{1,0:T(8,128)(2,1)S(1)}, bf16[512,1024]{1,0:T(8,128)(2,1)}, u32[]{:S(2)}) copy-start(bf16[512,1024]{1,0:T(8,128)(2,1)} %all-gather.7.cloned.1.call-done) | copy-start | bytes 3145732
  (64 other events, 1315.4 us)
Sparse Core Ops, SparseCore 0:
  9.7 30.6 all-gather.6
  41.9 27.4 all-gather.10
  71.8 36.1 all-gather.8
  110.4 36.7 all-gather.12
  148.5 45.9 all-gather.14
  195.9 44.5 all-gather.16
  303.6 70.0 reduce-scatter.24
  377.6 71.2 reduce-scatter.22
  451.7 19.1 reduce-scatter.44
  473.7 17.2 reduce-scatter.42
  493.8 19.7 reduce-scatter.36
  516.3 19.9 reduce-scatter.30
  539.1 19.9 reduce-scatter.26
  561.8 19.9 reduce-scatter.28
  583.9 42.1 reduce-scatter.34
  628.4 43.1 reduce-scatter.32
  673.7 26.4 reduce-scatter.40
  703.1 25.7 reduce-scatter.38
where the time goes:
time: 841 us; the launch traced here: 830 us
  waiting for transfers between devices  389 us (46%)
  blocking collectives  170 us (20%)
  local copies, waits for them, and re-layouts  116 us (14%)
  matrix products  99.7 us (12%)
  other arithmetic  29.2 us (3%)
  between operations  15.7 us (2%)
  loops' own time  9.44 us (1%)
    unnamed x23, waiting for transfers between devices  110 us
    psum x1, blocking collectives, shards(): lax.psum((share_query, share_pair, share_output, share_cross_query, share...  89.6 us
    reduce_scatter x1, waiting for transfers between devices, shards(): lax.psum_scatter(self_terms, 'ctx', scatter_dimension=0, tiled=True)  58 us
    dot_general x24, matrix products, matmul(): return jnp.dot(left, right, preferred_element_type=jnp.float32)  46.3 us
    reduce_scatter x1, waiting for transfers between devices, shards(): lax.psum_scatter(grad_ffn_in.astype(jnp.bfloat16), 'wa', scatter_dimensio...  45.5 us
    reduce_scatter x1, waiting for transfers between devices, shards(): lax.psum_scatter(grad_ffn_out.astype(jnp.bfloat16), 'wa', scatter_dimensi...  44.3 us
    dynamic_update_slice x8, local copies, waits for them, and re-layouts, attend_back(): lax.scan(visit, jnp.zeros(query_heads.shape, jnp.float32), jnp.arange(key...  41.7 us
    all_gather x1, waiting for transfers between devices, shards(): lax.all_gather(self_key_value, 'wa', axis=0, tiled=True)  31.5 us
  transfers between devices with their start and end apart: 18, of which 14 were waited for; matrix products, arithmetic and copies ran while one was open for 21% of the time, Pallas kernels for 0%

commit v1 on v0

--- a/solution.py
+++ b/solution.py
@@ -1,6 +1,10 @@
+import functools
+
 import jax
 import jax.numpy as jnp
 from jax import lax
+from jax.experimental import pallas as pl
+from jax.experimental.pallas import tpu as pltpu
 from jax.sharding import PartitionSpec as P
 
 D = 512
@@ -154,7 +158,7 @@
     return jnp.dot(left, right, preferred_element_type=jnp.float32)
 
 
-def shards(
+def general_shards(
     hidden,
     stream,
     encoder,
@@ -387,6 +391,734 @@
     )
 
 
+PAIR = 2 * HEAD
+PAIRS = HEADS // 2
+FF = 2048
+low_t = jnp.bfloat16
+wide_t = jnp.float32
+vmem_spec = pl.BlockSpec(memory_space=pltpu.VMEM)
+smem_spec = pl.BlockSpec(memory_space=pltpu.SMEM)
+
+
+def run(body, outs, ids, args, scratch=(), flops=0, vmem=56):
+    outs = [jax.ShapeDtypeStruct(shape, kind) for shape, kind in outs]
+    moved = sum(a.size * a.dtype.itemsize for a in list(args) + outs)
+    return pl.pallas_call(
+        body,
+        out_shape=outs,
+        in_specs=[smem_spec] + [vmem_spec] * len(args),
+        out_specs=[vmem_spec] * len(outs),
+        scratch_shapes=[pltpu.VMEM(shape, kind) for shape, kind in scratch],
+        compiler_params=pltpu.CompilerParams(vmem_limit_bytes=vmem * 1024 * 1024),
+        cost_estimate=pl.CostEstimate(flops=int(flops), bytes_accessed=moved, transcendentals=0),
+    )(ids, *args)
+
+
+def dot_nn(a, b):
+    return lax.dot_general(a, b, (((1,), (0,)), ((), ())), preferred_element_type=wide_t)
+
+
+def dot_nt(a, b):
+    return lax.dot_general(a, b, (((1,), (1,)), ((), ())), preferred_element_type=wide_t)
+
+
+def dot_tn(a, b):
+    return lax.dot_general(a, b, (((0,), (0,)), ((), ())), preferred_element_type=wide_t)
+
+
+def at16(start, size=16):
+    return pl.ds(pl.multiple_of(start, 16), size)
+
+
+def at128(start, size=128):
+    return pl.ds(pl.multiple_of(start, 128), size)
+
+
+def assemble(ids, parts, whole_ref, columns=None):
+    me, mw = ids[0], ids[1]
+    for d in range(8):
+        own = me ^ d
+        for e in range(4):
+            row = (mw ^ e) * 128 + own * 16
+            piece = parts[d][e * 16 : (e + 1) * 16, :]
+            if columns is not None:
+                piece = piece[:, columns]
+            whole_ref[at16(row), :] = piece
+
+
+def half_mask(shape, axis, core):
+    return (lax.broadcasted_iota(jnp.int32, shape, axis) // HEAD) == core
+
+
+def attend_rows(q_ref, kv_ref, bias_ref, out_ref):
+    rows, keys = bias_ref.shape
+    chunk = rows // 2
+
+    def step(i, carry):
+        p, r = i // 2, i % 2
+        here = pl.ds(pl.multiple_of(r * chunk, chunk), chunk)
+        q = q_ref[here, at128(p * PAIR)]
+        first = half_mask((chunk, PAIR), 1, 0)
+        both = jnp.concatenate(
+            (jnp.where(first, q, jnp.zeros_like(q)), jnp.where(first, jnp.zeros_like(q), q)), axis=0
+        )
+        bias = bias_ref[here, :]
+        s = dot_nt(both, kv_ref[:, at128(p * PAIR)]) + jnp.concatenate((bias, bias), axis=0)
+        top = jnp.max(s, axis=1, keepdims=True)
+        w = jnp.exp(s - top)
+        total = jnp.sum(w, axis=1, keepdims=True)
+        mixed = dot_nn(w.astype(low_t), kv_ref[:, at128(D + p * PAIR)]) / total
+        out_ref[here, at128(p * PAIR)] = jnp.where(first, mixed[:chunk], mixed[chunk:]).astype(low_t)
+        return carry
+
+    lax.fori_loop(0, 2 * PAIRS, step, 0)
+
+
+def project_pairs(parts, weight, kv_ref):
+    rows = parts[0].shape[0]
+    for d in range(8):
+        kv_ref[d * rows : (d + 1) * rows, :] = dot_nn(parts[d][...], weight).astype(low_t)
+
+
+def self_forward(ids, hidden, *refs):
+    stream, slices = refs[:8], refs[8:16]
+    code, low_row, high_row, out, w1, q_ref, kv_ref, bias_ref = refs[16:]
+    rows = hidden.shape[0]
+    assemble(ids, slices, w1)
+    q_ref[...] = (dot_nn(hidden[...], w1[:, :D]).astype(low_t) * 0.125).astype(low_t)
+    project_pairs(stream, w1[:, D:], kv_ref)
+    k = code[...]
+    seen = (k >= low_row[...]) & (k < high_row[...])
+    bias_ref[...] = jnp.where(seen, 0.0, neg_fill)
+    own = lax.broadcasted_iota(jnp.int32, (rows, rows), 0) == lax.broadcasted_iota(
+        jnp.int32, (rows, rows), 1
+    )
+    bias_ref[:, :rows] = jnp.where(own, 0.0, bias_ref[:, :rows])
+    attend_rows(q_ref, kv_ref, bias_ref, out)
+
+
+def layer_norm(values, gain_row, shift_row):
+    mean = jnp.mean(values, axis=1, keepdims=True)
+    centred = values - mean
+    scale = lax.rsqrt(jnp.mean(centred * centred, axis=1, keepdims=True) + layer_eps)
+    normed = centred * scale
+    return normed * gain_row + shift_row, normed, scale
+
+
+def layer_norm_back(grad, normed, scale, gain_row):
+    gain_term = jnp.sum(grad * normed, axis=0, keepdims=True)
+    shift_term = jnp.sum(grad, axis=0, keepdims=True)
+    scaled = grad * gain_row
+    grad_in = scale * (
+        scaled
+        - jnp.mean(scaled, axis=1, keepdims=True)
+        - normed * jnp.mean(scaled * normed, axis=1, keepdims=True)
+    )
+    return grad_in, gain_term, shift_term
+
+
+def deal_pairs(ids, value, out):
+    chip = ids[0] // 2
+    for p in range(PAIRS):
+        out[chip ^ p] = value[:, p * PAIR : (p + 1) * PAIR]
+
+
+def cross_forward(ids, hidden, self_low, *refs):
+    source, slices, norms = refs[:8], refs[8:16], refs[16:20]
+    code, seq_col, first, normed, scale_out, first_low, cross_low, dealt, w2, gs = refs[20:30]
+    q_ref, kv_ref, bias_ref = refs[30:]
+    assemble(ids, slices, w2)
+    for e in range(4):
+        gs[:, at128((ids[1] ^ e) * 128)] = norms[e][...]
+    gain, shift = gs[0:1, :].astype(wide_t), gs[3:4, :].astype(wide_t)
+    value, n0, s0 = layer_norm(
+        hidden[...].astype(wide_t) + dot_nn(self_low[...], w2[:, :D]), gain, shift
+    )
+    first[...] = value
+    normed[...] = n0
+    scale_out[...] = jnp.broadcast_to(s0, scale_out.shape)
+    low = value.astype(low_t)
+    first_low[...] = low
+    q = dot_nn(low, w2[:, D : 2 * D]).astype(low_t)
+    deal_pairs(ids, q, dealt)
+    q_ref[...] = (q * 0.125).astype(low_t)
+    project_pairs(source, w2[:, 2 * D : 4 * D], kv_ref)
+    bias_ref[...] = jnp.where(code[...] == seq_col[...], 0.0, neg_fill)
+    attend_rows(q_ref, kv_ref, bias_ref, cross_low)
+
+
+def feed_forward(ids, first, cross_low, w_cross, gs, cotangent, *refs):
+    slices = refs[:8]
+    (result, dealt, second_grad, second_low, activated, pre_grad, branch, cross_branch, sums) = refs[8:17]
+    win, wout, slope = refs[17:]
+    rows = first.shape[0]
+    me, mw = ids[0], ids[1]
+    for d in range(8):
+        own = me ^ d
+        for e in range(4):
+            w = mw ^ e
+            here = pl.ds(e * 16, 16)
+            win[at16(w * 128 + own * 16), :] = slices[d][here, :FF]
+            for g in range(4):
+                wout[at16(w * 512 + own * 64 + g * 16), :] = slices[d][
+                    here, FF + g * D : FF + (g + 1) * D
+                ]
+    gains, shifts = gs[0:3, :].astype(wide_t), gs[3:6, :].astype(wide_t)
+    second, n1, s1 = layer_norm(
+        first[...] + dot_nn(cross_low[...], w_cross[...]), gains[1:2], shifts[1:2]
+    )
+    low = second.astype(low_t)
+    second_low[...] = low
+    width = 512
+    total = second
+    for c in range(FF // width):
+        cols = slice(c * width, (c + 1) * width)
+        pre = dot_nn(low, win[:, cols])
+        sig = 1.0 / (1.0 + jnp.exp(-pre))
+        act = (pre * sig).astype(low_t)
+        activated[:, cols] = act
+        slope[:, cols] = sig * (1.0 + pre * (1.0 - sig))
+        total = total + dot_nn(act, wout[cols, :])
+    value, n2, s2 = layer_norm(total, gains[2:3], shifts[2:3])
+    result[...] = value.astype(low_t)
+    third, gain_c, shift_c = layer_norm_back(cotangent[...].astype(wide_t), n2, s2, gains[2:3])
+    third_low = third.astype(low_t)
+    branch[...] = third_low
+    total = third
+    for c in range(FF // width):
+        cols = slice(c * width, (c + 1) * width)
+        back = (dot_nt(third_low, wout[cols, :]) * slope[:, cols]).astype(low_t)
+        pre_grad[:, cols] = back
+        total = total + dot_nt(back, win[:, cols])
+    grad, gain_b, shift_b = layer_norm_back(total, n1, s1, gains[1:2])
+    second_grad[...] = grad
+    grad_low = grad.astype(low_t)
+    cross_branch[...] = grad_low
+    deal_pairs(ids, dot_nt(grad_low, w_cross[...]).astype(low_t), dealt)
+    zero = jnp.zeros_like(gain_b)
+    sums[...] = jnp.concatenate(
+        (zero, gain_b, gain_c, zero, shift_b, shift_c, zero, zero), axis=0
+    )
+
+
+def put_pieces(ids, value_ref, depth, keep, send, column):
+    me, mw = ids[0], ids[1]
+    width = value_ref.shape[1]
+    for d in range(8):
+        own = me ^ d
+        out = send if d % 2 else keep
+        for e in range(4):
+            w = mw ^ e
+            for g in range(depth):
+                row = (w * 8 + own) * (16 * depth) + g * 16
+                out[d // 2, e * 16 : (e + 1) * 16, column + g * width : column + (g + 1) * width] = (
+                    value_ref[at16(row), :]
+                )
+
+
+def weight_grads(depths, ids, *refs):
+    n = len(depths)
+    lefts, rights = refs[:n], refs[n : 2 * n]
+    keep, send = refs[2 * n : 2 * n + 2]
+    column = 0
+    for left, right, depth, scratch in zip(lefts, rights, depths, refs[2 * n + 2 :]):
+        scratch[...] = dot_tn(left[...], right[...]).astype(low_t)
+        put_pieces(ids, scratch, depth, keep, send, column)
+        column += depth * right.shape[1]
+
+
+def pair_back(is_self, ids, *refs):
+    at = 0
+
+    def take(n):
+        nonlocal at
+        at += n
+        return refs[at - n : at]
+
+    q_parts, do_parts, x_parts = take(8), take(8), take(8)
+    if is_self:
+        (w_query,) = take(1)
+    w_pair, code, low_rows, high_rows = take(4)
+    dq_keep, dq_send, dkv_keep, dkv_send, w_keep, w_send = take(6)
+    q_all, do_all, k_all, v_all, kt, dq_t, dq_all, dk, dv, s_ref, grads = take(11)
+    me, mw = ids[0], ids[1]
+    pair, core = me // 2, me % 2
+    rows = do_parts[0].shape[0]
+    keys = 8 * rows
+    mine = half_mask((rows, PAIR), 1, core)
+    nothing = jnp.zeros((rows, PAIR), low_t)
+    if is_self:
+        wq = w_query[:, at128(pair * PAIR)]
+    wk, wv = w_pair[:, at128(pair * PAIR)], w_pair[:, at128(D + pair * PAIR)]
+    for d in range(8):
+        here = slice(d * rows, (d + 1) * rows)
+        x = x_parts[d][...]
+        k_all[here, :] = dot_nn(x, wk).astype(low_t)
+        v_all[here, :] = dot_nn(x, wv).astype(low_t)
+        q = dot_nn(q_parts[d][...], wq).astype(low_t) if is_self else q_parts[d][...]
+        q_all[d] = (jnp.where(mine, q, nothing) * 0.125).astype(low_t)
+        do_all[d] = jnp.where(mine, do_parts[d][...], nothing)
+    kt[...] = k_all[...].astype(wide_t).T.astype(low_t)
+    dk[...] = jnp.zeros_like(dk)
+    dv[...] = jnp.zeros_like(dv)
+
+    def step(b, carry):
+        q, do = q_all[b], do_all[b]
+        c = jnp.concatenate((code[...],) * (rows // 128), axis=1)
+        low_row = low_rows[pl.ds(b, 1), :]
+        s = dot_nt(k_all[...], q)
+        if is_self:
+            s_ref[...] = jnp.where((c >= low_row) & (c < high_rows[pl.ds(b, 1), :]), s, neg_fill)
+            block = pl.ds(pl.multiple_of(b * rows, rows), rows)
+            own = lax.broadcasted_iota(jnp.int32, (rows, rows), 0) == lax.broadcasted_iota(
+                jnp.int32, (rows, rows), 1
+            )
+            s_ref[block, :] = jnp.where(own, dot_nt(k_all[block, :], q), s_ref[block, :])
+        else:
+            s_ref[...] = jnp.where(c == low_row, s, neg_fill)
+        s = s_ref[...]
+        w = jnp.exp(s - jnp.max(s, axis=0, keepdims=True))
+        inverse = 1.0 / jnp.sum(w, axis=0, keepdims=True)
+        dp = dot_nt(v_all[...], do)
+        offset = jnp.sum(w * dp, axis=0, keepdims=True) * inverse
+        probs = w * inverse
+        dv[...] += dot_nn(probs.astype(low_t), do)
+        ds = (probs * (dp - offset)).astype(low_t)
+        dk[...] += dot_nn(ds, q)
+        dqt = dot_nn(kt[...], ds) * 0.125
+        dqt = jnp.where(half_mask((PAIR, rows), 0, core), dqt, 0.0)
+        dq_t[b] = dqt.astype(low_t)
+        dq_all[b] = dqt.T.astype(low_t)
+        return carry
+
+    lax.fori_loop(0, 8, step, 0)
+    total_q = jnp.zeros((PAIR, D), wide_t)
+    total_k, total_v = total_q, total_q
+    for d in range(8):
+        here = slice(d * rows, (d + 1) * rows)
+        dk_low, dv_low = dk[here, :].astype(low_t), dv[here, :].astype(low_t)
+        (dq_send if d % 2 else dq_keep)[d // 2] = dq_all[d]
+        out = dkv_send if d % 2 else dkv_keep
+        out[d // 2, :, :PAIR] = dk_low
+        out[d // 2, :, PAIR:] = dv_low
+        x = x_parts[d][...]
+        total_k += dot_tn(dk_low, x)
+        total_v += dot_tn(dv_low, x)
+        if is_self:
+            total_q += dot_nn(dq_t[d], q_parts[d][...])
+    totals = (total_q, total_k, total_v) if is_self else (total_k, total_v)
+    for n, value in enumerate(totals):
+        grads[:, n * PAIR : (n + 1) * PAIR] = value.T.astype(low_t)
+    for e in range(4):
+        row = (mw ^ e) * 128
+        w_keep[e * 64 : (e + 1) * 64, :] = grads[at16(row + core * 64, 64), :]
+        w_send[e * 64 : (e + 1) * 64, :] = grads[at16(row + (1 - core) * 64, 64), :]
+
+
+def gather_pairs(ids, parts, column, out):
+    chip = ids[0] // 2
+    for k in range(PAIRS):
+        out[:, at128((chip ^ k) * PAIR)] = parts[k][:, column : column + PAIR]
+
+
+def first_back(ids, *refs):
+    parts = refs[:4]
+    second_grad, normed, scale, gs, w_cross_query, w_output, sums_in = refs[4:11]
+    first_grad, branch, dealt, dq, sums = refs[11:]
+    gather_pairs(ids, parts, 0, dq)
+    total = second_grad[...] + dot_nt(dq[...], w_cross_query[...])
+    grad, gain_a, shift_a = layer_norm_back(
+        total, normed[...], scale[:, 0:1], gs[0:1, :].astype(wide_t)
+    )
+    first_grad[...] = grad
+    low = grad.astype(low_t)
+    branch[...] = low
+    deal_pairs(ids, dot_nt(low, w_output[...]).astype(low_t), dealt)
+    zero = jnp.zeros_like(gain_a)
+    sums[...] = sums_in[...] + jnp.concatenate(
+        (gain_a, zero, zero, shift_a, zero, zero, zero, zero), axis=0
+    )
+
+
+def source_back(ids, *refs):
+    parts, w_pair, out, dkv = refs[:4], refs[4], refs[5], refs[6]
+    gather_pairs(ids, parts, 0, dkv.at[:, :D])
+    gather_pairs(ids, parts, PAIR, dkv.at[:, D:])
+    out[...] = dot_nt(dkv[...], w_pair[...])
+
+
+def hidden_back(ids, *refs):
+    parts, first_grad, w_query, out, dq = refs[:4], refs[4], refs[5], refs[6], refs[7]
+    gather_pairs(ids, parts, 0, dq)
+    out[...] = first_grad[...] + dot_nt(dq[...], w_query[...])
+
+
+def add_split(ids, keep, received, *outs):
+    for k in range(4):
+        outs[k][...] = (keep[k].astype(wide_t) + received[k].astype(wide_t)).astype(low_t)
+
+
+def add_rows(ids, *refs):
+    parts, outs = refs[:-4], refs[-4:]
+    size = outs[0].shape[0]
+    for e in range(4):
+        total = parts[0][e * size : (e + 1) * size, :].astype(wide_t)
+        for part in parts[1:]:
+            total = total + part[e * size : (e + 1) * size, :].astype(wide_t)
+        outs[e][...] = total.astype(low_t)
+
+
+def add_all(ids, *refs):
+    total = refs[0][...].astype(wide_t)
+    for part in refs[1:-1]:
+        total = total + part[...].astype(wide_t)
+    refs[-1][...] = total.astype(low_t)
+
+
+def place_rows(depths, ids, *refs):
+    parts, outs = refs[:8], refs[8:]
+    for d in range(8):
+        own = ids[0] ^ d
+        column = 0
+        for depth, out in zip(depths, outs):
+            width = out.shape[1]
+            for g in range(depth):
+                out[at16((own * depth + g) * 16), :] = parts[d][
+                    :, column + g * width : column + (g + 1) * width
+                ].astype(wide_t)
+            column += depth * width
+
+
+def place_pairs(ids, *refs):
+    parts, outs = refs[:8], refs[8:]
+    for d in range(8):
+        own = ids[0] ^ d
+        pair, rows = own // 2, at16((own % 2) * 64, 64)
+        column = 0
+        for out in outs:
+            for start in range(0, out.shape[1], D):
+                out[rows, at128(start + pair * PAIR)] = parts[d][:, column : column + PAIR].astype(
+                    wide_t
+                )
+                column += PAIR
+
+
+def swap(value, axis, bits):
+    size = lax.axis_size(axis)
+    return lax.ppermute(value, axis, [(i, i ^ bits) for i in range(size)])
+
+
+def gather_ctx(value):
+    parts = [value, None] + [swap(value, "ctx", d) if d % 2 == 0 else None for d in range(2, 8)]
+    for d in range(1, 8, 2):
+        parts[d] = swap(parts[d - 1], "ctx", 1)
+    return parts
+
+
+def gather_wa(value):
+    return [value] + [swap(value, "wa", e) for e in range(1, 4)]
+
+
+def exchange_pairs(dealt):
+    parts = [None] * 8
+    for k in range(4):
+        parts[2 * k] = dealt[k] if k == 0 else swap(dealt[k], "ctx", 2 * k)
+    for k in range(4):
+        parts[2 * k + 1] = swap(parts[2 * k], "ctx", 1)
+    return parts
+
+
+def return_pairs(ids, keep, send):
+    received = swap(send, "ctx", 1)
+    shape = keep.shape[1:]
+    sums = run(add_split, [(shape, low_t)] * 4, ids, [keep, received])
+    return [sums[0]] + [swap(sums[k], "ctx", 2 * k) for k in range(1, 4)]
+
+
+def reduce_wa(ids, parts):
+    rows, width = parts[0].shape
+    size = rows // 4
+    split = run(add_rows, [((size, width), low_t)] * 4, ids, parts)
+    moved = [split[0]] + [swap(split[e], "wa", e) for e in range(1, 4)]
+    (total,) = run(add_all, [((size, width), low_t)], ids, moved)
+    return gather_ctx(total)
+
+
+def reduce_slices(ids, keep, send):
+    return reduce_wa(ids, return_pairs(ids, keep, send))
+
+
+def reduce_halves(ids, keep, send):
+    return reduce_wa(ids, [keep, swap(send, "ctx", 1)])
+
+
+def fast_shards(
+    hidden,
+    stream,
+    encoder,
+    lengths,
+    order,
+    ranks,
+    thresholds,
+    self_query,
+    self_key_value,
+    self_output,
+    cross_query,
+    cross_key_value,
+    cross_output,
+    ffn_in,
+    ffn_out,
+    norm_gain,
+    norm_shift,
+    cotangent,
+):
+    rows, keys = hidden.shape[1], order.shape[1]
+    me, mw = lax.axis_index("ctx"), lax.axis_index("wa")
+    ids = jnp.stack((me, mw)).astype(jnp.int32)
+    inputs, stream_rows, source_rows = hidden[0], stream[0], encoder[0]
+
+    def row_slice(weight):
+        return lax.dynamic_slice_in_dim(weight, me * (weight.shape[0] // 8), weight.shape[0] // 8, 0)
+
+    out_slice = row_slice(ffn_out)
+    pack1 = jnp.concatenate((row_slice(self_query), row_slice(self_key_value)), axis=1)
+    pack2 = jnp.concatenate(
+        [row_slice(w) for w in (self_output, cross_query, cross_key_value, cross_output)], axis=1
+    )
+    pack3 = jnp.concatenate(
+        [row_slice(ffn_in)] + [out_slice[g * 16 : (g + 1) * 16] for g in range(4)], axis=1
+    )
+    norm_pack = jnp.concatenate(
+        (norm_gain, norm_shift, jnp.zeros((10, norm_gain.shape[1]), low_t)), axis=0
+    )
+
+    def gather_weights(pack):
+        return gather_ctx(jnp.concatenate(gather_wa(pack), axis=0))
+
+    stream_parts = gather_ctx(stream_rows)
+    slices1 = gather_weights(pack1)
+    norms = gather_wa(norm_pack)
+    slices2 = gather_weights(pack2)
+    source_parts = gather_ctx(source_rows)
+    slices3 = gather_weights(pack3)
+    hidden_parts = gather_ctx(inputs)
+
+    seq_ends = jnp.cumsum(lengths[0])
+    token_seq = sequence_ids(order[0], seq_ends)
+    source_seq = sequence_ids(jnp.arange(keys, dtype=jnp.int32), seq_ends)
+
+    def by_device(vector):
+        blocks = vector.reshape(8, rows)
+        return jnp.concatenate(
+            [lax.dynamic_slice_in_dim(blocks, me ^ d, 1, 0) for d in range(8)], axis=0
+        )
+
+    token_rows, source_blocks = by_device(token_seq), by_device(source_seq)
+    low_rows = token_rows * 1024
+    high_rows = low_rows + by_device(thresholds[0])
+    code_rows = low_rows + by_device(ranks[0])
+    code_wide = jnp.broadcast_to(code_rows.reshape(keys, 1), (keys, 128))
+    source_wide = jnp.broadcast_to(source_blocks.reshape(keys, 1), (keys, 128))
+
+    score_flops = 2 * rows * keys * D
+    self_low, w1 = run(
+        self_forward,
+        [((rows, D), low_t), ((D, 3 * D), low_t)],
+        ids,
+        [inputs, *stream_parts, *slices1]
+        + [code_rows.reshape(1, keys), low_rows[0].reshape(rows, 1), high_rows[0].reshape(rows, 1)],
+        [((rows, D), low_t), ((keys, 2 * D), low_t), ((rows, keys), wide_t)],
+        flops=8 * score_flops,
+    )
+    first, normed, scale, first_low, cross_low, cross_dealt, w2, gs = run(
+        cross_forward,
+        [
+            ((rows, D), wide_t),
+            ((rows, D), wide_t),
+            ((rows, 128), wide_t),
+            ((rows, D), low_t),
+            ((rows, D), low_t),
+            ((PAIRS, rows, PAIR), low_t),
+            ((D, 5 * D), low_t),
+            ((16, D), low_t),
+        ],
+        ids,
+        [inputs, self_low, *source_parts, *slices2, *norms]
+        + [source_blocks.reshape(1, keys), token_rows[0].reshape(rows, 1)],
+        [((rows, D), low_t), ((keys, 2 * D), low_t), ((rows, keys), wide_t)],
+        flops=8 * score_flops,
+    )
+    w_output, w_cross_query = w2[:, :D], w2[:, D : 2 * D]
+    w_cross_pair, w_cross_output = w2[:, 2 * D : 4 * D], w2[:, 4 * D :]
+    w_query, w_pair = w1[:, :D], w1[:, D:]
+    cross_q_parts = exchange_pairs(cross_dealt)
+    (
+        result,
+        cross_do_dealt,
+        second_grad,
+        second_low,
+        activated,
+        pre_grad,
+        branch,
+        cross_branch,
+        sums,
+    ) = run(
+        feed_forward,
+        [
+            ((rows, D), low_t),
+            ((PAIRS, rows, PAIR), low_t),
+            ((rows, D), wide_t),
+            ((rows, D), low_t),
+            ((rows, FF), low_t),
+            ((rows, FF), low_t),
+            ((rows, D), low_t),
+            ((rows, D), low_t),
+            ((8, D), wide_t),
+        ],
+        ids,
+        [first, cross_low, w_cross_output, gs, cotangent[0], *slices3],
+        [((D, FF), low_t), ((FF, D), low_t), ((rows, FF), wide_t)],
+        flops=2 * rows * D * (4 * FF + 2 * D),
+    )
+    cross_do_parts = exchange_pairs(cross_do_dealt)
+
+    def grads_of(depths, lefts, rights):
+        width = sum(depth * right.shape[1] for depth, right in zip(depths, rights))
+        return run(
+            functools.partial(weight_grads, depths),
+            [((4, 64, width), low_t)] * 2,
+            ids,
+            [*lefts, *rights],
+            [((left.shape[1], right.shape[1]), low_t) for left, right in zip(lefts, rights)],
+            flops=sum(2 * rows * a.shape[1] * b.shape[1] for a, b in zip(lefts, rights)),
+        )
+
+    keep_a, send_a = grads_of(
+        (1, 4, 1), (second_low, activated, cross_low), (pre_grad, branch, cross_branch)
+    )
+    parts_a = reduce_slices(ids, keep_a, send_a)
+
+    def back_of(is_self, q_parts, do_parts, x_parts, weights, code, low_limits, high_limits):
+        width = (3 if is_self else 2) * PAIR
+        return run(
+            functools.partial(pair_back, is_self),
+            [((4, rows, PAIR), low_t)] * 2
+            + [((4, rows, 2 * PAIR), low_t)] * 2
+            + [((256, width), low_t)] * 2,
+            ids,
+            [*q_parts, *do_parts, *x_parts, *weights, code, low_limits, high_limits],
+            [((8, rows, PAIR), low_t)] * 2
+            + [((keys, PAIR), low_t)] * 2
+            + [((PAIR, keys), low_t), ((8, PAIR, rows), low_t), ((8, rows, PAIR), low_t)]
+            + [((keys, PAIR), wide_t)] * 2
+            + [((keys, rows), wide_t), ((D, width), low_t)],
+            flops=16 * score_flops,
+        )
+
+    cq_keep, cq_send, ckv_keep, ckv_send, cw_keep, cw_send = back_of(
+        False,
+        cross_q_parts,
+        cross_do_parts,
+        source_parts,
+        [w_cross_pair],
+        source_wide,
+        token_rows,
+        token_rows,
+    )
+    cross_dq_parts = return_pairs(ids, cq_keep, cq_send)
+    first_grad, self_branch, self_dealt, cross_dq, sums = run(
+        first_back,
+        [
+            ((rows, D), wide_t),
+            ((rows, D), low_t),
+            ((PAIRS, rows, PAIR), low_t),
+            ((rows, D), low_t),
+            ((8, D), wide_t),
+        ],
+        ids,
+        [*cross_dq_parts, second_grad, normed, scale, gs, w_cross_query, w_output, sums],
+        flops=4 * rows * D * D,
+    )
+    self_do_parts = exchange_pairs(self_dealt)
+    keep_b, send_b = grads_of((1, 1), (first_low, self_low), (cross_dq, self_branch))
+    cross_dkv_parts = return_pairs(ids, ckv_keep, ckv_send)
+    (source_grad,) = run(
+        source_back,
+        [((rows, D), wide_t)],
+        ids,
+        [*cross_dkv_parts, w_cross_pair],
+        [((rows, 2 * D), low_t)],
+        flops=4 * rows * D * D,
+    )
+    parts_b = reduce_slices(ids, keep_b, send_b)
+    parts_c = reduce_halves(ids, cw_keep, cw_send)
+    for bits in (1, 2, 4):
+        sums = sums + swap(sums, "ctx", bits)
+    for bits in (1, 2):
+        sums = sums + swap(sums, "wa", bits)
+    norm_sums = lax.dynamic_slice_in_dim(sums, mw * 128, 128, 1)
+
+    q_keep, q_send, kv_keep, kv_send, w_keep, w_send = back_of(
+        True,
+        hidden_parts,
+        self_do_parts,
+        stream_parts,
+        [w_query, w_pair],
+        code_wide,
+        low_rows,
+        high_rows,
+    )
+    parts_d = reduce_halves(ids, w_keep, w_send)
+    dq_parts = return_pairs(ids, q_keep, q_send)
+    (hidden_grad,) = run(
+        hidden_back,
+        [((rows, D), wide_t)],
+        ids,
+        [*dq_parts, first_grad, w_query],
+        [((rows, D), low_t)],
+        flops=2 * rows * D * D,
+    )
+    dkv_parts = return_pairs(ids, kv_keep, kv_send)
+    (stream_grad,) = run(
+        source_back,
+        [((rows, D), wide_t)],
+        ids,
+        [*dkv_parts, w_pair],
+        [((rows, 2 * D), low_t)],
+        flops=4 * rows * D * D,
+    )
+
+    grad_in, grad_out, grad_cross_output = run(
+        functools.partial(place_rows, (1, 4, 1)),
+        [((128, FF), wide_t), ((D, D), wide_t), ((128, D), wide_t)],
+        ids,
+        parts_a,
+    )
+    grad_cross_query, grad_output = run(
+        functools.partial(place_rows, (1, 1)), [((128, D), wide_t)] * 2, ids, parts_b
+    )
+    (grad_cross_pair,) = run(place_pairs, [((128, 2 * D), wide_t)], ids, parts_c)
+    grad_query, grad_pair = run(
+        place_pairs, [((128, D), wide_t), ((128, 2 * D), wide_t)], ids, parts_d
+    )
+    return (
+        result[None],
+        hidden_grad[None],
+        stream_grad[None],
+        source_grad[None],
+        grad_query,
+        grad_pair,
+        grad_output,
+        grad_cross_query,
+        grad_cross_pair,
+        grad_cross_output,
+        grad_in,
+        grad_out,
+        norm_sums[0:3],
+        norm_sums[3:6],
+    )
+
+
 def solution(mesh):
     in_specs = (
         P("wa", "ctx", None),
@@ -424,4 +1156,6 @@
         P(None, "wa"),
         P(None, "wa"),
     )
-    return jax.shard_map(shards, mesh=mesh, in_specs=in_specs, out_specs=out_specs, check_vma=False)
+    fast = mesh.shape["ctx"] == HEADS and mesh.shape["wa"] == 4
+    body = fast_shards if fast else general_shards
+    return jax.shard_map(body, mesh=mesh, in_specs=in_specs, out_specs=out_specs, check_vma=False)

time: 841 us -> 443 us (0.53)
  waiting for transfers between devices: 389 us -> 128 us
  blocking collectives: 170 us -> 0 us
  Pallas kernels: 0 us -> 150 us
  starting transfers between devices: 0.95 us -> 118 us
  matrix products: 99.7 us -> 0 us
  local copies, waits for them, and re-layouts: 116 us -> 32.8 us
  other arithmetic: 29.2 us -> 5.85 us
  between operations: 15.7 us -> 2.7 us
  loops' own time: 9.44 us -> 0 us
    reduce_scatter x7 -> x0, waiting for transfers between devices: 215 us -> none  [the longest x1 58 us: shards(): lax.psum_scatter(self_terms, 'ctx', scatter_dimension=0, tiled=True)]
    pallas_call x0 -> x29, Pallas kernels: none -> 150 us  [run(): pl.pallas_call(body, out_shape=outs, in_specs=[smem_spec] + [vmem_spec] *...]
    ppermute x0 -> x146, waiting for transfers between devices: none -> 128 us  [swap(): return lax.ppermute(value, axis, [(i, i ^ bits) for i in range(size)])]
    ppermute x0 -> x146, starting transfers between devices: none -> 118 us  [swap(): return lax.ppermute(value, axis, [(i, i ^ bits) for i in range(size)])]
    unnamed x23 -> x0, waiting for transfers between devices: 110 us -> none
    dot_general x52 -> x0, matrix products: 99.7 us -> none  [the longest x24 46.3 us: matmul(): return jnp.dot(left, right, preferred_element_type=jnp.float32)]
    psum x1 -> x0, blocking collectives: 89.6 us -> none  [shards(): lax.psum((share_query, share_pair, share_output, share_cross_query, share...]
    all_gather x6 -> x0, blocking collectives: 80.3 us -> none  [the longest x1 16.5 us: shards(): lax.all_gather(self_output, 'wa', axis=0, tiled=True)]
  transfers between devices with their start and end apart: 18 -> 146, of which waited for: 14 -> 38; matrix products, arithmetic and copies ran while one was open for 21% -> 7% of each run, Pallas kernels for 0% -> 34%
where the time goes in v1:
time: 443 us; the launch traced here: 436 us
  Pallas kernels  150 us (34%)
  waiting for transfers between devices  128 us (29%)
  starting transfers between devices  118 us (27%)
  local copies, waits for them, and re-layouts  32.8 us (7%)
  other arithmetic  5.85 us (1%)
    pallas_call x29, Pallas kernels, run(): pl.pallas_call(body, out_shape=outs, in_specs=[smem_spec] + [vmem_spec] *...  150 us
    ppermute x146, waiting for transfers between devices, swap(): return lax.ppermute(value, axis, [(i, i ^ bits) for i in range(size)])  128 us
    ppermute x146, starting transfers between devices, swap(): return lax.ppermute(value, axis, [(i, i ^ bits) for i in range(size)])  118 us
    unnamed x301, local copies, waits for them, and re-layouts  13.7 us
  transfers between devices with their start and end apart: 146, of which 38 were waited for; matrix products, arithmetic and copies ran while one was open for 7% of the time, Pallas kernels for 34%

profile of v1, /device:TPU:0, one launch (start us, length us, event | category | flops | bytes accessed | tf_op | source)
XLA Modules:
  0.0 436.5 jit_solution(17523027606704502556)
XLA Ops:
  25.2 3.8 collective-permute-done.35.refs_18_
  30.4 4.1 collective-permute-done.36.refs_19_
  49.1 6.6 %collective-permute-done.13.refs_12_ = bf16[64,1536]{1,0:T(8,128)(2,1)S(1)} collective-permute-done((bf16[64,1536]{1,0:T(8,128)(2,1)S(1)}, bf16[64,1536]{1,0:T(8,128)(2,1)S(1)}, u32[]{:S(2)}, u32[]{:S(2)}) %collective-permute-start.13) | collective-permute-done | bytes 196640 | tf_op jit(solution)/shard_map/ppermute | solution.py:808
  55.8 3.9 collective-permute-start.18
  61.4 4.2 collective-permute-done.5.refs_6_.refs_22_
  77.5 7.8 %collective-permute-done.28.refs_10_ = bf16[64,2560]{1,0:T(8,128)(2,1)S(1)} collective-permute-done((bf16[64,2560]{1,0:T(8,128)(2,1)S(1)}, bf16[64,2560]{1,0:T(8,128)(2,1)S(1)}, u32[]{:S(2)}, u32[]{:S(2)}) %collective-permute-start.28) | collective-permute-done | bytes 327712 | tf_op jit(solution)/shard_map/ppermute | solution.py:808
  85.3 4.3 collective-permute-done.30.refs_12_
  101.7 5.2 %collective-permute-done.41.refs_2_ = bf16[64,4096]{1,0:T(8,128)(2,1)S(1)} collective-permute-done((bf16[64,4096]{1,0:T(8,128)(2,1)S(1)}, bf16[64,4096]{1,0:T(8,128)(2,1)S(1)}, u32[]{:S(2)}, u32[]{:S(2)}) %collective-permute-start.41) | collective-permute-done | bytes 524320 | tf_op jit(solution)/shard_map/ppermute | solution.py:808
  106.9 15.8 %shard_map.281 = (bf16[256,512]{1,0:T(8,128)(2,1)}, bf16[512,1536]{1,0:T(8,128)(2,1)}) custom-call(s32[2]{0:T(128)} %pad_add_fusion.ids, bf16[256,512]{1,0:T(8,128)(2,1)} %bitcast.73, bf16[256,512]{1,0:T(8,128)(2,1)} %bitcast.84, bf16[256,512]{1,0:T(8,128)(2,1)} %copy-done.99, bf16[256,512]{1,0:T(8,128)(2,1)} %copy-done.98, bf16[256,512]{1,0:T(8,128)(2,1)} %copy-done.100, ...), custom_call_target="tpu_custom_call" | custom-call | flops 4294967296 | bytes 5777408 | tf_op jit(solution)/shard_map/pallas_call | solution.py:406
  124.8 16.5 %shard_map.282 = (f32[256,512]{1,0:T(8,128)}, f32[256,512]{1,0:T(8,128)}, f32[256,128]{1,0:T(8,128)}, bf16[256,512]{1,0:T(8,128)(2,1)}, bf16[256,512]{1,0:T(8,12...) custom-call(s32[2]{0:T(128)} %pad_add_fusion.ids, ...), custom_call_target="tpu_custom_call" | custom-call | flops 4294967296 | bytes 9872384 | tf_op jit(solution)/shard_map/pallas_call | solution.py:406
  150.5 8.3 %shard_map.283 = (bf16[256,512]{1,0:T(8,128)(2,1)}, bf16[4,256,128]{2,1,0:T(8,128)(2,1)}, f32[256,512]{1,0:T(8,128)}, bf16[256,512]{1,0:T(8,128)(2,1)}, bf16[256...) custom-call(s32[2]{0:T(128)} %pad_add_fusion.ids, ...), custom_call_target="tpu_custom_call" | custom-call | flops 2415919104 | bytes 9732096 | tf_op jit(solution)/shard_map/pallas_call | solution.py:406
  167.1 5.6 %shard_map.305 = (bf16[4,64,4608]{2,1,0:T(8,128)(2,1)}, bf16[4,64,4608]{2,1,0:T(8,128)(2,1)}) custom-call(s32[2]{0:T(128)} %pad_add_fusion.ids, bf16[256,512]{1,0:T(8,128)(2,1)} %get-tuple-element.169.refs_0_, bf16[256,2048]{1,0:T(8,128)(2,1)} %get-tuple-element.170.refs_1_, bf16[256,512]{1,0:T(8,128)(2,1)} %get-tuple-element.103.cross_low.refs_2_, ...), custom_call_target="tpu_custom_call" | custom-call | flops 1207959552 | bytes 7864320 | tf_op jit(solution)/shard_map/pallas_call | solution.py:406
  177.0 25.6 %shard_map.284 = (bf16[4,256,128]{2,1,0:T(8,128)(2,1)}, bf16[4,256,128]{2,1,0:T(8,128)(2,1)}, bf16[4,256,256]{2,1,0:T(8,128)(2,1)}, bf16[4,256,256]{2,1,0:T(8,12...) custom-call(s32[2]{0:T(128)} %pad_add_fusion.ids, bf16[256,128]{1,0:T(8,128)(2,1)} %copy-done.44, ...), custom_call_target="tpu_custom_call" | custom-call | flops 8589934592 | bytes 7094272 | tf_op jit(solution)/shard_map/pallas_call | solution.py:406
  207.0 5.3 %collective-permute-done.52.refs_6_ = bf16[256,512]{1,0:T(8,128)(2,1)S(1)} collective-permute-done((bf16[256,512]{1,0:T(8,128)(2,1)S(1)}, bf16[256,512]{1,0:T(8,128)(2,1)S(1)}, u32[]{:S(2)}, u32[]{:S(2)}) %collective-permute-start.52) | collective-permute-done | bytes 262176 | tf_op jit(solution)/shard_map/ppermute | solution.py:808
  217.6 4.6 %collective-permute-done.71.refs_3_ = bf16[256,128]{1,0:T(8,128)(2,1)S(1)} collective-permute-done((bf16[256,128]{1,0:T(8,128)(2,1)}, bf16[256,128]{1,0:T(8,128)(2,1)S(1)}, u32[]{:S(2)}, u32[]{:S(2)}) %collective-permute-start.71) | collective-permute-done | bytes 65568 | tf_op jit(solution)/shard_map/ppermute | solution.py:808
  227.2 4.1 collective-permute-start.117
  251.6 27.8 %shard_map.287 = (bf16[4,256,128]{2,1,0:T(8,128)(2,1)}, bf16[4,256,128]{2,1,0:T(8,128)(2,1)}, bf16[4,256,256]{2,1,0:T(8,128)(2,1)}, bf16[4,256,256]{2,1,0:T(8,12...) custom-call(s32[2]{0:T(128)} %pad_add_fusion.ids, bf16[256,512]{1,0:T(8,128)(2,1)} %bitcast.75, ...), custom_call_target="tpu_custom_call" | custom-call | flops 8589934592 | bytes 9322496 | tf_op jit(solution)/shard_map/pallas_call | solution.py:406
  292.8 3.7 collective-permute-done.144
  308.6 3.7 collective-permute-done.94.refs_3_
  321.2 4.0 shard_map.306
  334.9 16.4 %collective-permute-done.80.refs_1_ = bf16[256,128]{1,0:T(8,128)(2,1)S(1)} collective-permute-done((bf16[256,128]{1,0:T(8,128)(2,1)}, bf16[256,128]{1,0:T(8,128)(2,1)S(1)}, u32[]{:S(2)}, u32[]{:S(2)}) %collective-permute-start.80) | collective-permute-done | bytes 65568 | tf_op jit(solution)/shard_map/ppermute | solution.py:808
  353.5 4.2 collective-permute-done.82.refs_3_
  359.9 4.7 %collective-permute-done.104.refs_2_ = bf16[64,1024]{1,0:T(8,128)(2,1)S(1)} collective-permute-done((bf16[64,1024]{1,0:T(8,128)(2,1)}, bf16[64,1024]{1,0:T(8,128)(2,1)S(1)}, u32[]{:S(2)}, u32[]{:S(2)}) %collective-permute-start.104) | collective-permute-done | bytes 131104 | tf_op jit(solution)/shard_map/ppermute | solution.py:808
  366.0 4.7 %collective-permute-done.105.refs_3_ = bf16[64,1024]{1,0:T(8,128)(2,1)S(1)} collective-permute-done((bf16[64,1024]{1,0:T(8,128)(2,1)}, bf16[64,1024]{1,0:T(8,128)(2,1)S(1)}, u32[]{:S(2)}, u32[]{:S(2)}) %collective-permute-start.105) | collective-permute-done | bytes 131104 | tf_op jit(solution)/shard_map/ppermute | solution.py:808
  (648 shorter events, 238.9 us)
Async XLA Ops:
  10.2 25.6 %collective-permute-start.24 = (bf16[16,2560]{1,0:T(8,128)(2,1)S(1)}, bf16[16,2560]{1,0:T(8,128)(2,1)S(1)}, u32[]{:S(2)}, u32[]{:S(2)}) collective-permute-start(bf16[16,2560]{1,0:T(8,128)(2,1)S(1)} %pad_maximum_fusion.3), channel_id=1, source_target_pairs={{0,1},{1,0},{2,3},{3,2},{4,5},{5,4},{6,7},{7,6},{8,9},{9,8},{10,11... | collective-permute-start | bytes 245768 | tf_op jit(solution)/shard_map/ppermute | solution.py:808
  11.1 25.6 %collective-permute-start.25 = (bf16[16,2560]{1,0:T(8,128)(2,1)S(1)}, bf16[16,2560]{1,0:T(8,128)(2,1)S(1)}, u32[]{:S(2)}, u32[]{:S(2)}) collective-permute-start(bf16[16,2560]{1,0:T(8,128)(2,1)S(1)} %pad_maximum_fusion.3), channel_id=1, source_target_pairs={{0,2},{1,3},{2,0},{3,1},{4,6},{5,7},{6,4},{7,5},{8,10},{9,11},{10,... | collective-permute-start | bytes 245768 | tf_op jit(solution)/shard_map/ppermute | solution.py:808
  18.4 22.9 %collective-permute-start.37 = (bf16[16,4096]{1,0:T(8,128)(2,1)S(1)}, bf16[16,4096]{1,0:T(8,128)(2,1)S(1)}, u32[]{:S(2)}, u32[]{:S(2)}) collective-permute-start(bf16[16,4096]{1,0:T(8,128)(2,1)S(1)} %dynamic-slice_dynamic-update-slice_fusion.1), channel_id=1, source_target_pairs={{0,1},{1,0},{2,3},{3,2},{4,5},{5,4},{6,7},{7,6},{8,9},{9,8},{10,11... | collective-permute-start | bytes 393224 | tf_op jit(solution)/shard_map/ppermute | solution.py:808
  18.6 29.7 %collective-permute-start.11 = (bf16[64,1536]{1,0:T(8,128)(2,1)S(1)}, bf16[64,1536]{1,0:T(8,128)(2,1)S(1)}, u32[]{:S(2)}, u32[]{:S(2)}) collective-permute-start(bf16[64,1536]{1,0:T(8,128)(2,1)S(1)} %pad_maximum_fusion.2.refs_8_), channel_id=1, source_target_pairs={{0,8},{4,12},{8,0},{12,4},{16,24},{20,28},{24,16},{28,20},{1,9},{5... | collective-permute-start | bytes 589832 | tf_op jit(solution)/shard_map/ppermute | solution.py:808
  93.5 29.3 %collective-permute-start.43 = (bf16[64,4096]{1,0:T(8,128)(2,1)S(1)}, bf16[64,4096]{1,0:T(8,128)(2,1)S(1)}, u32[]{:S(2)}, u32[]{:S(2)}) collective-permute-start(bf16[64,4096]{1,0:T(8,128)(2,1)S(1)} %pad_maximum_fusion.refs_0_), channel_id=1, source_target_pairs={{0,16},{4,20},{8,24},{12,28},{16,0},{20,4},{24,8},{28,12},{1,17},{... | collective-permute-start | bytes 1572872 | tf_op jit(solution)/shard_map/ppermute | solution.py:808
  94.7 28.6 %collective-permute-start.45 = (bf16[64,4096]{1,0:T(8,128)(2,1)S(1)}, bf16[64,4096]{1,0:T(8,128)(2,1)S(1)}, u32[]{:S(2)}, u32[]{:S(2)}) collective-permute-start(bf16[64,4096]{1,0:T(8,128)(2,1)S(1)} %pad_maximum_fusion.refs_0_), channel_id=1, source_target_pairs={{0,24},{4,28},{8,16},{12,20},{16,8},{20,12},{24,0},{28,4},{1,25},{... | collective-permute-start | bytes 1572872 | tf_op jit(solution)/shard_map/ppermute | solution.py:808
  123.3 25.7 %collective-permute-start.42 = (bf16[64,4096]{1,0:T(8,128)(2,1)S(1)}, bf16[64,4096]{1,0:T(8,128)(2,1)S(1)}, u32[]{:S(2)}, u32[]{:S(2)}) collective-permute-start(bf16[64,4096]{1,0:T(8,128)(2,1)S(1)} %collective-permute-done.41.refs_2_), channel_id=1, source_target_pairs={{0,4},{4,0},{8,12},{12,8},{16,20},{20,16},{24,28},{28,24},{1,5},{5... | collective-permute-start | bytes 1572872 | tf_op jit(solution)/shard_map/ppermute | solution.py:808
  123.5 25.9 %collective-permute-start.44 = (bf16[64,4096]{1,0:T(8,128)(2,1)S(1)}, bf16[64,4096]{1,0:T(8,128)(2,1)S(1)}, u32[]{:S(2)}, u32[]{:S(2)}) collective-permute-start(bf16[64,4096]{1,0:T(8,128)(2,1)S(1)} %collective-permute-done.43.refs_4_), channel_id=1, source_target_pairs={{0,4},{4,0},{8,12},{12,8},{16,20},{20,16},{24,28},{28,24},{1,5},{5... | collective-permute-start | bytes 1572872 | tf_op jit(solution)/shard_map/ppermute | solution.py:808
  123.8 25.7 %collective-permute-start.46 = (bf16[64,4096]{1,0:T(8,128)(2,1)S(1)}, bf16[64,4096]{1,0:T(8,128)(2,1)S(1)}, u32[]{:S(2)}, u32[]{:S(2)}) collective-permute-start(bf16[64,4096]{1,0:T(8,128)(2,1)S(1)} %collective-permute-done.45.refs_6_), channel_id=1, source_target_pairs={{0,4},{4,0},{8,12},{12,8},{16,20},{20,16},{24,28},{28,24},{1,5},{5... | collective-permute-start | bytes 1572872 | tf_op jit(solution)/shard_map/ppermute | solution.py:808
  172.7 31.2 %collective-permute-start.48 = (bf16[256,512]{1,0:T(8,128)(2,1)S(1)}, bf16[256,512]{1,0:T(8,128)(2,1)S(1)}, u32[]{:S(2)}, u32[]{:S(2)}) collective-permute-start(bf16[256,512]{1,0:T(8,128)(2,1)S(1)} %bitcast.76), channel_id=1, source_target_pairs={{0,8},{4,12},{8,0},{12,4},{16,24},{20,28},{24,16},{28,20},{1,9},{5... | collective-permute-start | bytes 786440 | tf_op jit(solution)/shard_map/ppermute | solution.py:808
  174.6 29.3 %collective-permute-start.50 = (bf16[256,512]{1,0:T(8,128)(2,1)S(1)}, bf16[256,512]{1,0:T(8,128)(2,1)S(1)}, u32[]{:S(2)}, u32[]{:S(2)}) collective-permute-start(bf16[256,512]{1,0:T(8,128)(2,1)S(1)} %bitcast.77), channel_id=1, source_target_pairs={{0,16},{4,20},{8,24},{12,28},{16,0},{20,4},{24,8},{28,12},{1,17},{... | collective-permute-start | bytes 786440 | tf_op jit(solution)/shard_map/ppermute | solution.py:808
  175.6 144.1 %collective-permute-start.127 = (bf16[4,64,4608]{2,1,0:T(8,128)(2,1)}, bf16[4,64,4608]{2,1,0:T(8,128)(2,1)S(1)}, u32[]{:S(2)}, u32[]{:S(2)}) collective-permute-start(bf16[4,64,4608]{2,1,0:T(8,128)(2,1)} %get-tuple-element.175), channel_id=1, source_target_pairs={{0,4},{4,0},{8,12},{12,8},{16,20},{20,16},{24,28},{28,24},{1,5},{5... | collective-permute-start | bytes 7077896 | tf_op jit(solution)/shard_map/ppermute | solution.py:808
  203.9 23.3 %collective-permute-start.47 = (bf16[256,512]{1,0:T(8,128)(2,1)S(1)}, bf16[256,512]{1,0:T(8,128)(2,1)S(1)}, u32[]{:S(2)}, u32[]{:S(2)}) collective-permute-start(bf16[256,512]{1,0:T(8,128)(2,1)S(1)} %bitcast.79), channel_id=1, source_target_pairs={{0,4},{4,0},{8,12},{12,8},{16,20},{20,16},{24,28},{28,24},{1,5},{5... | collective-permute-start | bytes 786440 | tf_op jit(solution)/shard_map/ppermute | solution.py:808
  203.9 27.4 %collective-permute-start.49 = (bf16[256,512]{1,0:T(8,128)(2,1)S(1)}, bf16[256,512]{1,0:T(8,128)(2,1)S(1)}, u32[]{:S(2)}, u32[]{:S(2)}) collective-permute-start(bf16[256,512]{1,0:T(8,128)(2,1)S(1)} %collective-permute-done.48.refs_2_), channel_id=1, source_target_pairs={{0,4},{4,0},{8,12},{12,8},{16,20},{20,16},{24,28},{28,24},{1,5},{5... | collective-permute-start | bytes 786440 | tf_op jit(solution)/shard_map/ppermute | solution.py:808
  246.4 40.6 %collective-permute-start.87 = (bf16[4,256,256]{2,1,0:T(8,128)(2,1)S(1)}, bf16[4,256,256]{2,1,0:T(8,128)(2,1)S(1)}, u32[]{:S(2)}, u32[]{:S(2)}) collective-permute-start(bf16[4,256,256]{2,1,0:T(8,128)(2,1)S(1)} %copy-done.82), channel_id=1, source_target_pairs={{0,4},{4,0},{8,12},{12,8},{16,20},{20,16},{24,28},{28,24},{1,5},{5... | collective-permute-start | bytes 1572872 | tf_op jit(solution)/shard_map/ppermute | solution.py:808
  246.6 32.7 %collective-permute-start.121 = (bf16[64,256]{1,0:T(8,128)(2,1)}, bf16[64,256]{1,0:T(8,128)(2,1)S(1)}, u32[]{:S(2)}, u32[]{:S(2)}) collective-permute-start(bf16[64,256]{1,0:T(8,128)(2,1)} %shard_map.303.refs_0_), channel_id=1, source_target_pairs={{0,8},{4,12},{8,0},{12,4},{16,24},{20,28},{24,16},{28,20},{1,9},{5... | collective-permute-start | bytes 98312 | tf_op jit(solution)/shard_map/ppermute | solution.py:808
  247.4 32.0 %collective-permute-start.123 = (bf16[64,256]{1,0:T(8,128)(2,1)}, bf16[64,256]{1,0:T(8,128)(2,1)S(1)}, u32[]{:S(2)}, u32[]{:S(2)}) collective-permute-start(bf16[64,256]{1,0:T(8,128)(2,1)} %shard_map.303.refs_0_), channel_id=1, source_target_pairs={{0,16},{4,20},{8,24},{12,28},{16,0},{20,4},{24,8},{28,12},{1,17},{... | collective-permute-start | bytes 98312 | tf_op jit(solution)/shard_map/ppermute | solution.py:808
  248.9 31.1 %collective-permute-start.125 = (bf16[64,256]{1,0:T(8,128)(2,1)}, bf16[64,256]{1,0:T(8,128)(2,1)S(1)}, u32[]{:S(2)}, u32[]{:S(2)}) collective-permute-start(bf16[64,256]{1,0:T(8,128)(2,1)} %shard_map.303.refs_0_), channel_id=1, source_target_pairs={{0,24},{4,28},{8,16},{12,20},{16,8},{20,12},{24,0},{28,4},{1,25},{... | collective-permute-start | bytes 98312 | tf_op jit(solution)/shard_map/ppermute | solution.py:808
  282.8 49.3 %collective-permute-start.102 = (bf16[4,64,1024]{2,1,0:T(8,128)(2,1)}, bf16[4,64,1024]{2,1,0:T(8,128)(2,1)S(1)}, u32[]{:S(2)}, u32[]{:S(2)}) collective-permute-start(bf16[4,64,1024]{2,1,0:T(8,128)(2,1)} %get-tuple-element.152), channel_id=1, source_target_pairs={{0,4},{4,0},{8,12},{12,8},{16,20},{20,16},{24,28},{28,24},{1,5},{5... | collective-permute-start | bytes 1572872 | tf_op jit(solution)/shard_map/ppermute | solution.py:808
  299.3 25.9 %collective-permute-start.79 = (bf16[4,256,128]{2,1,0:T(8,128)(2,1)S(1)}, bf16[4,256,128]{2,1,0:T(8,128)(2,1)S(1)}, u32[]{:S(2)}, u32[]{:S(2)}) collective-permute-start(bf16[4,256,128]{2,1,0:T(8,128)(2,1)S(1)} %copy-done.108), channel_id=1, source_target_pairs={{0,4},{4,0},{8,12},{12,8},{16,20},{20,16},{24,28},{28,24},{1,5},{5... | collective-permute-start | bytes 786440 | tf_op jit(solution)/shard_map/ppermute | solution.py:808
  325.2 48.0 %collective-permute-start.128 = (bf16[64,4608]{1,0:T(8,128)(2,1)}, bf16[64,4608]{1,0:T(8,128)(2,1)S(1)}, u32[]{:S(2)}, u32[]{:S(2)}) collective-permute-start(bf16[64,4608]{1,0:T(8,128)(2,1)} %get-tuple-element.177), channel_id=1, source_target_pairs={{0,8},{4,12},{8,0},{12,4},{16,24},{20,28},{24,16},{28,20},{1,9},{5... | collective-permute-start | bytes 1769480 | tf_op jit(solution)/shard_map/ppermute | solution.py:808
  326.5 49.8 %collective-permute-start.129 = (bf16[64,4608]{1,0:T(8,128)(2,1)}, bf16[64,4608]{1,0:T(8,128)(2,1)S(1)}, u32[]{:S(2)}, u32[]{:S(2)}) collective-permute-start(bf16[64,4608]{1,0:T(8,128)(2,1)} %get-tuple-element.178), channel_id=1, source_target_pairs={{0,16},{4,20},{8,24},{12,28},{16,0},{20,4},{24,8},{28,12},{1,17},{... | collective-permute-start | bytes 1769480 | tf_op jit(solution)/shard_map/ppermute | solution.py:808
  327.4 50.3 %collective-permute-start.130 = (bf16[64,4608]{1,0:T(8,128)(2,1)}, bf16[64,4608]{1,0:T(8,128)(2,1)S(1)}, u32[]{:S(2)}, u32[]{:S(2)}) collective-permute-start(bf16[64,4608]{1,0:T(8,128)(2,1)} %get-tuple-element.179), channel_id=1, source_target_pairs={{0,24},{4,28},{8,16},{12,20},{16,8},{20,12},{24,0},{28,4},{1,25},{... | collective-permute-start | bytes 1769480 | tf_op jit(solution)/shard_map/ppermute | solution.py:808
  359.9 43.5 %collective-permute-start.83 = (bf16[4,256,256]{2,1,0:T(8,128)(2,1)S(1)}, bf16[4,256,256]{2,1,0:T(8,128)(2,1)S(1)}, u32[]{:S(2)}, u32[]{:S(2)}) collective-permute-start(bf16[4,256,256]{2,1,0:T(8,128)(2,1)S(1)} %copy-done.81), channel_id=1, source_target_pairs={{0,4},{4,0},{8,12},{12,8},{16,20},{20,16},{24,28},{28,24},{1,5},{5... | collective-permute-start | bytes 1572872 | tf_op jit(solution)/shard_map/ppermute | solution.py:808
  (268 other events, 4277.7 us)

commit v2 on v0

--- a/solution.py
+++ b/solution.py
@@ -1,6 +1,11 @@
+import functools
+
 import jax
 import jax.numpy as jnp
 from jax import lax
+from jax.experimental import pallas as pl
+from jax.experimental.pallas import tpu as pltpu
+from jax.sharding import Mesh
 from jax.sharding import PartitionSpec as P
 
 D = 512
@@ -154,7 +159,7 @@
     return jnp.dot(left, right, preferred_element_type=jnp.float32)
 
 
-def shards(
+def general_shards(
     hidden,
     stream,
     encoder,
@@ -387,6 +392,809 @@
     )
 
 
+PAIR = 2 * HEAD
+PAIRS = HEADS // 2
+FF = 2048
+low_t = jnp.bfloat16
+wide_t = jnp.float32
+vmem_spec = pl.BlockSpec(memory_space=pltpu.VMEM)
+smem_spec = pl.BlockSpec(memory_space=pltpu.SMEM)
+
+
+def run(body, outs, ids, args, scratch=(), us=2, vmem=56):
+    outs = [jax.ShapeDtypeStruct(shape, kind) for shape, kind in outs]
+    moved = sum(a.size * a.dtype.itemsize for a in list(args) + outs)
+    return pl.pallas_call(
+        body,
+        name=getattr(body, "func", body).__name__,
+        out_shape=outs,
+        in_specs=[smem_spec] + [vmem_spec] * len(args),
+        out_specs=[vmem_spec] * len(outs),
+        scratch_shapes=[pltpu.VMEM(shape, kind) for shape, kind in scratch],
+        compiler_params=pltpu.CompilerParams(vmem_limit_bytes=vmem * 1024 * 1024),
+        cost_estimate=pl.CostEstimate(flops=us * 1_000_000_000, bytes_accessed=moved, transcendentals=0),
+    )(ids, *args)
+
+
+def dot_nn(a, b):
+    return lax.dot_general(a, b, (((1,), (0,)), ((), ())), preferred_element_type=wide_t)
+
+
+def dot_nt(a, b):
+    return lax.dot_general(a, b, (((1,), (1,)), ((), ())), preferred_element_type=wide_t)
+
+
+def dot_tn(a, b):
+    return lax.dot_general(a, b, (((0,), (0,)), ((), ())), preferred_element_type=wide_t)
+
+
+def at16(start, size=16):
+    return pl.ds(pl.multiple_of(start, 16), size)
+
+
+def at128(start, size=128):
+    return pl.ds(pl.multiple_of(start, 128), size)
+
+
+def half_mask(shape, axis, core):
+    return (lax.broadcasted_iota(jnp.int32, shape, axis) // HEAD) == core
+
+
+def attend_rows(q_ref, kv_ref, bias_ref, out_ref):
+    rows, keys = bias_ref.shape
+    chunk = rows // 2
+
+    def step(i, carry):
+        p, r = i // 2, i % 2
+        here = pl.ds(pl.multiple_of(r * chunk, chunk), chunk)
+        q = q_ref[here, at128(p * PAIR)]
+        first = half_mask((chunk, PAIR), 1, 0)
+        both = jnp.concatenate(
+            (jnp.where(first, q, jnp.zeros_like(q)), jnp.where(first, jnp.zeros_like(q), q)), axis=0
+        )
+        bias = bias_ref[here, :]
+        s = dot_nt(both, kv_ref[:, at128(p * PAIR)]) + jnp.concatenate((bias, bias), axis=0)
+        top = jnp.max(s, axis=1, keepdims=True)
+        w = jnp.exp(s - top)
+        total = jnp.sum(w, axis=1, keepdims=True)
+        mixed = dot_nn(w.astype(low_t), kv_ref[:, at128(D + p * PAIR)]) / total
+        out_ref[here, at128(p * PAIR)] = jnp.where(first, mixed[:chunk], mixed[chunk:]).astype(low_t)
+        return carry
+
+    lax.fori_loop(0, 2 * PAIRS, step, 0)
+
+
+def assemble(ids, parts, column, outs):
+    for chip, other, block in parts:
+        own = chip * 2 + (ids[1] ^ other)
+        for e in range(4):
+            rows = at16((ids[2] ^ e) * 128 + own * 16)
+            start = column
+            for out in outs:
+                width = out.shape[1]
+                out[rows, :] = block[e * 16 : (e + 1) * 16, start : start + width]
+                start += width
+
+
+def project_pairs(parts, weight, kv_ref):
+    for n, part in enumerate(parts):
+        for k in range(PAIRS):
+            rows = part.shape[1]
+            start = (n * 4 + k) * rows
+            kv_ref[start : start + rows, :] = dot_nn(part[k], weight[...]).astype(low_t)
+
+
+def self_forward(ids, hidden, own, other, slices, other_slices, *refs):
+    code, low_row, high_row, out, wq, wkv, q_ref, kv_ref, bias_ref = refs
+    rows = hidden.shape[0]
+    parts = [(k, n, part.at[k]) for n, part in enumerate((slices, other_slices)) for k in range(4)]
+    assemble(ids, parts, 0, (wq, wkv))
+    q_ref[...] = (dot_nn(hidden[...], wq[...]).astype(low_t) * 0.125).astype(low_t)
+    project_pairs((own, other), wkv, kv_ref)
+    k = code[...]
+    seen = (k >= low_row[...]) & (k < high_row[...])
+    bias_ref[...] = jnp.where(seen, 0.0, neg_fill)
+    mine = lax.broadcasted_iota(jnp.int32, (rows, rows), 0) == lax.broadcasted_iota(
+        jnp.int32, (rows, rows), 1
+    )
+    block = at128(ids[0] * rows, rows)
+    bias_ref[:, block] = jnp.where(mine, 0.0, bias_ref[:, block])
+    attend_rows(q_ref, kv_ref, bias_ref, out)
+
+
+def layer_norm(values, gain_row, shift_row):
+    mean = jnp.mean(values, axis=1, keepdims=True)
+    centred = values - mean
+    scale = lax.rsqrt(jnp.mean(centred * centred, axis=1, keepdims=True) + layer_eps)
+    normed = centred * scale
+    return normed * gain_row + shift_row, normed, scale
+
+
+def layer_norm_back(grad, normed, scale, gain_row):
+    gain_term = jnp.sum(grad * normed, axis=0, keepdims=True)
+    shift_term = jnp.sum(grad, axis=0, keepdims=True)
+    scaled = grad * gain_row
+    grad_in = scale * (
+        scaled
+        - jnp.mean(scaled, axis=1, keepdims=True)
+        - normed * jnp.mean(scaled * normed, axis=1, keepdims=True)
+    )
+    return grad_in, gain_term, shift_term
+
+
+def cross_forward(ids, hidden, self_low, own, other, *refs):
+    slices = refs[:2]
+    code, seq_col = refs[2:4]
+    first, normed, scale_out, first_low, cross_low, cross_q = refs[4:10]
+    wo, wcq, wckv, wco, gs, q_ref, kv_ref, bias_ref = refs[10:]
+    parts = [(k, n, slices[n].at[k]) for n in range(2) for k in range(4)]
+    assemble(ids, parts, 0, (wo, wcq, wckv, wco))
+    for e in range(4):
+        gs[:, at128((ids[2] ^ e) * 128)] = slices[0][0, e * 16 : (e + 1) * 16, 5 * D :]
+    gain, shift = gs[0:1, :].astype(wide_t), gs[3:4, :].astype(wide_t)
+    value, n0, s0 = layer_norm(
+        hidden[...].astype(wide_t) + dot_nn(self_low[...], wo[...]), gain, shift
+    )
+    first[...] = value
+    normed[...] = n0
+    scale_out[...] = jnp.broadcast_to(s0, scale_out.shape)
+    low = value.astype(low_t)
+    first_low[...] = low
+    q = dot_nn(low, wcq[...]).astype(low_t)
+    cross_q[...] = q
+    q_ref[...] = (q * 0.125).astype(low_t)
+    project_pairs((own, other), wckv, kv_ref)
+    bias_ref[...] = jnp.where(code[...] == seq_col[...], 0.0, neg_fill)
+    attend_rows(q_ref, kv_ref, bias_ref, cross_low)
+
+
+def feed_forward(ids, first, cross_low, cross_q, wco, gs, cotangent, *refs):
+    halves = refs[0:2]
+    (result, dealt, second_grad, second_low, activated, pre_grad, branch, cross_branch, sums) = refs[2:11]
+    slope, wins, wouts = refs[11:]
+    for n, half in enumerate(halves):
+        for w in range(4):
+            wins[n, w * 128 : (w + 1) * 128, :] = half[w, :128, :]
+            for k in range(2):
+                start = w * 256 + k * 128
+                wouts[n, start : start + 128, :] = half[w, 128:, k * D : (k + 1) * D]
+    gains, shifts = gs[0:3, :].astype(wide_t), gs[3:6, :].astype(wide_t)
+    second, n1, s1 = layer_norm(
+        first[...] + dot_nn(cross_low[...], wco[...]), gains[1:2], shifts[1:2]
+    )
+    low = second.astype(low_t)
+    second_low[...] = low
+    width = 512
+    chunks = [(n, c) for n in range(2) for c in range(FF // 2 // width)]
+    total = second
+    for n, c in chunks:
+        here = slice(c * width, (c + 1) * width)
+        cols = slice(n * (FF // 2) + c * width, n * (FF // 2) + (c + 1) * width)
+        pre = dot_nn(low, wins[n, :, here])
+        sig = 1.0 / (1.0 + jnp.exp(-pre))
+        act = (pre * sig).astype(low_t)
+        activated[:, cols] = act
+        slope[:, cols] = sig * (1.0 + pre * (1.0 - sig))
+        total = total + dot_nn(act, wouts[n, here, :])
+    value, n2, s2 = layer_norm(total, gains[2:3], shifts[2:3])
+    result[...] = value.astype(low_t)
+    third, gain_c, shift_c = layer_norm_back(cotangent[...].astype(wide_t), n2, s2, gains[2:3])
+    third_low = third.astype(low_t)
+    branch[...] = third_low
+    total = third
+    for n, c in chunks:
+        here = slice(c * width, (c + 1) * width)
+        cols = slice(n * (FF // 2) + c * width, n * (FF // 2) + (c + 1) * width)
+        back = (dot_nt(third_low, wouts[n, here, :]) * slope[:, cols]).astype(low_t)
+        pre_grad[:, cols] = back
+        total = total + dot_nt(back, wins[n, :, here])
+    grad, gain_b, shift_b = layer_norm_back(total, n1, s1, gains[1:2])
+    second_grad[...] = grad
+    grad_low = grad.astype(low_t)
+    cross_branch[...] = grad_low
+    mixed = dot_nt(grad_low, wco[...]).astype(low_t)
+    for p in range(PAIRS):
+        dealt[p, :, :PAIR] = cross_q[:, p * PAIR : (p + 1) * PAIR]
+        dealt[p, :, PAIR:] = mixed[:, p * PAIR : (p + 1) * PAIR]
+    zero = jnp.zeros_like(gain_b)
+    sums[...] = jnp.concatenate((zero, gain_b, gain_c, zero, shift_b, shift_c, zero, zero), axis=0)
+
+
+def put_slices(ids, value, keep, send, column):
+    width = value.shape[1]
+    for other, out in enumerate((keep, send)):
+        for chip in range(4):
+            own = chip * 2 + (ids[1] ^ other)
+            for e in range(4):
+                rows = at16((ids[2] ^ e) * 128 + own * 16)
+                out[chip, e * 16 : (e + 1) * 16, column : column + width] = value[rows, :]
+
+
+def grads_a(ids, second_low, pre_grad, activated, branch, cross_low, cross_branch, *refs):
+    keep, send, g_in, g_out, g_cross = refs
+    core, mw = ids[1], ids[2]
+    g_in[...] = dot_tn(second_low[...], pre_grad[...]).astype(low_t)
+    g_out[...] = dot_tn(activated[...], branch[...]).astype(low_t)
+    g_cross[...] = dot_tn(cross_low[...], cross_branch[...]).astype(low_t)
+    put_slices(ids, g_cross, keep, send, 2 * FF)
+    half = FF // 2
+    for other, out in enumerate((keep, send)):
+        for chip in range(4):
+            own = chip * 2 + (core ^ other)
+            for e in range(4):
+                w, here = mw ^ e, slice(e * 16, (e + 1) * 16)
+                rows = at16(w * 128 + own * 16)
+                for n in range(2):
+                    for k in range(4):
+                        out[chip, here, at128(k * 512 + (core ^ n) * 256, 256)] = g_in[
+                            rows, n * half + k * 256 : n * half + (k + 1) * 256
+                        ]
+                for g in range(4):
+                    row = (core ^ (chip // 2)) * half + w * 256 + (own % 4) * 64 + g * 16
+                    out[chip, here, FF + g * D : FF + (g + 1) * D] = g_out[at16(row), :]
+
+
+def grads_b(ids, first_low, cross_dq, self_low, branch, sums, keep, send, g_query, g_output):
+    g_query[...] = dot_tn(first_low[...], cross_dq[...]).astype(low_t)
+    g_output[...] = dot_tn(self_low[...], branch[...]).astype(low_t)
+    put_slices(ids, g_query, keep, send, 0)
+    put_slices(ids, g_output, keep, send, D)
+    row = jnp.concatenate((sums[...], jnp.zeros_like(sums[...])), axis=0).astype(low_t)
+    for e in range(4):
+        w = ids[2] ^ e
+        piece = row[:, :128]
+        for k in range(1, 4):
+            piece = jnp.where(w == k, row[:, k * 128 : (k + 1) * 128], piece)
+        for out in (keep, send):
+            for chip in range(4):
+                out[chip, e * 16 : (e + 1) * 16, 2 * D :] = piece
+
+
+def pair_back(is_self, ids, *refs):
+    at = 0
+
+    def take(n):
+        nonlocal at
+        at += n
+        return refs[at - n : at]
+
+    if is_self:
+        hidden_parts, do_parts, x_parts = take(2), take(2), take(2)
+        w_query, w_pair, code, low_rows, high_rows = take(5)
+        keep, send = take(2)
+    else:
+        both_parts, x_parts = take(2), take(2)
+        w_pair, code, low_rows = take(3)
+        dq_keep, dq_send, keep, send = take(4)
+    q_all, do_all, k_all, v_all, kt, dq_t, dq_all, dk, dv, s_ref, grads = take(11)
+    chip, core, mw = ids[0], ids[1], ids[2]
+    rows = q_all.shape[1]
+    mine = half_mask((rows, PAIR), 1, core)
+    nothing = jnp.zeros((rows, PAIR), low_t)
+    pair = at128(chip * PAIR)
+    if is_self:
+        wq = w_query[:, pair]
+    wk, wv = w_pair[:, pair], w_pair[:, at128(D + chip * PAIR)]
+    for n in range(2):
+        for k in range(4):
+            b = n * 4 + k
+            here = slice(b * rows, (b + 1) * rows)
+            x = x_parts[n][k]
+            k_all[here, :] = dot_nn(x, wk).astype(low_t)
+            v_all[here, :] = dot_nn(x, wv).astype(low_t)
+            if is_self:
+                q, do = dot_nn(hidden_parts[n][k], wq).astype(low_t), do_parts[n][k]
+            else:
+                q, do = both_parts[n][k, :, :PAIR], both_parts[n][k, :, PAIR:]
+            q_all[b] = (jnp.where(mine, q, nothing) * 0.125).astype(low_t)
+            do_all[b] = jnp.where(mine, do, nothing)
+    kt[...] = k_all[...].astype(wide_t).T.astype(low_t)
+    dk[...] = jnp.zeros_like(dk)
+    dv[...] = jnp.zeros_like(dv)
+
+    def step(b, carry):
+        q, do = q_all[b], do_all[b]
+        c = jnp.concatenate((code[...],) * (rows // 128), axis=1)
+        low_row = low_rows[pl.ds(b, 1), :]
+        s = dot_nt(k_all[...], q)
+        if is_self:
+            s_ref[...] = jnp.where((c >= low_row) & (c < high_rows[pl.ds(b, 1), :]), s, neg_fill)
+            block = at128(b * rows, rows)
+            own = lax.broadcasted_iota(jnp.int32, (rows, rows), 0) == lax.broadcasted_iota(
+                jnp.int32, (rows, rows), 1
+            )
+            s_ref[block, :] = jnp.where(own, dot_nt(k_all[block, :], q), s_ref[block, :])
+        else:
+            s_ref[...] = jnp.where(c == low_row, s, neg_fill)
+        s = s_ref[...]
+        w = jnp.exp(s - jnp.max(s, axis=0, keepdims=True))
+        inverse = 1.0 / jnp.sum(w, axis=0, keepdims=True)
+        dp = dot_nt(v_all[...], do)
+        offset = jnp.sum(w * dp, axis=0, keepdims=True) * inverse
+        probs = w * inverse
+        dv[...] += dot_nn(probs.astype(low_t), do)
+        ds = (probs * (dp - offset)).astype(low_t)
+        dk[...] += dot_nn(ds, q)
+        dqt = dot_nn(kt[...], ds) * 0.125
+        dqt = jnp.where(half_mask((PAIR, rows), 0, core), dqt, 0.0)
+        dq_t[b] = dqt.astype(low_t)
+        dq_all[b] = dqt.T.astype(low_t)
+        return carry
+
+    lax.fori_loop(0, 8, step, 0)
+    total_q = jnp.zeros((PAIR, D), wide_t)
+    total_k, total_v = total_q, total_q
+    at_kv = PAIR if is_self else 0
+    for n, out in enumerate((keep, send)):
+        for k in range(4):
+            b = n * 4 + k
+            here = slice(b * rows, (b + 1) * rows)
+            dk_low, dv_low = dk[here, :].astype(low_t), dv[here, :].astype(low_t)
+            if is_self:
+                out[k, :, :PAIR] = dq_all[b]
+            else:
+                (dq_keep, dq_send)[n][k] = dq_all[b]
+            out[k, :, at_kv : at_kv + PAIR] = dk_low
+            out[k, :, at_kv + PAIR :] = dv_low
+            x = x_parts[n][k]
+            total_k += dot_tn(dk_low, x)
+            total_v += dot_tn(dv_low, x)
+            if is_self:
+                total_q += dot_nn(dq_t[b], hidden_parts[n][k])
+    totals = (total_q, total_k, total_v) if is_self else (total_k, total_v)
+    for n, value in enumerate(totals):
+        grads[:, n * PAIR : (n + 1) * PAIR] = value.T.astype(low_t)
+    for e in range(4):
+        row, here = (mw ^ e) * 128, slice(e * 64, (e + 1) * 64)
+        keep[4, here, :] = grads[at16(row + core * 64, 64), :]
+        send[4, here, :] = grads[at16(row + (1 - core) * 64, 64), :]
+
+
+def first_back(ids, back, second_grad, normed, scale, gs, wcq, wo, sums_in, *refs):
+    first_grad, branch, dealt, dq, sums = refs
+    for p in range(PAIRS):
+        dq[:, p * PAIR : (p + 1) * PAIR] = back[p]
+    total = second_grad[...] + dot_nt(dq[...], wcq[...])
+    grad, gain_a, shift_a = layer_norm_back(
+        total, normed[...], scale[:, 0:1], gs[0:1, :].astype(wide_t)
+    )
+    first_grad[...] = grad
+    low = grad.astype(low_t)
+    branch[...] = low
+    mixed = dot_nt(low, wo[...]).astype(low_t)
+    for p in range(PAIRS):
+        dealt[p] = mixed[:, p * PAIR : (p + 1) * PAIR]
+    zero = jnp.zeros_like(gain_a)
+    sums[...] = sums_in[...] + jnp.concatenate(
+        (gain_a, zero, zero, shift_a, zero, zero, zero, zero), axis=0
+    )
+
+
+def source_back(ids, parts, wckv, out, dkv):
+    base = parts.shape[2] - 8 * PAIR
+    for p in range(PAIRS):
+        for g in range(4):
+            rows = slice(g * 64, (g + 1) * 64)
+            start = base + g * 2 * PAIR
+            dkv[rows, p * PAIR : (p + 1) * PAIR] = parts[p, :, start : start + PAIR]
+            dkv[rows, D + p * PAIR : D + (p + 1) * PAIR] = parts[
+                p, :, start + PAIR : start + 2 * PAIR
+            ]
+    out[...] = dot_nt(dkv[...], wckv[...])
+
+
+def hidden_back(ids, back, first_grad, wq, wkv, hidden_grad, stream_grad, dq, dkv):
+    for p in range(PAIRS):
+        dq[:, p * PAIR : (p + 1) * PAIR] = back[p, :, :PAIR]
+        dkv[:, p * PAIR : (p + 1) * PAIR] = back[p, :, PAIR : 2 * PAIR]
+        dkv[:, D + p * PAIR : D + (p + 1) * PAIR] = back[p, :, 2 * PAIR :]
+    hidden_grad[...] = first_grad[...] + dot_nt(dq[...], wq[...])
+    stream_grad[...] = dot_nt(dkv[...], wkv[...])
+
+
+def plus(a, b):
+    return (a.astype(wide_t) + b.astype(wide_t)).astype(low_t)
+
+
+def add_two(ids, keep, received, out):
+    for k in range(4):
+        out[k] = plus(keep[k], received[k])
+
+
+def add_mixed(ids, keep, received, cross_keep, cross_received, out):
+    width = keep.shape[2]
+    for k in range(4):
+        out[k, :, :width] = plus(keep[k], received[k])
+        for g in range(4):
+            rows = slice(g * 64, (g + 1) * 64)
+            start = width + g * 2 * PAIR
+            out[k, :, start : start + 2 * PAIR] = plus(
+                cross_keep[k, rows, :], cross_received[k, rows, :]
+            )
+
+
+def add_chips(ids, parts, *outs):
+    for e in range(4):
+        here = slice(e * 16, (e + 1) * 16)
+        total = parts[0, here, :].astype(wide_t)
+        for k in range(1, 4):
+            total = total + parts[k, here, :].astype(wide_t)
+        outs[e][...] = total.astype(low_t)
+
+
+def add_four(ids, a, b, c, d, out):
+    total = a[...].astype(wide_t) + b[...].astype(wide_t) + c[...].astype(wide_t) + d[...].astype(wide_t)
+    for k in range(4):
+        out[k] = total.astype(low_t)
+
+
+def end_sums(ids, keep, received, cross_keep, cross_received, mixed, back, *outs):
+    for k in range(4):
+        back[k] = plus(keep[k], received[k])
+    width = 2 * D + 128
+    for e in range(4):
+        here = slice(e * 16, (e + 1) * 16)
+        total = mixed[0, here, :width].astype(wide_t)
+        for k in range(1, 4):
+            total = total + mixed[k, here, :width].astype(wide_t)
+        outs[e][:, :width] = total.astype(low_t)
+        start = width
+        for one, two in ((cross_keep, cross_received), (keep, received)):
+            for g in range(4):
+                rows = slice(e * 64 + g * 16, e * 64 + (g + 1) * 16)
+                outs[e][:, start : start + one.shape[2]] = plus(one[4, rows, :], two[4, rows, :])
+                start += one.shape[2]
+
+
+def place_a(ids, own, other, g_in, g_out, g_cross):
+    for n, part in enumerate((own, other)):
+        for chip in range(4):
+            c = chip * 2 + (ids[1] ^ n)
+            rows = at16(c * 16)
+            g_in[rows, :] = part[chip, :, :FF].astype(wide_t)
+            for g in range(4):
+                g_out[at16(c * 64 + g * 16), :] = part[
+                    chip, :, FF + g * D : FF + (g + 1) * D
+                ].astype(wide_t)
+            g_cross[rows, :] = part[chip, :, 2 * FF :].astype(wide_t)
+
+
+def place_end(ids, own, other, g_cross_query, g_output, norms, g_cross_pair, g_query, g_pair):
+    norms[...] = own[0, :, 2 * D : 2 * D + 128].astype(wide_t)
+    for n, part in enumerate((own, other)):
+        for chip in range(4):
+            core = ids[1] ^ n
+            rows = at16((chip * 2 + core) * 16)
+            g_cross_query[rows, :] = part[chip, :, :D].astype(wide_t)
+            g_output[rows, :] = part[chip, :, D : 2 * D].astype(wide_t)
+            start = 2 * D + 128
+            for outs in (((g_cross_pair, 0), (g_cross_pair, D)), ((g_query, 0), (g_pair, 0), (g_pair, D))):
+                for g in range(4):
+                    here = at16(core * 64 + g * 16)
+                    for out, base in outs:
+                        column = base + chip * PAIR
+                        out[here, column : column + PAIR] = part[
+                            chip, :, start : start + PAIR
+                        ].astype(wide_t)
+                        start += PAIR
+
+
+def pack_start(ids, stream, *refs):
+    weights, (gain, shift), (many, pack) = refs[:6], refs[6:8], refs[8:]
+    for k in range(4):
+        many[k] = stream[...]
+    rows = at16((ids[0] * 2 + ids[1]) * 16)
+    start = 0
+    for w in weights:
+        pack[:, start : start + w.shape[1]] = w[rows, :]
+        start += w.shape[1]
+    norms = (gain[...].astype(wide_t), shift[...].astype(wide_t), jnp.zeros((10, 128), wide_t))
+    pack[:, start:] = jnp.concatenate(norms, axis=0).astype(low_t)
+
+
+def pack_first(ids, *refs):
+    parts, outs = refs[:4], refs[4:]
+    for e in range(4):
+        start = 0
+        for out in outs:
+            piece = parts[e][:, start : start + out.shape[2]]
+            for k in range(4):
+                out[k, e * 16 : (e + 1) * 16, :] = piece
+            start += out.shape[2]
+
+
+def core_swap(value):
+    return lax.ppermute(value, "core", [(0, 1), (1, 0)])
+
+
+def chip_swaps(parts):
+    moves = [[(i, i ^ k) for i in range(4)] for k in range(4)]
+    return [parts[0]] + [lax.ppermute(parts[k], "chip", moves[k]) for k in range(1, 4)]
+
+
+def shard_swaps(parts):
+    moves = [[(i, i ^ k) for i in range(4)] for k in range(4)]
+    return [parts[0]] + [lax.ppermute(parts[k], "wa", moves[k]) for k in range(1, 4)]
+
+
+def deal(value):
+    return lax.all_to_all(value, "chip", 0, 0, tiled=True)
+
+
+def deal_both(value):
+    own = deal(value)
+    return own, core_swap(own)
+
+
+def after(value, *others):
+    return lax.optimization_barrier((value,) + others)[0]
+
+
+def fast_shards(
+    hidden,
+    stream,
+    encoder,
+    lengths,
+    order,
+    ranks,
+    thresholds,
+    self_query,
+    self_key_value,
+    self_output,
+    cross_query,
+    cross_key_value,
+    cross_output,
+    ffn_in,
+    ffn_out,
+    norm_gain,
+    norm_shift,
+    cotangent,
+):
+    rows, keys = hidden.shape[1], order.shape[1]
+    chip, core, mw = lax.axis_index("chip"), lax.axis_index("core"), lax.axis_index("wa")
+    ids = jnp.stack((chip, core, mw)).astype(jnp.int32)
+    inputs = hidden[0]
+    me = chip * 2 + core
+
+    stream_copies, pack = run(
+        pack_start,
+        [((4, rows, D), low_t), ((16, 8 * D + 128), low_t)],
+        ids,
+        [stream[0], self_query, self_key_value, self_output, cross_query, cross_key_value, cross_output]
+        + [norm_gain, norm_shift],
+    )
+    stream_own, stream_other = deal_both(stream_copies)
+    source_own = lax.all_gather(encoder[0], "chip", axis=0)
+    shards = shard_swaps([pack] * 4)
+    copies1, copies2 = run(
+        pack_first,
+        [((4, 64, 3 * D), low_t), ((4, 64, 5 * D + 128), low_t)],
+        ids,
+        [after(shards[0], stream_own)] + shards[1:],
+    )
+    slices1, slices1_other = deal_both(copies1)
+    slices2 = deal(after(copies2, slices1))
+    half_columns = [
+        lax.dynamic_slice_in_dim(ffn_in, k * 512 + core * 256, 256, 1) for k in range(4)
+    ]
+    half_rows = [lax.dynamic_slice_in_dim(ffn_out, core * 256 + n * 128, 128, 0) for n in range(2)]
+    half = jnp.concatenate(
+        (jnp.concatenate(half_columns, axis=1), jnp.concatenate(half_rows, axis=1)), axis=0
+    )
+    ffn_own = lax.all_gather(after(half, source_own), "wa", axis=0)
+    hidden_own = lax.all_gather(after(inputs, ffn_own), "chip", axis=0)
+
+    seq_ends = jnp.cumsum(lengths[0])
+    token_seq = sequence_ids(order[0], seq_ends)
+    source_seq = sequence_ids(jnp.arange(keys, dtype=jnp.int32), seq_ends)
+
+    def by_device(vector):
+        blocks = vector.reshape(4, 2, rows)
+        return jnp.concatenate(
+            [lax.dynamic_index_in_dim(blocks, core ^ n, 1, keepdims=False) for n in range(2)], axis=0
+        )
+
+    token_rows, source_blocks = by_device(token_seq), by_device(source_seq)
+    low_rows = token_rows * 1024
+    high_rows = low_rows + by_device(thresholds[0])
+    code_rows = low_rows + by_device(ranks[0])
+    code_wide = jnp.broadcast_to(code_rows.reshape(keys, 1), (keys, 128))
+    source_wide = jnp.broadcast_to(source_blocks.reshape(keys, 1), (keys, 128))
+
+    def own_column(blocks):
+        return lax.dynamic_slice_in_dim(blocks, chip, 1, 0).reshape(rows, 1)
+
+    attend_scratch = [((rows, D), low_t), ((keys, 2 * D), low_t), ((rows, keys), wide_t)]
+    self_low, wq, wkv = run(
+        self_forward,
+        [((rows, D), low_t), ((D, D), low_t), ((D, 2 * D), low_t)],
+        ids,
+        [inputs, stream_own, stream_other, slices1, slices1_other]
+        + [code_rows.reshape(1, keys), own_column(low_rows), own_column(high_rows)],
+        attend_scratch,
+        us=15,
+    )
+    slices2_other = core_swap(after(slices2, self_low))
+    source_other = core_swap(after(source_own, self_low))
+    first, normed, scale, first_low, cross_low, cross_q, wo, wcq, wckv, wco, gs = run(
+        cross_forward,
+        [((rows, D), wide_t)] * 2
+        + [((rows, 128), wide_t)]
+        + [((rows, D), low_t)] * 3
+        + [((D, D), low_t), ((D, D), low_t), ((D, 2 * D), low_t), ((D, D), low_t), ((16, D), low_t)],
+        ids,
+        [inputs, self_low, source_own, source_other, slices2, slices2_other]
+        + [source_blocks.reshape(1, keys), own_column(token_rows)],
+        attend_scratch,
+        us=15,
+    )
+    ffn_other = core_swap(after(ffn_own, cross_low))
+    (
+        result,
+        cross_dealt,
+        second_grad,
+        second_low,
+        activated,
+        pre_grad,
+        branch,
+        cross_branch,
+        sums,
+    ) = run(
+        feed_forward,
+        [
+            ((rows, D), low_t),
+            ((PAIRS, rows, 2 * PAIR), low_t),
+            ((rows, D), wide_t),
+            ((rows, D), low_t),
+            ((rows, FF), low_t),
+            ((rows, FF), low_t),
+            ((rows, D), low_t),
+            ((rows, D), low_t),
+            ((8, D), wide_t),
+        ],
+        ids,
+        [first, cross_low, cross_q, wco, gs, cotangent[0], ffn_own, ffn_other],
+        [((rows, FF), wide_t), ((2, D, FF // 2), low_t), ((2, FF // 2, D), low_t)],
+        us=8,
+    )
+    both_own, both_other = deal_both(cross_dealt)
+
+    width_a = 2 * FF + D
+    keep_a, send_a = run(
+        grads_a,
+        [((4, 64, width_a), low_t)] * 2,
+        ids,
+        [second_low, pre_grad, activated, branch, cross_low, cross_branch],
+        [((D, FF), low_t), ((FF, D), low_t), ((D, D), low_t)],
+        us=6,
+    )
+    (sum_a,) = run(add_two, [((4, 64, width_a), low_t)], ids, [keep_a, core_swap(after(send_a, both_own))])
+    rows_a = deal(after(sum_a, both_own))
+
+    def back_scratch(width):
+        return (
+            [((8, rows, PAIR), low_t)] * 2
+            + [((keys, PAIR), low_t)] * 2
+            + [((PAIR, keys), low_t), ((8, PAIR, rows), low_t), ((8, rows, PAIR), low_t)]
+            + [((keys, PAIR), wide_t)] * 2
+            + [((keys, rows), wide_t), ((D, width), low_t)]
+        )
+
+    cq_keep, cq_send, ckv_keep, ckv_send = run(
+        functools.partial(pair_back, False),
+        [((4, rows, PAIR), low_t)] * 2 + [((5, rows, 2 * PAIR), low_t)] * 2,
+        ids,
+        [after(both_own, sum_a), both_other, source_own, source_other, wckv, source_wide, token_rows],
+        back_scratch(2 * PAIR),
+        us=25,
+    )
+    (cq_sum,) = run(add_two, [((4, rows, PAIR), low_t)], ids, [cq_keep, core_swap(cq_send)])
+    cross_back = deal(after(cq_sum, rows_a))
+    shards_a = run(add_chips, [((16, width_a), low_t)] * 4, ids, [after(rows_a, cq_sum)])
+    moved_a = shard_swaps([after(part, cross_back) for part in shards_a])
+    ckv_received = core_swap(after(ckv_send, cross_back))
+    first_grad, self_branch, self_dealt, cross_dq, sums = run(
+        first_back,
+        [
+            ((rows, D), wide_t),
+            ((rows, D), low_t),
+            ((PAIRS, rows, PAIR), low_t),
+            ((rows, D), low_t),
+            ((8, D), wide_t),
+        ],
+        ids,
+        [cross_back, second_grad, normed, scale, gs, wcq, wo, sums],
+        us=3,
+    )
+    do_own, do_other = deal_both(self_dealt)
+    width_b = 2 * D + 128
+    keep_b, send_b = run(
+        grads_b,
+        [((4, 64, width_b), low_t)] * 2,
+        ids,
+        [first_low, cross_dq, self_low, self_branch, sums],
+        [((D, D), low_t)] * 2,
+        us=3,
+    )
+    width_m = width_b + 8 * PAIR
+    (sum_b,) = run(
+        add_mixed,
+        [((4, 64, width_m), low_t)],
+        ids,
+        [keep_b, core_swap(after(send_b, do_own)), ckv_keep, ckv_received],
+    )
+    mixed_b = deal(after(sum_b, do_own))
+    hidden_other = core_swap(after(hidden_own, cross_back))
+    keep_s, send_s = run(
+        functools.partial(pair_back, True),
+        [((5, rows, 3 * PAIR), low_t)] * 2,
+        ids,
+        [hidden_own, hidden_other, after(do_own, sum_b, *moved_a), do_other, stream_own, stream_other]
+        + [wq, wkv, code_wide, low_rows, high_rows],
+        back_scratch(3 * PAIR),
+        us=25,
+    )
+    keep_s_received = core_swap(send_s)
+    (copies_a,) = run(add_four, [((4, 16, width_a), low_t)], ids, [after(moved_a[0], keep_s)] + moved_a[1:])
+    a_own, a_other = deal_both(copies_a)
+    end_width = width_b + 8 * PAIR + 12 * PAIR
+    back_s, *end_parts = run(
+        end_sums,
+        [((4, rows, 3 * PAIR), low_t)] + [((16, end_width), low_t)] * 4,
+        ids,
+        [keep_s, keep_s_received, ckv_keep, ckv_received, mixed_b],
+    )
+    self_back = deal(after(back_s, a_own))
+    (copies_end,) = run(add_four, [((4, 16, end_width), low_t)], ids, shard_swaps(end_parts))
+    end_own = deal(after(copies_end, self_back))
+    (source_grad,) = run(
+        source_back,
+        [((rows, D), wide_t)],
+        ids,
+        [mixed_b, wckv],
+        [((rows, 2 * D), low_t)],
+        us=3,
+    )
+    hidden_grad, stream_grad = run(
+        hidden_back,
+        [((rows, D), wide_t)] * 2,
+        ids,
+        [self_back, first_grad, wq, wkv],
+        [((rows, D), low_t), ((rows, 2 * D), low_t)],
+        us=3,
+    )
+    grad_in, grad_out, grad_cross_output = run(
+        place_a,
+        [((128, FF), wide_t), ((D, D), wide_t), ((128, D), wide_t)],
+        ids,
+        [a_own, a_other],
+    )
+    end_other = core_swap(after(end_own, hidden_grad, source_grad, grad_in))
+    grad_cross_query, grad_output, norm_sums, grad_cross_pair, grad_query, grad_pair = run(
+        place_end,
+        [((128, D), wide_t)] * 2
+        + [((16, 128), wide_t), ((128, 2 * D), wide_t), ((128, D), wide_t), ((128, 2 * D), wide_t)],
+        ids,
+        [end_own, end_other],
+    )
+    return (
+        result[None],
+        hidden_grad[None],
+        stream_grad[None],
+        source_grad[None],
+        grad_query,
+        grad_pair,
+        grad_output,
+        grad_cross_query,
+        grad_cross_pair,
+        grad_cross_output,
+        grad_in,
+        grad_out,
+        norm_sums[0:3],
+        norm_sums[3:6],
+    )
+
+
 def solution(mesh):
     in_specs = (
         P("wa", "ctx", None),
@@ -424,4 +1232,18 @@
         P(None, "wa"),
         P(None, "wa"),
     )
-    return jax.shard_map(shards, mesh=mesh, in_specs=in_specs, out_specs=out_specs, check_vma=False)
+    if mesh.axis_names != ("ctx", "wa") or mesh.shape["ctx"] != HEADS or mesh.shape["wa"] != 4:
+        return jax.shard_map(
+            general_shards, mesh=mesh, in_specs=in_specs, out_specs=out_specs, check_vma=False
+        )
+
+    def finer(spec):
+        return P(*(("chip", "core") if axis == "ctx" else axis for axis in spec))
+
+    return jax.shard_map(
+        fast_shards,
+        mesh=Mesh(mesh.devices.reshape(4, 2, 4), ("chip", "core", "wa")),
+        in_specs=tuple(finer(spec) for spec in in_specs),
+        out_specs=tuple(finer(spec) for spec in out_specs),
+        check_vma=False,
+    )

time: 841 us -> 318 us (0.38); the launches traced: 830 us -> 317 us
  waiting for transfers between devices: 389 us -> 83.7 us
  blocking collectives: 170 us -> 0 us
  Pallas kernels: 0 us -> 140 us
  matrix products: 99.7 us -> 0 us
  local copies, waits for them, and re-layouts: 116 us -> 16.8 us
  starting transfers between devices: 0.95 us -> 58.2 us
  other arithmetic: 29.2 us -> 3.85 us
  loops' own time: 9.44 us -> 0 us
    reduce_scatter x7 -> x0, waiting for transfers between devices: 215 us -> none  [the longest x1 58 us: shards(): lax.psum_scatter(self_terms, 'ctx', scatter_dimension=0, tiled=True)]
    pallas_call x0 -> x21, Pallas kernels: none -> 140 us  [run(): pl.pallas_call(body, name=getattr(body, 'func', body).__name__, out_shape...]
    unnamed x23 -> x3, waiting for transfers between devices: 110 us -> 0.7 us
    dot_general x52 -> x0, matrix products: 99.7 us -> none  [the longest x24 46.3 us: matmul(): return jnp.dot(left, right, preferred_element_type=jnp.float32)]
    psum x1 -> x0, blocking collectives: 89.6 us -> none  [shards(): lax.psum((share_query, share_pair, share_output, share_cross_query, share...]
    all_gather x6 -> x0, blocking collectives: 80.3 us -> none  [the longest x1 16.5 us: shards(): lax.all_gather(self_output, 'wa', axis=0, tiled=True)]
    all_gather x6 -> x3, waiting for transfers between devices: 64.1 us -> 10.1 us  [the longest x1 10.1 us: fast_shards(): ffn_own = lax.all_gather(after(half, source_own), 'wa', axis=0)]
    all_to_all x0 -> x11, starting transfers between devices: none -> 42.1 us  [deal(): return lax.all_to_all(value, 'chip', 0, 0, tiled=True)]
  transfers between devices with their start and end apart: 18 -> 38, of which waited for: 14 -> 19; matrix products, arithmetic and copies ran while one was open for 21% -> 3% of each run, Pallas kernels for 0% -> 40%
where the time goes in v2:
time: 318 us; the launch traced here: 317 us
  Pallas kernels  140 us (44%)
  waiting for transfers between devices  83.7 us (26%)
  starting transfers between devices  58.2 us (18%)
  local copies, waits for them, and re-layouts  16.8 us (5%)
  between operations  14.2 us (4%)
  other arithmetic  3.85 us (1%)
    pallas_call x21, Pallas kernels, run(): pl.pallas_call(body, name=getattr(body, 'func', body).__name__, out_shape...  140 us
    all_to_all x11, starting transfers between devices, deal(): return lax.all_to_all(value, 'chip', 0, 0, tiled=True)  42.1 us
    all_to_all x11, waiting for transfers between devices, deal(): return lax.all_to_all(value, 'chip', 0, 0, tiled=True)  42 us
    ppermute x15, waiting for transfers between devices, core_swap(): return lax.ppermute(value, 'core', [(0, 1), (1, 0)])  15.7 us
    ppermute x9, waiting for transfers between devices, shard_swaps(): lax.ppermute(parts[k], 'wa', moves[k])  15.1 us
    ppermute x9, starting transfers between devices, shard_swaps(): lax.ppermute(parts[k], 'wa', moves[k])  14.2 us
    unnamed x89, local copies, waits for them, and re-layouts  10.2 us
    all_gather x1, waiting for transfers between devices, fast_shards(): ffn_own = lax.all_gather(after(half, source_own), 'wa', axis=0)  10.1 us
  transfers between devices with their start and end apart: 38, of which 19 were waited for; matrix products, arithmetic and copies ran while one was open for 3% of the time, Pallas kernels for 40%

profile of v2, /device:TPU:0, one launch (start us, length us, event | category | flops | bytes accessed | tf_op | source)
XLA Modules:
  0.0 316.9 jit_solution(14938492867837407824)
XLA Ops:
  10.2 5.3 %all-to-all-start = ((bf16[4,256,512]{2,1,0:T(8,128)(2,1)}), bf16[4,256,512]{2,1,0:T(8,128)(2,1)S(1)}, u32[]{:S(2)}, u32[]{:S(2)}) async-start(bf16[4,256,512]{2,1,0:T(8,128)(2,1)} %get-tuple-element.101), calls=%async_computation | async-start | bytes 2097152 | tf_op jit(solution)/shard_map/all_to_all | solution.py:921
  20.0 9.1 %all-to-all-done.own.refs_4_ = bf16[4,256,512]{2,1,0:T(8,128)(2,1)S(1)} async-done(((bf16[4,256,512]{2,1,0:T(8,128)(2,1)}), bf16[4,256,512]{2,1,0:T(8,128)(2,1)S(1)}, u32[]{:S(2)}, u32[]{:S(2)}) %all-to-all-start) | async-done | bytes 1048608 | tf_op jit(solution)/shard_map/all_to_all | solution.py:921
  34.1 3.9 %all-to-all-start.1 = ((bf16[4,64,1536]{2,1,0:T(8,128)(2,1)}), bf16[4,64,1536]{2,1,0:T(8,128)(2,1)S(1)}, u32[]{:S(2)}, u32[]{:S(2)}) async-start(bf16[4,64,1536]{2,1,0:T(8,128)(2,1)} %get-tuple-element.104), calls=%async_computation.1 | async-start | bytes 1572864 | tf_op jit(solution)/shard_map/all_to_all | solution.py:921
  40.3 12.3 %all-to-all-done.1.slices = bf16[4,64,1536]{2,1,0:T(8,128)(2,1)S(1)} async-done(((bf16[4,64,1536]{2,1,0:T(8,128)(2,1)}), bf16[4,64,1536]{2,1,0:T(8,128)(2,1)S(1)}, u32[]{:S(2)}, u32[]{:S(2)}) %all-to-all-start.1) | async-done | bytes 786464 | tf_op jit(solution)/shard_map/all_to_all | solution.py:921
  56.7 3.6 %all-to-all-start.2 = ((bf16[4,64,2688]{2,1,0:T(8,128)(2,1)}), bf16[4,64,2688]{2,1,0:T(8,128)(2,1)S(1)}, u32[]{:S(2)}, u32[]{:S(2)}) async-start(bf16[4,64,2688]{2,1,0:T(8,128)(2,1)} %get-tuple-element.108), calls=%async_computation.2 | async-start | bytes 2752512 | tf_op jit(solution)/shard_map/all_to_all | solution.py:921
  61.0 15.2 %self_forward.1 = (bf16[256,512]{1,0:T(8,128)(2,1)}, bf16[512,512]{1,0:T(8,128)(2,1)}, bf16[512,1024]{1,0:T(8,128)(2,1)}) custom-call(s32[3]{0:T(128)} %pad_add_fusion.2.ids, bf16[256,512]{1,0:T(8,128)(2,1)} %bitcast.59, bf16[4,256,512]{2,1,0:T(8,128)(2,1)} %copy-done.3, bf16[4,256,512]{2,1,0:T(8,128)(2,1)} %collective-permute-done.other.refs_5_, ...), custom_call_target="tpu_custom_call" | custom-call | flops 15000000512 | bytes 5777408 | tf_op jit(solution)/shard_map/self_forward/pallas_call | solution.py:407
  84.0 16.3 %cross_forward.1 = (f32[256,512]{1,0:T(8,128)}, f32[256,512]{1,0:T(8,128)}, f32[256,128]{1,0:T(8,128)}, bf16[256,512]{1,0:T(8,128)(2,1)}, bf16[256,512]{1,0:T(8,...) custom-call(s32[3]{0:T(128)} %pad_add_fusion.2.ids, ...), custom_call_target="tpu_custom_call" | custom-call | flops 15000000512 | bytes 9987072 | tf_op jit(solution)/shard_map/cross_forward/pallas_call | solution.py:407
  100.3 10.1 %all-gather.8.cloned.1.call-done = bf16[1024,1024]{1,0:T(8,128)(2,1)} async-done(((bf16[256,1024]{1,0:T(8,128)(2,1)}), bf16[1024,1024]{1,0:T(8,128)(2,1)}) %all-gather.8.cloned.1.call-update) | async-done | bytes 2097168 | tf_op jit(solution)/shard_map/all_gather | solution.py:984
  110.3 4.4 %collective-permute-done.7.refs_1_ = bf16[4,256,1024]{2,1,0:T(8,128)(2,1)S(1)} collective-permute-done((bf16[4,256,1024]{2,1,0:T(8,128)(2,1)}, bf16[4,256,1024]{2,1,0:T(8,128)(2,1)S(1)}, u32[]{:S(2)}, u32[]{:S(2)}) %collective-permute-start.7) | collective-permute-done | bytes 2097184 | tf_op jit(solution)/shard_map/ppermute | solution.py:907
  116.1 8.4 %feed_forward.1 = (bf16[256,512]{1,0:T(8,128)(2,1)}, bf16[4,256,256]{2,1,0:T(8,128)(2,1)}, f32[256,512]{1,0:T(8,128)}, bf16[256,512]{1,0:T(8,128)(2,1)}, bf16[25...) custom-call(s32[3]{0:T(128)} %pad_add_fusion.2.ids, ...), custom_call_target="tpu_custom_call" | custom-call | flops 8000000000 | bytes 10256384 | tf_op jit(solution)/shard_map/feed_forward/pallas_call | solution.py:407
  124.5 3.6 %all-to-all-start.3 = ((bf16[4,256,256]{2,1,0:T(8,128)(2,1)}), bf16[4,256,256]{2,1,0:T(8,128)(2,1)S(1)}, u32[]{:S(2)}, u32[]{:S(2)}) async-start(bf16[4,256,256]{2,1,0:T(8,128)(2,1)} %get-tuple-element.119), calls=%async_computation.3 | async-start | bytes 1048576 | tf_op jit(solution)/shard_map/all_to_all | solution.py:921
  128.2 5.7 %grads_a.1 = (bf16[4,64,4608]{2,1,0:T(8,128)(2,1)}, bf16[4,64,4608]{2,1,0:T(8,128)(2,1)}) custom-call(s32[3]{0:T(128)} %pad_add_fusion.2.ids, bf16[256,512]{1,0:T(8,128)(2,1)} %get-tuple-element.120.second_low, bf16[256,2048]{1,0:T(8,128)(2,1)} %get-tuple-element.121.pre_grad, bf16[256,2048]{1,0:T(8,128)(2,1)} %get-tuple-element.122.activated, ...), custom_call_target="tpu_custom_call" | custom-call | flops 6000000000 | bytes 7864320 | tf_op jit(solution)/shard_map/grads_a/pallas_call | solution.py:407
  137.1 5.1 %collective-permute-done.8.received = bf16[4,64,4608]{2,1,0:T(8,128)(2,1)} collective-permute-done((bf16[4,64,4608]{2,1,0:T(8,128)(2,1)}, bf16[4,64,4608]{2,1,0:T(8,128)(2,1)}, u32[]{:S(2)}, u32[]{:S(2)}) %collective-permute-start.8) | collective-permute-done | bytes 2359328 | tf_op jit(solution)/shard_map/ppermute | solution.py:907
  142.2 4.4 %add_two.2 = bf16[4,64,4608]{2,1,0:T(8,128)(2,1)} custom-call(s32[3]{0:T(128)} %pad_add_fusion.2.ids, bf16[4,64,4608]{2,1,0:T(8,128)(2,1)} %get-tuple-element.125.keep, bf16[4,64,4608]{2,1,0:T(8,128)(2,1)} %collective-permute-done.8.received), custom_call_target="tpu_custom_call" | custom-call | flops 2000000000 | bytes 7077888 | tf_op jit(solution)/shard_map/add_two/pallas_call | solution.py:407
  146.6 3.6 %all-to-all-start.4 = ((bf16[4,64,4608]{2,1,0:T(8,128)(2,1)}), bf16[4,64,4608]{2,1,0:T(8,128)(2,1)S(1)}, u32[]{:S(2)}, u32[]{:S(2)}) async-start(bf16[4,64,4608]{2,1,0:T(8,128)(2,1)} %add_two.2), calls=%async_computation.4 | async-start | bytes 4718592 | tf_op jit(solution)/shard_map/all_to_all | solution.py:921
  151.5 25.5 %pair_back.2 = (bf16[4,256,128]{2,1,0:T(8,128)(2,1)}, bf16[4,256,128]{2,1,0:T(8,128)(2,1)}, bf16[5,256,256]{2,1,0:T(8,128)(2,1)}, bf16[5,256,256]{2,1,0:T(8,128)(2,1)}) custom-call(s32[3]{0:T(128)} %pad_add_fusion.2.ids, bf16[4,256,256]{2,1,0:T(8,128)(2,1)} %copy-done.7, bf16[4,256,256]{2,1,0:T(8,128)(2,1)} %collective-permute-done.9.refs_1_, ...), custom_call_target="tpu_custom_call" | custom-call | flops 24999999488 | bytes 7086080 | tf_op jit(solution)/shard_map/pair_back/pallas_call | solution.py:407
  187.5 5.3 %all-to-all-done.5.back = bf16[4,256,128]{2,1,0:T(8,128)(2,1)S(1)} async-done(((bf16[4,256,128]{2,1,0:T(8,128)(2,1)}), bf16[4,256,128]{2,1,0:T(8,128)(2,1)S(1)}, u32[]{:S(2)}, u32[]{:S(2)}) %all-to-all-start.5) | async-done | bytes 262176 | tf_op jit(solution)/shard_map/all_to_all | solution.py:921
  217.5 5.7 %collective-permute-done.15.c = bf16[16,4608]{1,0:T(8,128)(2,1)S(1)} collective-permute-done((bf16[16,4608]{1,0:T(8,128)(2,1)}, bf16[16,4608]{1,0:T(8,128)(2,1)S(1)}, u32[]{:S(2)}, u32[]{:S(2)}) %collective-permute-start.15) | collective-permute-done | bytes 147488 | tf_op jit(solution)/shard_map/ppermute | solution.py:917
  223.2 3.7 %all-to-all-start.7 = ((bf16[4,64,2176]{2,1,0:T(8,128)(2,1)}), bf16[4,64,2176]{2,1,0:T(8,128)(2,1)S(1)}, u32[]{:S(2)}, u32[]{:S(2)}) async-start(bf16[4,64,2176]{2,1,0:T(8,128)(2,1)} %add_mixed.1), calls=%async_computation.7 | async-start | bytes 2228224 | tf_op jit(solution)/shard_map/all_to_all | solution.py:921
  228.3 27.8 %pair_back.3 = (bf16[5,256,384]{2,1,0:T(8,128)(2,1)}, bf16[5,256,384]{2,1,0:T(8,128)(2,1)}) custom-call(s32[3]{0:T(128)} %pad_add_fusion.2.ids, bf16[4,256,512]{2,1,0:T(8,128)(2,1)} %bitcast.81, bf16[4,256,512]{2,1,0:T(8,128)(2,1)} %collective-permute-done.11.refs_1_, bf16[4,256,128]{2,1,0:T(8,128)(2,1)} %copy-done.9, bf16[4,256,128]{2,1,0:T(8,128)(2,1)} %copy-done.25, ...), custom_call_target="tpu_custom_call" | custom-call | flops 24999999488 | bytes 9322496 | tf_op jit(solution)/shard_map/pair_back/pallas_call | solution.py:407
  258.2 4.0 %all-to-all-start.8 = ((bf16[4,16,4608]{2,1,0:T(8,128)(2,1)}), bf16[4,16,4608]{2,1,0:T(8,128)(2,1)S(1)}, u32[]{:S(2)}, u32[]{:S(2)}) async-start(bf16[4,16,4608]{2,1,0:T(8,128)(2,1)} %add_four.2), calls=%async_computation.8 | async-start | bytes 1179648 | tf_op jit(solution)/shard_map/all_to_all | solution.py:921
  266.6 5.0 %all-to-all-done.8.own = bf16[4,16,4608]{2,1,0:T(8,128)(2,1)S(1)} async-done(((bf16[4,16,4608]{2,1,0:T(8,128)(2,1)}), bf16[4,16,4608]{2,1,0:T(8,128)(2,1)S(1)}, u32[]{:S(2)}, u32[]{:S(2)}) %all-to-all-start.8) | async-done | bytes 589856 | tf_op jit(solution)/shard_map/all_to_all | solution.py:921
  283.9 6.5 %collective-permute-done.20.c = bf16[16,3712]{1,0:T(8,128)(2,1)S(1)} collective-permute-done((bf16[16,3712]{1,0:T(8,128)(2,1)}, bf16[16,3712]{1,0:T(8,128)(2,1)S(1)}, u32[]{:S(2)}, u32[]{:S(2)}) %collective-permute-start.20) | collective-permute-done | bytes 118816 | tf_op jit(solution)/shard_map/ppermute | solution.py:917
  293.0 4.0 %all-to-all-start.10 = ((bf16[4,16,3712]{2,1,0:T(8,128)(2,1)}), bf16[4,16,3712]{2,1,0:T(8,128)(2,1)S(1)}, u32[]{:S(2)}, u32[]{:S(2)}) async-start(bf16[4,16,3712]{2,1,0:T(8,128)(2,1)} %add_four.3), calls=%async_computation.10 | async-start | bytes 950272 | tf_op jit(solution)/shard_map/all_to_all | solution.py:921
  (190 shorter events, 104.3 us)
Async XLA Ops:
  10.2 18.9 %all-to-all-start = ((bf16[4,256,512]{2,1,0:T(8,128)(2,1)}), bf16[4,256,512]{2,1,0:T(8,128)(2,1)S(1)}, u32[]{:S(2)}, u32[]{:S(2)}) async-start(bf16[4,256,512]{2,1,0:T(8,128)(2,1)} %get-tuple-element.101), calls=%async_computation | async-start | bytes 2097152 | tf_op jit(solution)/shard_map/all_to_all | solution.py:921
  15.5 44.9 %all-gather.6.cloned.1.call-start = ((), (), s32[]{:S(2)}) async-start(), calls=%async_computation.11 | async-start | bytes 1310720 | tf_op jit(solution)/shard_map/all_gather | solution.py:967
  15.5 13.6 %collective-permute-start.1 = (bf16[16,4224]{1,0:T(8,128)(2,1)S(1)}, bf16[16,4224]{1,0:T(8,128)(2,1)S(1)}, u32[]{:S(2)}, u32[]{:S(2)}) collective-permute-start(bf16[16,4224]{1,0:T(8,128)(2,1)S(1)} %copy-done.30), channel_id=1, source_target_pairs={{0,1},{1,0},{2,3},{3,2},{4,5},{5,4},{6,7},{7,6},{8,9},{9,8},{10,11... | collective-permute-start | bytes 405512 | tf_op jit(solution)/shard_map/ppermute | solution.py:917
  17.1 13.1 %collective-permute-start.2 = (bf16[16,4224]{1,0:T(8,128)(2,1)S(1)}, bf16[16,4224]{1,0:T(8,128)(2,1)S(1)}, u32[]{:S(2)}, u32[]{:S(2)}) collective-permute-start(bf16[16,4224]{1,0:T(8,128)(2,1)S(1)} %copy-done.30), channel_id=1, source_target_pairs={{0,2},{1,3},{2,0},{3,1},{4,6},{5,7},{6,4},{7,5},{8,10},{9,11},{10,... | collective-permute-start | bytes 405512 | tf_op jit(solution)/shard_map/ppermute | solution.py:917
  19.7 10.5 %collective-permute-start.3 = (bf16[16,4224]{1,0:T(8,128)(2,1)S(1)}, bf16[16,4224]{1,0:T(8,128)(2,1)S(1)}, u32[]{:S(2)}, u32[]{:S(2)}) collective-permute-start(bf16[16,4224]{1,0:T(8,128)(2,1)S(1)} %copy-done.30), channel_id=1, source_target_pairs={{0,3},{1,2},{2,1},{3,0},{4,7},{5,6},{6,5},{7,4},{8,11},{9,10},{10,... | collective-permute-start | bytes 405512 | tf_op jit(solution)/shard_map/ppermute | solution.py:917
  34.1 18.6 %all-to-all-start.1 = ((bf16[4,64,1536]{2,1,0:T(8,128)(2,1)}), bf16[4,64,1536]{2,1,0:T(8,128)(2,1)S(1)}, u32[]{:S(2)}, u32[]{:S(2)}) async-start(bf16[4,64,1536]{2,1,0:T(8,128)(2,1)} %get-tuple-element.104), calls=%async_computation.1 | async-start | bytes 1572864 | tf_op jit(solution)/shard_map/all_to_all | solution.py:921
  38.0 23.0 %collective-permute-start = (bf16[4,256,512]{2,1,0:T(8,128)(2,1)S(1)}, bf16[4,256,512]{2,1,0:T(8,128)(2,1)}, u32[]{:S(2)}, u32[]{:S(2)}) collective-permute-start(bf16[4,256,512]{2,1,0:T(8,128)(2,1)S(1)} %all-to-all-done.own.refs_4_), channel_id=1, source_target_pairs={{0,4},{4,0},{1,5},{5,1},{2,6},{6,2},{3,7},{7,3},{8,12},{12,8},{9,1... | collective-permute-start | bytes 3145736 | tf_op jit(solution)/shard_map/ppermute | solution.py:907
  56.7 21.5 %all-to-all-start.2 = ((bf16[4,64,2688]{2,1,0:T(8,128)(2,1)}), bf16[4,64,2688]{2,1,0:T(8,128)(2,1)S(1)}, u32[]{:S(2)}, u32[]{:S(2)}) async-start(bf16[4,64,2688]{2,1,0:T(8,128)(2,1)} %get-tuple-element.108), calls=%async_computation.2 | async-start | bytes 2752512 | tf_op jit(solution)/shard_map/all_to_all | solution.py:921
  60.2 50.1 %all-gather.8.cloned.1.call-start = ((), (), s32[]{:S(2)}) async-start(), calls=%async_computation.12 | async-start | bytes 2621440 | tf_op jit(solution)/shard_map/all_gather | solution.py:984
  124.5 12.0 %all-to-all-start.3 = ((bf16[4,256,256]{2,1,0:T(8,128)(2,1)}), bf16[4,256,256]{2,1,0:T(8,128)(2,1)S(1)}, u32[]{:S(2)}, u32[]{:S(2)}) async-start(bf16[4,256,256]{2,1,0:T(8,128)(2,1)} %get-tuple-element.119), calls=%async_computation.3 | async-start | bytes 1048576 | tf_op jit(solution)/shard_map/all_to_all | solution.py:921
  128.1 59.4 %all-gather.10.cloned.1.call-start = ((), (), s32[]{:S(2)}) async-start(), calls=%async_computation.13 | async-start | bytes 1310720 | tf_op jit(solution)/shard_map/all_gather | solution.py:985
  136.5 13.7 %collective-permute-start.9 = (bf16[4,256,256]{2,1,0:T(8,128)(2,1)S(1)}, bf16[4,256,256]{2,1,0:T(8,128)(2,1)}, u32[]{:S(2)}, u32[]{:S(2)}) collective-permute-start(bf16[4,256,256]{2,1,0:T(8,128)(2,1)S(1)} %all-to-all-done.3.refs_0_), channel_id=1, source_target_pairs={{0,4},{4,0},{1,5},{5,1},{2,6},{6,2},{3,7},{7,3},{8,12},{12,8},{9,1... | collective-permute-start | bytes 1572872 | tf_op jit(solution)/shard_map/ppermute | solution.py:907
  146.6 37.5 %all-to-all-start.4 = ((bf16[4,64,4608]{2,1,0:T(8,128)(2,1)}), bf16[4,64,4608]{2,1,0:T(8,128)(2,1)S(1)}, u32[]{:S(2)}, u32[]{:S(2)}) async-start(bf16[4,64,4608]{2,1,0:T(8,128)(2,1)} %add_two.2), calls=%async_computation.4 | async-start | bytes 4718592 | tf_op jit(solution)/shard_map/all_to_all | solution.py:921
  192.8 34.2 %collective-permute-start.11 = (bf16[4,256,512]{2,1,0:T(8,128)(2,1)}, bf16[4,256,512]{2,1,0:T(8,128)(2,1)}, u32[]{:S(2)}, u32[]{:S(2)}) collective-permute-start(bf16[4,256,512]{2,1,0:T(8,128)(2,1)} %bitcast.80), channel_id=1, source_target_pairs={{0,4},{4,0},{1,5},{5,1},{2,6},{6,2},{3,7},{7,3},{8,12},{12,8},{9,1... | collective-permute-start | bytes 3145736 | tf_op jit(solution)/shard_map/ppermute | solution.py:907
  205.8 21.2 %collective-permute-start.17 = (bf16[4,256,128]{2,1,0:T(8,128)(2,1)S(1)}, bf16[4,256,128]{2,1,0:T(8,128)(2,1)S(1)}, u32[]{:S(2)}, u32[]{:S(2)}) collective-permute-start(bf16[4,256,128]{2,1,0:T(8,128)(2,1)S(1)} %all-to-all-done.6.refs_2_), channel_id=1, source_target_pairs={{0,4},{4,0},{1,5},{5,1},{2,6},{6,2},{3,7},{7,3},{8,12},{12,8},{9,1... | collective-permute-start | bytes 786440 | tf_op jit(solution)/shard_map/ppermute | solution.py:907
  209.0 14.2 %collective-permute-start.15 = (bf16[16,4608]{1,0:T(8,128)(2,1)}, bf16[16,4608]{1,0:T(8,128)(2,1)S(1)}, u32[]{:S(2)}, u32[]{:S(2)}) collective-permute-start(bf16[16,4608]{1,0:T(8,128)(2,1)} %get-tuple-element.158), channel_id=1, source_target_pairs={{0,2},{1,3},{2,0},{3,1},{4,6},{5,7},{6,4},{7,5},{8,10},{9,11},{10,... | collective-permute-start | bytes 442376 | tf_op jit(solution)/shard_map/ppermute | solution.py:917
  210.6 12.6 %collective-permute-start.16 = (bf16[16,4608]{1,0:T(8,128)(2,1)}, bf16[16,4608]{1,0:T(8,128)(2,1)S(1)}, u32[]{:S(2)}, u32[]{:S(2)}) collective-permute-start(bf16[16,4608]{1,0:T(8,128)(2,1)} %get-tuple-element.160), channel_id=1, source_target_pairs={{0,3},{1,2},{2,1},{3,0},{4,7},{5,6},{6,5},{7,4},{8,11},{9,10},{10,... | collective-permute-start | bytes 442376 | tf_op jit(solution)/shard_map/ppermute | solution.py:917
  223.2 35.0 %all-to-all-start.7 = ((bf16[4,64,2176]{2,1,0:T(8,128)(2,1)}), bf16[4,64,2176]{2,1,0:T(8,128)(2,1)S(1)}, u32[]{:S(2)}, u32[]{:S(2)}) async-start(bf16[4,64,2176]{2,1,0:T(8,128)(2,1)} %add_mixed.1), calls=%async_computation.7 | async-start | bytes 2228224 | tf_op jit(solution)/shard_map/all_to_all | solution.py:921
  258.2 13.4 %all-to-all-start.8 = ((bf16[4,16,4608]{2,1,0:T(8,128)(2,1)}), bf16[4,16,4608]{2,1,0:T(8,128)(2,1)S(1)}, u32[]{:S(2)}, u32[]{:S(2)}) async-start(bf16[4,16,4608]{2,1,0:T(8,128)(2,1)} %add_four.2), calls=%async_computation.8 | async-start | bytes 1179648 | tf_op jit(solution)/shard_map/all_to_all | solution.py:921
  271.6 21.4 %all-to-all-start.9 = ((bf16[4,256,384]{2,1,0:T(8,128)(2,1)}), bf16[4,256,384]{2,1,0:T(8,128)(2,1)S(1)}, u32[]{:S(2)}, u32[]{:S(2)}) async-start(bf16[4,256,384]{2,1,0:T(8,128)(2,1)} %get-tuple-element.169), calls=%async_computation.9 | async-start | bytes 1572864 | tf_op jit(solution)/shard_map/all_to_all | solution.py:921
  275.1 21.9 %collective-permute-start.22 = (bf16[4,16,4608]{2,1,0:T(8,128)(2,1)S(1)}, bf16[4,16,4608]{2,1,0:T(8,128)(2,1)S(1)}, u32[]{:S(2)}, u32[]{:S(2)}) collective-permute-start(bf16[4,16,4608]{2,1,0:T(8,128)(2,1)S(1)} %all-to-all-done.8.own), channel_id=1, source_target_pairs={{0,4},{4,0},{1,5},{5,1},{2,6},{6,2},{3,7},{7,3},{8,12},{12,8},{9,1... | collective-permute-start | bytes 1769480 | tf_op jit(solution)/shard_map/ppermute | solution.py:907
  278.1 12.3 %collective-permute-start.20 = (bf16[16,3712]{1,0:T(8,128)(2,1)}, bf16[16,3712]{1,0:T(8,128)(2,1)S(1)}, u32[]{:S(2)}, u32[]{:S(2)}) collective-permute-start(bf16[16,3712]{1,0:T(8,128)(2,1)} %get-tuple-element.175), channel_id=1, source_target_pairs={{0,2},{1,3},{2,0},{3,1},{4,6},{5,7},{6,4},{7,5},{8,10},{9,11},{10,... | collective-permute-start | bytes 356360 | tf_op jit(solution)/shard_map/ppermute | solution.py:917
  278.9 11.5 %collective-permute-start.21 = (bf16[16,3712]{1,0:T(8,128)(2,1)}, bf16[16,3712]{1,0:T(8,128)(2,1)S(1)}, u32[]{:S(2)}, u32[]{:S(2)}) collective-permute-start(bf16[16,3712]{1,0:T(8,128)(2,1)} %get-tuple-element.176), channel_id=1, source_target_pairs={{0,3},{1,2},{2,1},{3,0},{4,7},{5,6},{6,5},{7,4},{8,11},{9,10},{10,... | collective-permute-start | bytes 356360 | tf_op jit(solution)/shard_map/ppermute | solution.py:917
  293.0 10.8 %all-to-all-start.10 = ((bf16[4,16,3712]{2,1,0:T(8,128)(2,1)}), bf16[4,16,3712]{2,1,0:T(8,128)(2,1)S(1)}, u32[]{:S(2)}, u32[]{:S(2)}) async-start(bf16[4,16,3712]{2,1,0:T(8,128)(2,1)} %add_four.3), calls=%async_computation.10 | async-start | bytes 950272 | tf_op jit(solution)/shard_map/all_to_all | solution.py:921
  (52 other events, 416.0 us)
Sparse Core Ops, SparseCore 0:
  20.1 32.8 all-gather.5
  62.7 47.6 all-gather.7
  137.2 41.0 all-gather.9

commit v3 on v0

--- a/solution.py
+++ b/solution.py
@@ -1,6 +1,11 @@
+import functools
+
 import jax
 import jax.numpy as jnp
 from jax import lax
+from jax.experimental import pallas as pl
+from jax.experimental.pallas import tpu as pltpu
+from jax.sharding import Mesh
 from jax.sharding import PartitionSpec as P
 
 D = 512
@@ -154,7 +159,7 @@
     return jnp.dot(left, right, preferred_element_type=jnp.float32)
 
 
-def shards(
+def general_shards(
     hidden,
     stream,
     encoder,
@@ -387,6 +392,992 @@
     )
 
 
+PAIR = 2 * HEAD
+PAIRS = HEADS // 2
+FF = 2048
+low_t = jnp.bfloat16
+wide_t = jnp.float32
+vmem_spec = pl.BlockSpec(memory_space=pltpu.VMEM)
+smem_spec = pl.BlockSpec(memory_space=pltpu.SMEM)
+
+
+def run(body, outs, ids, args, scratch=(), us=2, vmem=56):
+    outs = [jax.ShapeDtypeStruct(shape, kind) for shape, kind in outs]
+    arrays = [arg[0] if isinstance(arg, tuple) else arg for arg in args]
+
+    def view(arg, ref):
+        if not isinstance(arg, tuple):
+            return ref
+        if len(arg) == 3:
+            return ref.at[arg[2]]
+        return ref.at[:, :, arg[1] * D : (arg[1] + 1) * D]
+
+    def kernel(ids, *refs):
+        views = [view(arg, ref) for arg, ref in zip(args, refs)]
+        body(ids, *views, *refs[len(args) :])
+
+    moved = sum(a.size * a.dtype.itemsize for a in arrays + outs)
+    return pl.pallas_call(
+        kernel,
+        name=getattr(body, "func", body).__name__,
+        out_shape=outs,
+        in_specs=[smem_spec] + [vmem_spec] * len(args),
+        out_specs=[vmem_spec] * len(outs),
+        scratch_shapes=[pltpu.VMEM(shape, kind) for shape, kind in scratch],
+        compiler_params=pltpu.CompilerParams(vmem_limit_bytes=vmem * 1024 * 1024),
+        cost_estimate=pl.CostEstimate(flops=us * 1_000_000_000, bytes_accessed=moved, transcendentals=0),
+    )(ids, *arrays)
+
+
+def dot_nn(a, b):
+    return lax.dot_general(a, b, (((1,), (0,)), ((), ())), preferred_element_type=wide_t)
+
+
+def dot_nt(a, b):
+    return lax.dot_general(a, b, (((1,), (1,)), ((), ())), preferred_element_type=wide_t)
+
+
+def dot_tn(a, b):
+    return lax.dot_general(a, b, (((0,), (0,)), ((), ())), preferred_element_type=wide_t)
+
+
+def at16(start, size=16):
+    return pl.ds(pl.multiple_of(start, 16), size)
+
+
+def at128(start, size=128):
+    return pl.ds(pl.multiple_of(start, 128), size)
+
+
+def half_mask(shape, axis, core):
+    return (lax.broadcasted_iota(jnp.int32, shape, axis) // HEAD) == core
+
+
+def attend_rows(q_ref, k_ref, vt_ref, bias_ref, s_ref, ot_ref, lse_ref):
+    keys, rows = bias_ref.shape
+    tile = min(1024, keys)
+    tiles = keys // tile
+
+    def step(p, carry):
+        q = q_ref[:, at128(p * PAIR)]
+        for h in range(2):
+            mine = half_mask((rows, PAIR), 1, h)
+            own_q = jnp.where(mine, q, jnp.zeros_like(q))
+            top = jnp.full((8, rows), neg_fill, wide_t)
+            for t in range(tiles):
+                here = slice(t * tile, (t + 1) * tile)
+                s = dot_nt(k_ref[here, at128(p * PAIR)], own_q) + bias_ref[here, :]
+                s_ref[h, here, :] = s
+                top = jnp.maximum(top, jnp.max(s.reshape(tile // 8, 8, rows), axis=0))
+            top = jnp.max(top, axis=0, keepdims=True)
+            total = jnp.zeros((8, rows), wide_t)
+            mixed = jnp.zeros((HEAD, rows), wide_t)
+            features = pl.ds(pl.multiple_of(p * PAIR + h * HEAD, HEAD), HEAD)
+            for t in range(tiles):
+                here = slice(t * tile, (t + 1) * tile)
+                w = jnp.exp(s_ref[h, here, :] - top)
+                total = total + jnp.sum(w.reshape(tile // 8, 8, rows), axis=0)
+                mixed = mixed + dot_nn(vt_ref[features, here], w.astype(low_t))
+            total = jnp.sum(total, axis=0, keepdims=True)
+            ot_ref[features, :] = mixed / total
+            lse_ref[pl.ds(p * 2 + h, 1), :] = top + jnp.log(total)
+        return carry
+
+    lax.fori_loop(0, PAIRS, step, 0)
+
+
+def finish_rows(ot_ref, low_out, mixed_out):
+    mixed = ot_ref[...].T
+    low_out[...] = mixed.astype(low_t)
+    mixed_out[...] = mixed
+
+
+def three_parts(value):
+    high = value.astype(low_t).astype(wide_t)
+    rest = value - high
+    middle = rest.astype(low_t).astype(wide_t)
+    return high, middle, rest - middle
+
+
+def side_rows(lse, grad_low, mixed, row_data):
+    product = grad_low.astype(wide_t) * mixed[...]
+    lane = lax.broadcasted_iota(jnp.int32, (grad_low.shape[0], PAIR), 1)
+    sums = jnp.zeros((grad_low.shape[0], PAIR), wide_t)
+    for p in range(PAIRS):
+        piece = product[:, p * PAIR : (p + 1) * PAIR]
+        for h in range(2):
+            mine = half_mask(piece.shape, 1, h)
+            offset = jnp.sum(jnp.where(mine, piece, 0.0), axis=1, keepdims=True)
+            sums = jnp.where(lane == p * 2 + h, offset, sums)
+    offsets = sums.T
+    seq = row_data[16:17, :]
+    onehot = [(seq == float(n)).astype(wide_t) for n in range(4)]
+    sides = []
+    for p in range(PAIRS):
+        pieces = []
+        for h in range(2):
+            head = p * 2 + h
+            pieces += three_parts(-lse[head : head + 1, :])
+            pieces += three_parts(-offsets[head : head + 1, :])
+        sides.append(jnp.concatenate(pieces + onehot, axis=0).astype(low_t))
+    return sides
+
+
+def side_lanes(side, core):
+    side = side.astype(wide_t)
+    head = jnp.where(core == 0, side[0:6], side[6:12])
+    gap = jnp.zeros((5, side.shape[1]), wide_t)
+    rest = jnp.zeros((HEAD - 20, side.shape[1]), wide_t)
+    half = jnp.concatenate((head[0:3], gap, head[3:6], gap, side[12:16], rest), axis=0)
+    return jnp.concatenate((half, half), axis=0).T.astype(low_t)
+
+
+def assemble(ids, parts, column, outs):
+    for chip, other, block in parts:
+        own = chip * 2 + (ids[1] ^ other)
+        for e in range(4):
+            rows = at16((ids[2] ^ e) * 128 + own * 16)
+            start = column
+            for out in outs:
+                width = out.shape[1]
+                out[rows, :] = block[e * 16 : (e + 1) * 16, start : start + width]
+                start += width
+
+
+def project_pairs(parts, w_pair, k_ref, vt_ref, wvt_ref):
+    wvt_ref[...] = w_pair[:, D:].astype(wide_t).T.astype(low_t)
+    for n, part in enumerate(parts):
+        for k in range(PAIRS):
+            rows = part.shape[1]
+            start = (n * 4 + k) * rows
+            k_ref[start : start + rows, :] = dot_nn(part[k], w_pair[:, :D]).astype(low_t)
+            vt_ref[:, start : start + rows] = dot_nt(wvt_ref[...], part[k]).astype(low_t)
+
+
+def self_forward(ids, hidden, own, other, *refs):
+    slices, (cols, row_data), refs = refs[:8], refs[8:10], refs[10:]
+    out, mixed, lse, wq, wkv, q_ref, k_ref, vt_ref, wvt_ref, bias_ref, s_ref, ot_ref = refs
+    rows = hidden.shape[0]
+    parts = [(ids[0] ^ k, n, slices[n * 4 + k]) for n in range(2) for k in range(4)]
+    assemble(ids, parts, 0, (wq, wkv))
+    q_ref[...] = (dot_nn(hidden[...], wq[...]).astype(low_t) * 0.125).astype(low_t)
+    project_pairs((own, other), wkv, k_ref, vt_ref, wvt_ref)
+    seq, limit = row_data[16:17, :], row_data[17:18, :]
+    for b in range(8):
+        seen = (cols[:, b : b + 1] == seq) & (cols[:, 8 + b : 9 + b] < limit)
+        bias_ref[b * rows : (b + 1) * rows, :] = jnp.where(seen, 0.0, neg_fill)
+    mine = lax.broadcasted_iota(jnp.int32, (rows, rows), 0) == lax.broadcasted_iota(
+        jnp.int32, (rows, rows), 1
+    )
+    block = at128(ids[0] * rows, rows)
+    bias_ref[block, :] = jnp.where(mine, 0.0, bias_ref[block, :])
+    attend_rows(q_ref, k_ref, vt_ref, bias_ref, s_ref, ot_ref, lse)
+    finish_rows(ot_ref, out, mixed)
+
+
+def layer_norm(values, gain_row, shift_row):
+    mean = jnp.mean(values, axis=1, keepdims=True)
+    centred = values - mean
+    scale = lax.rsqrt(jnp.mean(centred * centred, axis=1, keepdims=True) + layer_eps)
+    normed = centred * scale
+    return normed * gain_row + shift_row, normed, scale
+
+
+def layer_norm_back(grad, normed, scale, gain_row):
+    gain_term = jnp.sum(grad * normed, axis=0, keepdims=True)
+    shift_term = jnp.sum(grad, axis=0, keepdims=True)
+    scaled = grad * gain_row
+    grad_in = scale * (
+        scaled
+        - jnp.mean(scaled, axis=1, keepdims=True)
+        - normed * jnp.mean(scaled * normed, axis=1, keepdims=True)
+    )
+    return grad_in, gain_term, shift_term
+
+
+def cross_forward(ids, hidden, self_low, own, other, *refs):
+    slices, (cols, row_data) = refs[:2], refs[2:4]
+    first, normed, scale_out, first_low, cross_low, mixed, lse, cross_q = refs[4:12]
+    wo, wcq, wckv, wco, gs, q_ref, k_ref, vt_ref, wvt_ref, bias_ref, s_ref, ot_ref = refs[12:]
+    for n in range(2):
+        for e in range(4):
+            rows = at16(e * 128 + (ids[1] ^ n) * 64, 64)
+            start = 0
+            for out in (wo, wcq, wckv, wco):
+                width = out.shape[1]
+                out[rows, :] = slices[n][e, :, start : start + width]
+                start += width
+    for e in range(4):
+        gs[:, e * 128 : (e + 1) * 128] = slices[0][e, :16, 5 * D :]
+    gain, shift = gs[0:1, :].astype(wide_t), gs[3:4, :].astype(wide_t)
+    value, n0, s0 = layer_norm(
+        hidden[...].astype(wide_t) + dot_nn(self_low[...], wo[...]), gain, shift
+    )
+    first[...] = value
+    normed[...] = n0
+    scale_out[...] = jnp.broadcast_to(s0, scale_out.shape)
+    low = value.astype(low_t)
+    first_low[...] = low
+    q = dot_nn(low, wcq[...]).astype(low_t)
+    cross_q[...] = q
+    q_ref[...] = (q * 0.125).astype(low_t)
+    rows = hidden.shape[0]
+    project_pairs((own, other), wckv, k_ref, vt_ref, wvt_ref)
+    for b in range(8):
+        seen = cols[:, 16 + b : 17 + b] == row_data[16:17, :]
+        bias_ref[b * rows : (b + 1) * rows, :] = jnp.where(seen, 0.0, neg_fill)
+    attend_rows(q_ref, k_ref, vt_ref, bias_ref, s_ref, ot_ref, lse)
+    finish_rows(ot_ref, cross_low, mixed)
+
+
+def feed_forward(ids, first, cross_low, cross_mixed, lse, row_data, cross_q, wco, gs, cotangent, *refs):
+    slices = refs[0:2]
+    result, dealt, second_grad, keep, send, sums, slope, wins, wouts = refs[2:]
+    half_ff = FF // 2
+    for n, part in enumerate(slices):
+        core = ids[1] ^ n
+        for chip in range(4):
+            for e in range(4):
+                w, here = ids[2] ^ e, slice(e * 16, (e + 1) * 16)
+                rows = at16(w * 128 + (chip * 2 + core) * 16)
+                for g in range(4):
+                    row = w * 256 + ((chip % 2) * 2 + core) * 64 + g * 16
+                    wouts[(chip // 2) ^ ids[1], at16(row), :] = part[
+                        chip, here, FF + g * D : FF + (g + 1) * D
+                    ]
+                    for h in range(2):
+                        column = g * 512 + h * 256
+                        wins[h ^ ids[1], rows, g * 256 : (g + 1) * 256] = part[
+                            chip, here, column : column + 256
+                        ]
+    gains, shifts = gs[0:3, :].astype(wide_t), gs[3:6, :].astype(wide_t)
+    second, n1, s1 = layer_norm(
+        first[...] + dot_nn(cross_low[...], wco[...]), gains[1:2], shifts[1:2]
+    )
+    low = second.astype(low_t)
+    for out in (keep, send):
+        out[:, 2 * half_ff : 2 * half_ff + D] = low
+        out[:, 2 * half_ff + 2 * D : 2 * half_ff + 3 * D] = cross_low[...]
+    width = 512
+    chunks = [(n, c) for n in range(2) for c in range(FF // 2 // width)]
+    total = second
+    for n, c in chunks:
+        here = slice(c * width, (c + 1) * width)
+        wide = slice(n * half_ff + c * width, n * half_ff + (c + 1) * width)
+        pre = dot_nn(low, wins[n, :, here])
+        sig = 1.0 / (1.0 + jnp.exp(-pre))
+        act = (pre * sig).astype(low_t)
+        (keep, send)[n][:, half_ff + c * width : half_ff + (c + 1) * width] = act
+        slope[:, wide] = sig * (1.0 + pre * (1.0 - sig))
+        total = total + dot_nn(act, wouts[n, here, :])
+    value, n2, s2 = layer_norm(total, gains[2:3], shifts[2:3])
+    result[...] = value.astype(low_t)
+    third, gain_c, shift_c = layer_norm_back(cotangent[...].astype(wide_t), n2, s2, gains[2:3])
+    third_low = third.astype(low_t)
+    for out in (keep, send):
+        out[:, 2 * half_ff + D : 2 * half_ff + 2 * D] = third_low
+    total = third
+    for n, c in chunks:
+        here = slice(c * width, (c + 1) * width)
+        wide = slice(n * half_ff + c * width, n * half_ff + (c + 1) * width)
+        back = (dot_nt(third_low, wouts[n, here, :]) * slope[:, wide]).astype(low_t)
+        (keep, send)[n][:, here] = back
+        total = total + dot_nt(back, wins[n, :, here])
+    grad, gain_b, shift_b = layer_norm_back(total, n1, s1, gains[1:2])
+    second_grad[...] = grad
+    grad_low = grad.astype(low_t)
+    for out, core in ((keep, ids[1]), (send, 1 - ids[1])):
+        half = grad_low[:, : D // 2]
+        out[:, 2 * half_ff + 3 * D :] = jnp.where(core == 0, half, grad_low[:, D // 2 :])
+    mixed = dot_nt(grad_low, wco[...]).astype(low_t)
+    rows = grad_low.shape[0]
+    sides = side_rows(lse, mixed, cross_mixed, row_data)
+    for p in range(PAIRS):
+        dealt[p, :rows, :PAIR] = cross_q[:, p * PAIR : (p + 1) * PAIR]
+        dealt[p, :rows, PAIR:] = mixed[:, p * PAIR : (p + 1) * PAIR]
+        dealt[p, rows:, :] = sides[p]
+    zero = jnp.zeros_like(gain_b)
+    sums[...] = jnp.concatenate((zero, gain_b, gain_c, zero, shift_b, shift_c, zero, zero), axis=0)
+
+
+def grads_a(ids, keep, received, out, g_in, g_out, g_cross):
+    half = FF // 2
+
+    def both(left, right):
+        return (dot_tn(keep[:, left], keep[:, right]) + dot_tn(received[:, left], received[:, right])).astype(low_t)
+
+    at = [0, half] + [2 * half + n * D for n in range(4)]
+    pre, act = slice(at[0], at[1]), slice(at[1], at[2])
+    second, branch, low = (slice(at[n], at[n] + D) for n in (2, 3, 4))
+    g_in[...] = both(second, pre)
+    g_out[...] = both(act, branch)
+    g_cross[...] = both(low, slice(at[5], at[5] + D // 2))
+    for chip in range(4):
+        for e in range(4):
+            w, here = ids[2] ^ e, slice(e * 32, (e + 1) * 32)
+            rows = at16(w * 128 + chip * 32, 32)
+            out[chip, here, :half] = g_in[rows, :]
+            for g in range(2):
+                out[chip, here, half + g * D : half + (g + 1) * D] = g_out[
+                    at16(w * 256 + chip * 64 + g * 32, 32), :
+                ]
+            out[chip, here, half + 2 * D :] = g_cross[rows, :]
+
+
+def grads_b(ids, first_low, cross_dq, self_low, branch, sums, dkv, out, g_query, g_output):
+    g_query[...] = dot_tn(first_low[...], cross_dq[...]).astype(low_t)
+    g_output[...] = dot_tn(self_low[...], branch[...]).astype(low_t)
+    row = jnp.concatenate((sums[...], jnp.zeros_like(sums[...])), axis=0).astype(low_t)
+    rows = dkv.shape[2]
+    for e in range(4):
+        w, here = ids[2] ^ e, slice(e * 16, (e + 1) * 16)
+        piece = row[:, :128]
+        for k in range(1, 4):
+            piece = jnp.where(w == k, row[:, k * 128 : (k + 1) * 128], piece)
+        for device in range(8):
+            own = at16(w * 128 + device * 16)
+            out[device, here, :D] = g_query[own, :]
+            out[device, here, D : 2 * D] = g_output[own, :]
+            out[device, here, 2 * D : 2 * D + 128] = piece
+    for device in range(8):
+        for n in range(2):
+            start = 2 * D + 128 + n * rows
+            out[device, :, start : start + rows] = dkv[device, n * HEAD : (n + 1) * HEAD, :]
+
+
+def pair_setup(is_self, ids, own, other, w_pair, cols, *refs):
+    if is_self:
+        hidden_own, hidden_other, w_query, q_all, k_all, v_all, kt, turn = refs
+    else:
+        k_all, v_all, kt, turn = refs
+    chip, core = ids[0], ids[1]
+    rows = own.shape[1]
+    mine = half_mask((rows, PAIR), 1, core)
+    features = pl.ds(pl.multiple_of(core * HEAD, HEAD), HEAD)
+    lane = lax.broadcasted_iota(jnp.int32, (rows, PAIR), 1) % HEAD
+    ones_v = jnp.where((lane >= 8) & (lane < 11), 1.0, 0.0).astype(low_t)
+    pair = at128(chip * PAIR)
+    wk, wv = w_pair[:, pair], w_pair[:, at128(D + chip * PAIR)]
+    if is_self:
+        wq = w_query[:, pair]
+    for n, part in enumerate((own, other)):
+        for k in range(4):
+            b = n * 4 + k
+            here = slice(b * rows, (b + 1) * rows)
+            column = b if is_self else 16 + b
+            seq = cols[:, column : column + 1].astype(jnp.int32)
+            other_seq = (lane >= 16) & (lane < 20) & (lane != seq + 16)
+            ones_k = jnp.where(other_seq, neg_fill, jnp.where(lane < 3, 1.0, 0.0)).astype(low_t)
+            key = dot_nn(part[k], wk)
+            turn[...] = key.T
+            kt[:, here] = turn[features, :].astype(low_t)
+            k_all[here, :] = jnp.where(mine, key.astype(low_t), ones_k)
+            v_all[here, :] = jnp.where(mine, dot_nn(part[k], wv).astype(low_t), ones_v)
+            if is_self:
+                q_all[b] = dot_nn((hidden_own, hidden_other)[n][k], wq).astype(low_t)
+
+
+def pair_back(is_self, ids, *refs):
+    if is_self:
+        q_parts, do_own, do_other, k_all, v_all, kt, cols, row_data, back = refs[:9]
+        do_parts = (do_own, do_other)
+    else:
+        both_own, both_other, k_all, v_all, kt, back, dkv = refs[:7]
+        both_parts = (both_own, both_other)
+    q_all, do_all, dq_t, dk, dv, rank, turn = refs[-7:]
+    core = ids[1]
+    rows = q_all.shape[1]
+    keys = 8 * rows
+    mine = half_mask((rows, PAIR), 1, core)
+    features = pl.ds(pl.multiple_of(core * HEAD, HEAD), HEAD)
+    for n in range(2):
+        for k in range(4):
+            b = n * 4 + k
+            if is_self:
+                here = slice(b * rows, (b + 1) * rows)
+                rank[here, :] = jnp.broadcast_to(cols[:, 8 + b : 9 + b], (rows, 128))
+                q, do = q_parts[b], do_parts[n][k, :rows, :]
+                side = jnp.concatenate(
+                    (do_parts[n][k, rows : rows + 16, :], do_parts[n][k, rows + 16 :, :]), axis=1
+                )
+            else:
+                q, do = both_parts[n][k, :rows, :PAIR], both_parts[n][k, :rows, PAIR:]
+                side = both_parts[n][k, rows:, :]
+            side = side_lanes(side, core)
+            q_all[b] = jnp.where(mine, (q * 0.125).astype(low_t), side)
+            do_all[b] = jnp.where(mine, do, side)
+    dk[...] = jnp.zeros_like(dk)
+    dv[...] = jnp.zeros_like(dv)
+    tile = min(1024, keys)
+
+    def step(b, carry):
+        q, do = q_all[b], do_all[b]
+        dqt = jnp.zeros((HEAD, rows), wide_t)
+        for t in range(keys // tile):
+            here = slice(t * tile, (t + 1) * tile)
+            w = jnp.exp(dot_nt(k_all[here, :], q))
+            if is_self:
+                ranks = jnp.concatenate((rank[here, :],) * (rows // 128), axis=1)
+                index = lax.broadcasted_iota(jnp.int32, (tile, rows), 0)
+                own = lax.broadcasted_iota(jnp.int32, (tile, rows), 1) + (b * rows - t * tile)
+                w = jnp.where((ranks < row_data[pl.ds(8 + b, 1), :]) | (index == own), w, 0.0)
+            ds = (w * dot_nt(v_all[here, :], do)).astype(low_t)
+            dv[here, :] += dot_nn(w.astype(low_t), do)
+            dk[here, :] += dot_nn(ds, q)
+            dqt = dqt + dot_nn(kt[:, here], ds)
+        dq_t[b] = (dqt * 0.125).astype(low_t)
+        return carry
+
+    lax.fori_loop(0, 8, step, 0)
+    for n in range(2):
+        for k in range(4):
+            b = n * 4 + k
+            device = k * 2 + (core ^ n)
+            here = slice(b * rows, (b + 1) * rows)
+            back[device, :HEAD, :] = dq_t[b]
+            out, start = (back, HEAD) if is_self else (dkv, 0)
+            for value in (dk, dv):
+                turn[...] = value[here, :].T
+                out[device, start : start + HEAD, :] = turn[features, :].astype(low_t)
+                start += HEAD
+
+
+def pair_grads(is_self, ids, grads, own, other, *refs):
+    dw = refs[-1]
+    totals = [jnp.zeros((HEAD, D), wide_t) for n in range(grads.shape[1] // HEAD)]
+    for n in range(2):
+        for k in range(4):
+            device = k * 2 + (ids[1] ^ n)
+            for m in range(len(totals)):
+                source = refs[:2] if is_self and m == 0 else (own, other)
+                totals[m] += dot_nn(grads[device, m * HEAD : (m + 1) * HEAD, :], source[n][k])
+    for n, value in enumerate(totals):
+        for w in range(4):
+            dw[w, n * HEAD : (n + 1) * HEAD, :] = value[:, w * 128 : (w + 1) * 128].astype(low_t)
+
+
+def turned(value):
+    return value.astype(wide_t).T.astype(low_t)
+
+
+def first_back(ids, back, second_grad, normed, scale, self_mixed, lse, row_data, gs, wcq, wo, sums_in, *refs):
+    first_grad, branch, dealt, dq, sums = refs
+    dq[...] = turned(back[...].reshape(D, back.shape[2]))
+    total = second_grad[...] + dot_nt(dq[...], wcq[...])
+    grad, gain_a, shift_a = layer_norm_back(
+        total, normed[...], scale[:, 0:1], gs[0:1, :].astype(wide_t)
+    )
+    first_grad[...] = grad
+    low = grad.astype(low_t)
+    branch[...] = low
+    mixed = dot_nt(low, wo[...]).astype(low_t)
+    rows = low.shape[0]
+    sides = side_rows(lse, mixed, self_mixed, row_data)
+    for p in range(PAIRS):
+        dealt[p, :rows, :] = mixed[:, p * PAIR : (p + 1) * PAIR]
+        dealt[p, rows : rows + 16, :] = sides[p][:, :PAIR]
+        dealt[p, rows + 16 :, :] = sides[p][:, PAIR:]
+    zero = jnp.zeros_like(gain_a)
+    sums[...] = sums_in[...] + jnp.concatenate(
+        (gain_a, zero, zero, shift_a, zero, zero, zero, zero), axis=0
+    )
+
+
+def source_back(ids, parts, wckv, out, dkv):
+    rows = out.shape[0]
+    for device in range(8):
+        for n in range(2):
+            start = 2 * D + 128 + n * rows
+            dkv[n * D + device * HEAD : n * D + (device + 1) * HEAD, :] = parts[
+                device, :, start : start + rows
+            ]
+    out[...] = dot_nt(turned(dkv[...]), wckv[...])
+
+
+def hidden_back(ids, back, first_grad, wq, wkv, hidden_grad, stream_grad, all_t):
+    for device in range(8):
+        for n in range(3):
+            all_t[n * D + device * HEAD : n * D + (device + 1) * HEAD, :] = back[
+                device, n * HEAD : (n + 1) * HEAD, :
+            ]
+    hidden_grad[...] = first_grad[...] + dot_nt(turned(all_t[:D, :]), wq[...])
+    stream_grad[...] = dot_nt(turned(all_t[D:, :]), wkv[...])
+
+
+def add_parts(parts, rows, columns):
+    total = parts[0, rows, columns].astype(wide_t)
+    for n in range(1, parts.shape[0]):
+        total = total + parts[n, rows, columns].astype(wide_t)
+    return total.astype(low_t)
+
+
+def add_chips(ids, parts, dw, *outs):
+    width = parts.shape[2]
+    for e in range(4):
+        outs[e][:, :width] = add_parts(parts, slice(e * 32, (e + 1) * 32), slice(None))
+        piece = dw[ids[2] ^ e]
+        for g in range(4):
+            outs[e][:, width + g * 128 : width + (g + 1) * 128] = piece[g * 32 : (g + 1) * 32, :]
+
+
+def end_sums(ids, parts, dw, *outs):
+    width = 2 * D + 128
+    for e in range(4):
+        outs[e][:, :width] = add_parts(parts, slice(e * 16, (e + 1) * 16), slice(0, width))
+        outs[e][:, width : width + 128] = jnp.zeros((16, 128), low_t)
+        piece = dw[ids[2] ^ e]
+        for g in range(12):
+            start = width + 128 + g * 128
+            outs[e][:, start : start + 128] = piece[g * 16 : (g + 1) * 16, :]
+
+
+def add_shards(ids, *refs):
+    out = refs[8]
+
+    def total(parts):
+        value = parts[0][...].astype(wide_t)
+        for part in parts[1:]:
+            value = value + part[...].astype(wide_t)
+        return value.astype(low_t)
+
+    first, last = total(refs[:4]), total(refs[4:8])
+    width, half = first.shape[1], last.shape[1] // 2
+    for k in range(4):
+        out[k, :, :width] = first
+        out[k, :16, width:] = last[:, :half]
+        out[k, 16:, width:] = last[:, half:]
+
+
+def place_all(ids, own, other, *refs):
+    g_in, g_out, g_cross, g_cross_pair, g_cross_query, g_output, gains, shifts, g_query, g_pair = refs[:10]
+    pair_t, all_t = refs[10:]
+    half = FF // 2
+    start_cross = half + 2 * D
+    start_pair = start_cross + D // 2
+    start_end = start_pair + 4 * 128
+    half_end = own.shape[2] - start_end
+    for n, part in enumerate((own, other)):
+        core = ids[1] ^ n
+        for chip in range(4):
+            rows = slice(chip * 32, (chip + 1) * 32)
+            device = chip * 2 + core
+            for k in range(4):
+                g_in[rows, at128(k * 512 + core * 256, 256)] = part[
+                    chip, :, k * 256 : (k + 1) * 256
+                ].astype(wide_t)
+            for g in range(2):
+                g_out[at16(core * 256 + chip * 64 + g * 32, 32), :] = part[
+                    chip, :, half + g * D : half + (g + 1) * D
+                ].astype(wide_t)
+            g_cross[rows, at128(core * 256, 256)] = part[chip, :, start_cross:start_pair].astype(wide_t)
+            for g in range(4):
+                column = start_pair + g * 128
+                row = (g // 2) * D + device * HEAD + (g % 2) * 32
+                pair_t[at16(row, 32), :] = part[chip, :, column : column + 128].astype(wide_t)
+
+            def piece(column, width):
+                row, at = (0, column) if column < half_end else (16, column - half_end)
+                return part[chip, row : row + 16, start_end + at : start_end + at + width].astype(wide_t)
+
+            own_rows = at16(device * 16)
+            for column in range(0, D, 128):
+                g_cross_query[own_rows, column : column + 128] = piece(column, 128)
+                g_output[own_rows, column : column + 128] = piece(D + column, 128)
+            if n == 0 and chip == 0:
+                norms = piece(2 * D, 128)
+                gains[...], shifts[...] = norms[0:3], norms[3:6]
+            for g in range(12):
+                row = (g // 4) * D + device * HEAD + (g % 4) * 16
+                all_t[at16(row), :] = piece(2 * D + 256 + g * 128, 128)
+    g_cross_pair[...] = pair_t[...].T
+    g_query[...] = all_t[:D, :].T
+    g_pair[...] = all_t[D:, :].T
+
+
+def pack_start(ids, stream, source, wq, wkv, ffn_in, ffn_out, many, pack):
+    own = ids[0] * 2 + ids[1]
+    for k in range(4):
+        many[k, :, :D] = stream[...]
+        many[k, :, D:] = source[...]
+        start = 3 * D + FF + k * D
+        pack[:, start : start + D] = ffn_out[at16(own * 64 + k * 16), :]
+    pack[:, :D] = wq[at16(own * 16), :]
+    pack[:, D : 3 * D] = wkv[at16(own * 16), :]
+    pack[:, 3 * D : 3 * D + FF] = ffn_in[at16(own * 16), :]
+
+
+def pack_more(ids, *refs):
+    weights, gain, shift, rows_in, pack, many = refs[:4], *refs[4:]
+    rows = at16(ids[1] * 64, 64)
+    norms = (gain[...].astype(wide_t), shift[...].astype(wide_t), jnp.zeros((58, 128), wide_t))
+    norms = jnp.concatenate(norms, axis=0).astype(low_t)
+    for k in range(4):
+        start = 0
+        for w in weights:
+            pack[k, :, start : start + w.shape[1]] = w[rows, :]
+            start += w.shape[1]
+        pack[k, :, start:] = norms
+        many[k] = rows_in[...]
+
+
+def mask_data(ids, order, ranks, limits, cols, row_data, all_rows):
+    rows = cols.shape[0]
+    ends = [ids[3]]
+    for n in range(1, 4):
+        ends.append(ends[-1] + ids[3 + n])
+
+    def sequence(position):
+        return sum((position >= end).astype(wide_t) for end in ends)
+
+    for n in range(2):
+        for k in range(4):
+            b = n * 4 + k
+            device = k * 2 + (ids[1] ^ n)
+            here = at128(device * rows, rows)
+            index = lax.broadcasted_iota(jnp.int32, (1, rows), 1) + device * rows
+            all_rows[b : b + 1, :] = sequence(order[:, here])
+            all_rows[8 + b : 9 + b, :] = ranks[:, here].astype(wide_t)
+            all_rows[16 + b : 17 + b, :] = sequence(index)
+            row_data[8 + b : 9 + b, :] = limits[:, here].astype(wide_t)
+    row_data[0:8, :] = all_rows[0:8, :]
+    all_rows[24:32, :] = jnp.zeros((8, rows), wide_t)
+    all_rows[24:25, :] = all_rows[pl.ds(ids[0], 1), :]
+    row_data[16:24, :] = jnp.zeros((8, rows), wide_t)
+    row_data[16:17, :] = all_rows[pl.ds(ids[0], 1), :]
+    row_data[17:18, :] = row_data[pl.ds(8 + ids[0], 1), :]
+    cols[:, :32] = all_rows[...].T
+
+
+def pack_first(ids, *refs):
+    parts, (one, two) = refs[:4], refs[4:]
+    width = one.shape[1]
+    for e in range(4):
+        here = slice(e * 16, (e + 1) * 16)
+        one[here, :] = parts[e][:, :width]
+        for k in range(4):
+            two[k, here, :] = parts[e][:, width:]
+
+
+def core_swap(value):
+    return lax.ppermute(value, "core", [(0, 1), (1, 0)])
+
+
+def chip_swaps(parts):
+    moves = [[(i, i ^ k) for i in range(4)] for k in range(4)]
+    return [parts[0]] + [lax.ppermute(parts[k], "chip", moves[k]) for k in range(1, 4)]
+
+
+def shard_swaps(parts):
+    moves = [[(i, i ^ k) for i in range(4)] for k in range(4)]
+    return [parts[0]] + [lax.ppermute(parts[k], "wa", moves[k]) for k in range(1, 4)]
+
+
+def deal(value):
+    return lax.all_to_all(value, "chip", 0, 0, tiled=True)
+
+
+def deal_all(value):
+    return lax.all_to_all(value, ("chip", "core"), 0, 0, tiled=True)
+
+
+def deal_both(value):
+    own = deal(value)
+    return own, core_swap(own)
+
+
+def after(value, *others):
+    return lax.optimization_barrier((value,) + others)[0]
+
+
+def fast_shards(
+    hidden,
+    stream,
+    encoder,
+    lengths,
+    order,
+    ranks,
+    thresholds,
+    self_query,
+    self_key_value,
+    self_output,
+    cross_query,
+    cross_key_value,
+    cross_output,
+    ffn_in,
+    ffn_out,
+    norm_gain,
+    norm_shift,
+    cotangent,
+):
+    rows, keys = hidden.shape[1], order.shape[1]
+    chip, core, mw = lax.axis_index("chip"), lax.axis_index("core"), lax.axis_index("wa")
+    ids = jnp.concatenate((jnp.stack((chip, core, mw)).astype(jnp.int32), lengths[0]))
+    inputs = hidden[0]
+
+    many, pack1 = run(
+        pack_start,
+        [((4, rows, 2 * D), low_t), ((16, 3 * D + 2 * FF), low_t)],
+        ids,
+        [stream[0], encoder[0], self_query, self_key_value, ffn_in, ffn_out],
+    )
+    x_own = deal(many)
+    shards1 = shard_swaps([pack1] * 4)
+    copies2, hidden_copies = run(
+        pack_more,
+        [((4, 64, 5 * D + 128), low_t), ((4, rows, D), low_t)],
+        ids,
+        [after(self_output, pack1), cross_query, cross_key_value, cross_output, norm_gain, norm_shift]
+        + [inputs],
+    )
+    cols, row_data = run(
+        mask_data,
+        [((rows, 32), wide_t), ((24, rows), wide_t)],
+        ids,
+        [order, ranks, thresholds],
+        [((32, rows), wide_t)],
+    )
+    part1, copies3 = run(
+        pack_first,
+        [((64, 3 * D), low_t), ((4, 64, 2 * FF), low_t)],
+        ids,
+        [after(shards1[0], x_own, cols, copies2)] + shards1[1:],
+    )
+    slices1 = chip_swaps([part1] * 4)
+    slices1 = slices1 + [core_swap(part) for part in slices1]
+    shards2 = lax.all_to_all(after(copies2, x_own), "wa", 0, 0, tiled=True)
+    x_other = core_swap(after(x_own, part1))
+    stream_own, stream_other = (x_own, 0), (x_other, 0)
+    source_own, source_other = (x_own, 1), (x_other, 1)
+
+    attend_scratch = [
+        ((rows, D), low_t),
+        ((keys, D), low_t),
+        ((D, keys), low_t),
+        ((D, D), low_t),
+        ((keys, rows), wide_t),
+        ((2, keys, rows), wide_t),
+        ((D, rows), wide_t),
+    ]
+    self_low, self_mixed, self_lse, wq, wkv = run(
+        self_forward,
+        [((rows, D), low_t), ((rows, D), wide_t), ((HEADS, rows), wide_t)]
+        + [((D, D), low_t), ((D, 2 * D), low_t)],
+        ids,
+        [inputs, stream_own, stream_other, *slices1, cols, row_data],
+        attend_scratch,
+        us=15,
+    )
+    shards2_other = core_swap(after(shards2, self_low))
+    slices3 = deal(after(copies3, shards2, self_low))
+    (
+        first,
+        normed,
+        scale,
+        first_low,
+        cross_low,
+        cross_mixed,
+        cross_lse,
+        cross_q,
+        wo,
+        wcq,
+        wckv,
+        wco,
+        gs,
+    ) = run(
+        cross_forward,
+        [((rows, D), wide_t)] * 2
+        + [((rows, 128), wide_t)]
+        + [((rows, D), low_t)] * 2
+        + [((rows, D), wide_t), ((HEADS, rows), wide_t), ((rows, D), low_t)]
+        + [((D, D), low_t), ((D, D), low_t), ((D, 2 * D), low_t), ((D, D), low_t), ((16, D), low_t)],
+        ids,
+        [inputs, self_low, source_own, source_other, shards2, shards2_other, cols, row_data],
+        attend_scratch,
+        us=15,
+    )
+    slices3_other = core_swap(after(slices3, cross_low))
+    hidden_own = deal(after(hidden_copies, slices3))
+    width_s = 2 * FF // 2 + 3 * D + D // 2
+    result, cross_dealt, second_grad, keep_a, send_a, sums = run(
+        feed_forward,
+        [
+            ((rows, D), low_t),
+            ((PAIRS, rows + 16, 2 * PAIR), low_t),
+            ((rows, D), wide_t),
+            ((rows, width_s), low_t),
+            ((rows, width_s), low_t),
+            ((8, D), wide_t),
+        ],
+        ids,
+        [first, cross_low, cross_mixed, cross_lse, row_data, cross_q, wco, gs]
+        + [cotangent[0], slices3, slices3_other],
+        [((rows, FF), wide_t), ((2, D, FF // 2), low_t), ((2, FF // 2, D), low_t)],
+        us=8,
+    )
+    head_shapes = [((keys, PAIR), low_t)] * 2 + [((HEAD, keys), low_t)]
+    cross_head = run(
+        functools.partial(pair_setup, False),
+        head_shapes,
+        ids,
+        [source_own, source_other, wckv, after(cols, cross_dealt)],
+        [((PAIR, rows), wide_t)],
+        us=4,
+    )
+    both_own = deal(after(cross_dealt, hidden_own))
+    both_other = core_swap(after(both_own, cross_head[0]))
+    width_a = FF // 2 + 2 * D + D // 2
+    (dealt_a,) = run(
+        grads_a,
+        [((4, 128, width_a), low_t)],
+        ids,
+        [keep_a, core_swap(after(send_a, hidden_own))],
+        [((D, FF // 2), low_t), ((FF // 2, D), low_t), ((D, D // 2), low_t)],
+        us=6,
+    )
+    rows_a = deal(after(dealt_a, both_own))
+
+    back_scratch = (
+        [((8, rows, PAIR), low_t)] * 2
+        + [((8, HEAD, rows), low_t)]
+        + [((keys, PAIR), wide_t)] * 3
+        + [((PAIR, rows), wide_t)]
+    )
+    cross_dq_t, cross_dkv = run(
+        functools.partial(pair_back, False),
+        [((8, HEAD, rows), low_t), ((8, 2 * HEAD, rows), low_t)],
+        ids,
+        [after(both_own, dealt_a), both_other, *cross_head],
+        back_scratch,
+        us=16,
+    )
+    hidden_other = core_swap(after(hidden_own, both_own))
+    self_head = run(
+        functools.partial(pair_setup, True),
+        [((8, rows, PAIR), low_t)] + head_shapes,
+        ids,
+        [stream_own, stream_other, wkv, after(cols, cross_dq_t), hidden_own, hidden_other, wq],
+        [((PAIR, rows), wide_t)],
+        us=4,
+    )
+    (cross_dw,) = run(
+        functools.partial(pair_grads, False),
+        [((4, 2 * HEAD, 128), low_t)],
+        ids,
+        [cross_dkv, source_own, source_other],
+    )
+    cross_back = deal_all(after(cross_dq_t, rows_a, self_head[0]))
+    shards_a = run(
+        add_chips,
+        [((32, width_a + 512), low_t)] * 4,
+        ids,
+        [after(rows_a, cross_dq_t), cross_dw],
+    )
+    first_grad, self_branch, self_dealt, cross_dq, sums = run(
+        first_back,
+        [
+            ((rows, D), wide_t),
+            ((rows, D), low_t),
+            ((PAIRS, rows + 32, PAIR), low_t),
+            ((rows, D), low_t),
+            ((8, D), wide_t),
+        ],
+        ids,
+        [after(cross_back, *shards_a), second_grad, normed, scale, self_mixed, self_lse, row_data, gs, wcq, wo, sums],
+        us=4,
+    )
+    do_own = deal(self_dealt)
+    moved_a = shard_swaps([after(part, first_grad) for part in shards_a])
+    (dealt_b,) = run(
+        grads_b,
+        [((8, 64, 2 * D + 128 + 2 * rows), low_t)],
+        ids,
+        [first_low, cross_dq, self_low, self_branch, sums, cross_dkv],
+        [((D, D), low_t)] * 2,
+        us=3,
+    )
+    rows_b = deal_all(after(dealt_b, do_own))
+    do_other = core_swap(after(do_own, dealt_b))
+    (self_back_t,) = run(
+        functools.partial(pair_back, True),
+        [((8, 3 * HEAD, rows), low_t)],
+        ids,
+        [self_head[0], after(do_own, dealt_b, *shards_a), do_other, *self_head[1:], cols, row_data],
+        back_scratch,
+        us=16,
+    )
+    (self_dw,) = run(
+        functools.partial(pair_grads, True),
+        [((4, 3 * HEAD, 128), low_t)],
+        ids,
+        [self_back_t, stream_own, stream_other, hidden_own, hidden_other],
+    )
+    self_back = deal_all(after(self_back_t, rows_b, *moved_a))
+    end_width = 2 * D + 2 * 128 + 12 * 128
+    end_parts = run(end_sums, [((16, end_width), low_t)] * 4, ids, [rows_b, self_dw])
+    moved_end = shard_swaps(end_parts)
+    (source_grad,) = run(
+        source_back,
+        [((rows, D), wide_t)],
+        ids,
+        [rows_b, after(wckv, end_parts[0])],
+        [((2 * D, rows), low_t)],
+        us=3,
+    )
+    (copies_end,) = run(
+        add_shards,
+        [((4, 32, width_a + 512 + end_width // 2), low_t)],
+        ids,
+        [*moved_a, after(moved_end[0], source_grad), *moved_end[1:]],
+    )
+    all_own = deal(after(copies_end, self_back))
+    hidden_grad, stream_grad = run(
+        hidden_back,
+        [((rows, D), wide_t)] * 2,
+        ids,
+        [self_back, first_grad, wq, wkv],
+        [((3 * D, rows), low_t)],
+        us=3,
+    )
+    all_other = core_swap(after(all_own, hidden_grad))
+    (
+        grad_in,
+        grad_out,
+        grad_cross_output,
+        grad_cross_pair,
+        grad_cross_query,
+        grad_output,
+        gain_grads,
+        shift_grads,
+        grad_query,
+        grad_pair,
+    ) = run(
+        place_all,
+        [((128, FF), wide_t), ((D, D), wide_t), ((128, D), wide_t), ((128, 2 * D), wide_t)]
+        + [((128, D), wide_t)] * 2
+        + [((3, 128), wide_t)] * 2
+        + [((128, D), wide_t), ((128, 2 * D), wide_t)],
+        ids,
+        [all_own, all_other],
+        [((2 * D, 128), wide_t), ((3 * D, 128), wide_t)],
+    )
+    return (
+        result[None],
+        hidden_grad[None],
+        stream_grad[None],
+        source_grad[None],
+        grad_query,
+        grad_pair,
+        grad_output,
+        grad_cross_query,
+        grad_cross_pair,
+        grad_cross_output,
+        grad_in,
+        grad_out,
+        gain_grads,
+        shift_grads,
+    )
+
+
 def solution(mesh):
     in_specs = (
         P("wa", "ctx", None),
@@ -424,4 +1415,18 @@
         P(None, "wa"),
         P(None, "wa"),
     )
-    return jax.shard_map(shards, mesh=mesh, in_specs=in_specs, out_specs=out_specs, check_vma=False)
+    if mesh.axis_names != ("ctx", "wa") or mesh.shape["ctx"] != HEADS or mesh.shape["wa"] != 4:
+        return jax.shard_map(
+            general_shards, mesh=mesh, in_specs=in_specs, out_specs=out_specs, check_vma=False
+        )
+
+    def finer(spec):
+        return P(*(("chip", "core") if axis == "ctx" else axis for axis in spec))
+
+    return jax.shard_map(
+        fast_shards,
+        mesh=Mesh(mesh.devices.reshape(4, 2, 4), ("chip", "core", "wa")),
+        in_specs=tuple(finer(spec) for spec in in_specs),
+        out_specs=tuple(finer(spec) for spec in out_specs),
+        check_vma=False,
+    )

time: 841 us -> 283 us (0.34); the launches traced: 830 us -> 282 us
  waiting for transfers between devices: 389 us -> 76.4 us
  blocking collectives: 170 us -> 0 us
  Pallas kernels: 0 us -> 133 us
  local copies, waits for them, and re-layouts: 116 us -> 8.31 us
  matrix products: 99.7 us -> 0 us
  starting transfers between devices: 0.95 us -> 61.8 us
  other arithmetic: 29.2 us -> 1.24 us
  between operations: 15.7 us -> 0.96 us
  loops' own time: 9.44 us -> 0 us
    reduce_scatter x7 -> x0, waiting for transfers between devices: 215 us -> none  [the longest x1 58 us: shards(): lax.psum_scatter(self_terms, 'ctx', scatter_dimension=0, tiled=True)]
    pallas_call x0 -> x22, Pallas kernels: none -> 133 us  [run(): pl.pallas_call(kernel, name=getattr(body, 'func', body).__name__, out_sha...]
    unnamed x23 -> x0, waiting for transfers between devices: 110 us -> none
    dot_general x52 -> x0, matrix products: 99.7 us -> none  [the longest x24 46.3 us: matmul(): return jnp.dot(left, right, preferred_element_type=jnp.float32)]
    psum x1 -> x0, blocking collectives: 89.6 us -> none  [shards(): lax.psum((share_query, share_pair, share_output, share_cross_query, share...]
    all_gather x6 -> x0, blocking collectives: 80.3 us -> none  [the longest x1 16.5 us: shards(): lax.all_gather(self_output, 'wa', axis=0, tiled=True)]
    all_gather x6 -> x0, waiting for transfers between devices: 64.1 us -> none  [the longest x1 31.5 us: shards(): lax.all_gather(self_key_value, 'wa', axis=0, tiled=True)]
    all_to_all x0 -> x11, waiting for transfers between devices: none -> 60 us  [the longest x7 52.5 us: deal(): return lax.all_to_all(value, 'chip', 0, 0, tiled=True)]
  transfers between devices with their start and end apart: 18 -> 35, of which waited for: 14 -> 17; matrix products, arithmetic and copies ran while one was open for 21% -> 0% of each run, Pallas kernels for 0% -> 42%
where the time goes in v3:
time: 283 us; the launch traced here: 282 us
  Pallas kernels  133 us (47%)
  waiting for transfers between devices  76.4 us (27%)
  starting transfers between devices  61.8 us (22%)
  local copies, waits for them, and re-layouts  8.31 us (3%)
    pallas_call x22, Pallas kernels, run(): pl.pallas_call(kernel, name=getattr(body, 'func', body).__name__, out_sha...  133 us
    all_to_all x7, waiting for transfers between devices, deal(): return lax.all_to_all(value, 'chip', 0, 0, tiled=True)  52.5 us
    all_to_all x7, starting transfers between devices, deal(): return lax.all_to_all(value, 'chip', 0, 0, tiled=True)  28.3 us
    ppermute x9, starting transfers between devices, shard_swaps(): lax.ppermute(parts[k], 'wa', moves[k])  13.2 us
    all_to_all x3, starting transfers between devices, deal_all(): return lax.all_to_all(value, ('chip', 'core'), 0, 0, tiled=True)  10.8 us
    ppermute x3, waiting for transfers between devices, chip_swaps(): lax.ppermute(parts[k], 'chip', moves[k])  8.87 us
    unnamed x66, local copies, waits for them, and re-layouts  8.31 us
  transfers between devices with their start and end apart: 35, of which 17 were waited for; matrix products, arithmetic and copies ran while one was open for 0% of the time, Pallas kernels for 42%

profile of v3, /device:TPU:0, one launch (start us, length us, event | category | flops | bytes accessed | tf_op | source)
XLA Modules:
  0.0 282.0 jit_solution(7688664934949818508)
XLA Ops:
  4.9 5.3 %all-to-all-start = ((bf16[4,256,1024]{2,1,0:T(8,128)(2,1)}), bf16[4,256,1024]{2,1,0:T(8,128)(2,1)S(1)}, u32[]{:S(2)}, u32[]{:S(2)}) async-start(bf16[4,256,1024]{2,1,0:T(8,128)(2,1)} %get-tuple-element.111), calls=%async_computation | async-start | bytes 4194304 | tf_op jit(solution)/shard_map/all_to_all | solution.py:1076
  19.1 16.0 %all-to-all-done.refs_1_.refs_2_.refs_0_ = bf16[4,256,1024]{2,1,0:T(8,128)(2,1)S(1)} async-done(((bf16[4,256,1024]{2,1,0:T(8,128)(2,1)}), bf16[4,256,1024]{2,1,0:T(8,128)(2,1)S(1)}, u32[]{:S(2)}, u32[]{:S(2)}) %all-to-all-start) | async-done | bytes 2097184 | tf_op jit(solution)/shard_map/all_to_all | solution.py:1076
  39.3 5.0 %all-to-all-start.1 = ((bf16[4,64,2688]{2,1,0:T(8,128)(2,1)}), bf16[4,64,2688]{2,1,0:T(8,128)(2,1)S(1)}, u32[]{:S(2)}, u32[]{:S(2)}) async-start(bf16[4,64,2688]{2,1,0:T(8,128)(2,1)} %get-tuple-element.121), calls=%async_computation.1 | async-start | bytes 2752512 | tf_op jit(solution)/shard_map/all_to_all | solution.py:1147
  47.8 5.4 %collective-permute-done.6.refs_6_ = bf16[64,1536]{1,0:T(8,128)(2,1)S(1)} collective-permute-done((bf16[64,1536]{1,0:T(8,128)(2,1)}, bf16[64,1536]{1,0:T(8,128)(2,1)S(1)}, u32[]{:S(2)}, u32[]{:S(2)}) %collective-permute-start.6) | collective-permute-done | bytes 196640 | tf_op jit(solution)/shard_map/ppermute | solution.py:1067
  59.0 14.7 %self_forward.1 = (bf16[256,512]{1,0:T(8,128)(2,1)}, f32[256,512]{1,0:T(8,128)}, f32[8,256]{1,0:T(8,128)}, bf16[512,512]{1,0:T(8,128)(2,1)}, bf16[512,1024]{1,0:T(8,128)(2,1)}) custom-call(s32[7]{0:T(128)} %pad_add_fusion.ids, bf16[256,512]{1,0:T(8,128)(2,1)} %bitcast.16, bf16[4,256,1024]{2,1,0:T(8,128)(2,1)} %copy-done.1, ...), custom_call_target="tpu_custom_call" | custom-call | flops 15000000512 | bytes 8454144 | tf_op jit(solution)/shard_map/self_forward/pallas_call | solution.py:420
  73.7 4.0 %all-to-all-done.1.refs_4_ = bf16[4,64,2688]{2,1,0:T(8,128)(2,1)S(1)} async-done(((bf16[4,64,2688]{2,1,0:T(8,128)(2,1)}), bf16[4,64,2688]{2,1,0:T(8,128)(2,1)S(1)}, u32[]{:S(2)}, u32[]{:S(2)}) %all-to-all-start.1) | async-done | bytes 1376288 | tf_op jit(solution)/shard_map/all_to_all | solution.py:1147
  82.4 15.9 %cross_forward.1 = (f32[256,512]{1,0:T(8,128)}, f32[256,512]{1,0:T(8,128)}, f32[256,128]{1,0:T(8,128)}, bf16[256,512]{1,0:T(8,128)(2,1)}, bf16[256,512]{1,0:T(8,...) custom-call(s32[7]{0:T(128)} %pad_add_fusion.ids, ...), custom_call_target="tpu_custom_call" | custom-call | flops 15000000512 | bytes 12664832 | tf_op jit(solution)/shard_map/cross_forward/pallas_call | solution.py:420
  98.3 8.8 %all-to-all-done.2.refs_9_ = bf16[4,64,4096]{2,1,0:T(8,128)(2,1)S(1)} async-done(((bf16[4,64,4096]{2,1,0:T(8,128)(2,1)}), bf16[4,64,4096]{2,1,0:T(8,128)(2,1)S(1)}, u32[]{:S(2)}, u32[]{:S(2)}) %all-to-all-start.2) | async-done | bytes 2097184 | tf_op jit(solution)/shard_map/all_to_all | solution.py:1076
  107.1 3.7 %all-to-all-start.3 = ((bf16[4,256,512]{2,1,0:T(8,128)(2,1)}), bf16[4,256,512]{2,1,0:T(8,128)(2,1)S(1)}, u32[]{:S(2)}, u32[]{:S(2)}) async-start(bf16[4,256,512]{2,1,0:T(8,128)(2,1)} %get-tuple-element.137), calls=%async_computation.3 | async-start | bytes 2097152 | tf_op jit(solution)/shard_map/all_to_all | solution.py:1076
  111.4 10.2 %feed_forward.1 = (bf16[256,512]{1,0:T(8,128)(2,1)}, bf16[4,272,256]{2,1,0:T(8,128)(2,1)}, f32[256,512]{1,0:T(8,128)}, bf16[256,3840]{1,0:T(8,128)(2,1)}, bf16[256,3840]{1,0:T(8,128)(2,1)}, /*index=5*/f32[8,512]{1,0:T(8,128)}) custom-call(s32[7]{0:T(128)} %pad_add_fusion.ids, f32[256,512]{1,0:T(8,128)} %get-tuple-element.123.refs_0_, ...), custom_call_target="tpu_custom_call" | custom-call | flops 8000000000 | bytes 11894784 | tf_op jit(solution)/shard_map/feed_forward/pallas_call | solution.py:420
  125.2 4.1 %all-to-all-start.4 = ((bf16[4,272,256]{2,1,0:T(8,128)(2,1)}), bf16[4,272,256]{2,1,0:T(8,128)(2,1)}, u32[]{:S(2)}, u32[]{:S(2)}) async-start(bf16[4,272,256]{2,1,0:T(8,128)(2,1)} %get-tuple-element.138), calls=%async_computation.4 | async-start | bytes 1114112 | tf_op jit(solution)/shard_map/all_to_all | solution.py:1076
  129.4 4.8 %pair_setup.2 = (bf16[2048,128]{1,0:T(8,128)(2,1)}, bf16[2048,128]{1,0:T(8,128)(2,1)}, bf16[64,2048]{1,0:T(8,128)(2,1)}) custom-call(s32[7]{0:T(128)} %pad_add_fusion.ids, bf16[4,256,1024]{2,1,0:T(8,128)(2,1)} %copy-done.1, bf16[4,256,1024]{2,1,0:T(8,128)(2,1)} %collective-permute-done.3.refs_2_.refs_3_.refs_1_, ...), custom_call_target="tpu_custom_call" | custom-call | flops 4000000000 | bytes 6586368 | tf_op jit(solution)/shard_map/pair_setup/pallas_call | solution.py:420
  134.1 4.6 %all-to-all-done.4.refs_0_ = bf16[4,272,256]{2,1,0:T(8,128)(2,1)} async-done(((bf16[4,272,256]{2,1,0:T(8,128)(2,1)}), bf16[4,272,256]{2,1,0:T(8,128)(2,1)}, u32[]{:S(2)}, u32[]{:S(2)}) %all-to-all-start.4) | async-done | bytes 557088 | tf_op jit(solution)/shard_map/all_to_all | solution.py:1076
  140.6 5.1 %grads_a.1 = bf16[4,128,2304]{2,1,0:T(8,128)(2,1)} custom-call(s32[7]{0:T(128)} %pad_add_fusion.ids, bf16[256,3840]{1,0:T(8,128)(2,1)} %get-tuple-element.139.refs_0_, bf16[256,3840]{1,0:T(8,128)(2,1)} %copy-done.10), custom_call_target="tpu_custom_call" | custom-call | flops 6000000000 | bytes 6291456 | tf_op jit(solution)/shard_map/grads_a/pallas_call | solution.py:420
  149.4 14.8 %pair_back.2 = (bf16[8,64,256]{2,1,0:T(8,128)(2,1)}, bf16[8,128,256]{2,1,0:T(8,128)(2,1)}) custom-call(s32[7]{0:T(128)} %pad_add_fusion.ids, bf16[4,272,256]{2,1,0:T(8,128)(2,1)} %all-to-all-done.4.refs_0_, bf16[4,272,256]{2,1,0:T(8,128)(2,1)} %collective-permute-done.14.refs_1_, bf16[2048,128]{1,0:T(8,128)(2,1)} %get-tuple-element.145.refs_2_, ...), custom_call_target="tpu_custom_call" | custom-call | flops 16000000000 | bytes 3211264 | tf_op jit(solution)/shard_map/pair_back/pallas_call | solution.py:420
  164.2 6.2 %pair_setup.3 = (bf16[8,256,128]{2,1,0:T(8,128)(2,1)}, bf16[2048,128]{1,0:T(8,128)(2,1)}, bf16[2048,128]{1,0:T(8,128)(2,1)}, bf16[64,2048]{1,0:T(8,128)(2,1)}) custom-call(s32[7]{0:T(128)} %pad_add_fusion.ids, bf16[4,256,1024]{2,1,0:T(8,128)(2,1)} %copy-done.1, bf16[4,256,1024]{2,1,0:T(8,128)(2,1)} %collective-permute-done.3.refs_2_.refs_3_.refs_1_, ...), custom_call_target="tpu_custom_call" | custom-call | flops 4000000000 | bytes 9732096 | tf_op jit(solution)/shard_map/pair_setup/pallas_call | solution.py:420
  170.4 7.1 %all-to-all-done.5.refs_0_ = bf16[4,128,2304]{2,1,0:T(8,128)(2,1)S(1)} async-done(((bf16[4,128,2304]{2,1,0:T(8,128)(2,1)}), bf16[4,128,2304]{2,1,0:T(8,128)(2,1)S(1)}, u32[]{:S(2)}, u32[]{:S(2)}) %all-to-all-start.5) | async-done | bytes 2359328 | tf_op jit(solution)/shard_map/all_to_all | solution.py:1076
  181.1 3.9 %pair_grads.2.refs_1_ = bf16[4,128,128]{2,1,0:T(8,128)(2,1)} custom-call(s32[7]{0:T(128)} %pad_add_fusion.ids, bf16[8,128,256]{2,1,0:T(8,128)(2,1)} %get-tuple-element.157.refs_0_.refs_5_, bf16[4,256,1024]{2,1,0:T(8,128)(2,1)} %copy-done.1, bf16[4,256,1024]{2,1,0:T(8,128)(2,1)} %collective-permute-done.3.refs_2_.refs_3_.refs_1_), custom_call_target="tpu_custom_call" | custom-call | flops 2000000000 | bytes 4849664 | tf_op jit(solution)/shard_map/pair_grads/pallas_call | solution.py:420
  192.1 3.8 %all-to-all-start.7 = ((bf16[4,288,128]{2,1,0:T(8,128)(2,1)}), bf16[4,288,128]{2,1,0:T(8,128)(2,1)S(1)}, u32[]{:S(2)}, u32[]{:S(2)}) async-start(bf16[4,288,128]{2,1,0:T(8,128)(2,1)} %get-tuple-element.171), calls=%async_computation.7 | async-start | bytes 589824 | tf_op jit(solution)/shard_map/all_to_all | solution.py:1076
  210.6 18.1 %pair_back.3.refs_0_ = bf16[8,192,256]{2,1,0:T(8,128)(2,1)} custom-call(s32[7]{0:T(128)} %pad_add_fusion.ids, bf16[8,256,128]{2,1,0:T(8,128)(2,1)} %get-tuple-element.153.refs_0_, bf16[4,288,128]{2,1,0:T(8,128)(2,1)} %copy-done.8, bf16[4,288,128]{2,1,0:T(8,128)(2,1)} %copy-done.12, bf16[2048,128]{1,0:T(8,128)(2,1)} %get-tuple-element.178.refs_3_, ...), custom_call_target="tpu_custom_call" | custom-call | flops 16000000000 | bytes 3268608 | tf_op jit(solution)/shard_map/pair_back/pallas_call | solution.py:420
  235.8 4.9 %pair_grads.3.refs_1_ = bf16[4,192,128]{2,1,0:T(8,128)(2,1)} custom-call(s32[7]{0:T(128)} %pad_add_fusion.ids, bf16[8,192,256]{2,1,0:T(8,128)(2,1)} %pair_back.3.refs_0_, bf16[4,256,1024]{2,1,0:T(8,128)(2,1)} %copy-done.1, bf16[4,256,1024]{2,1,0:T(8,128)(2,1)} %collective-permute-done.3.refs_2_.refs_3_.refs_1_, bf16[4,256,512]{2,1,0:T(8,128)(2,1)} %copy-done.6, ...), custom_call_target="tpu_custom_call" | custom-call | flops 2000000000 | bytes 7274496 | tf_op jit(solution)/shard_map/pair_grads/pallas_call | solution.py:420
  257.2 4.2 %all-to-all-start.10 = ((bf16[4,32,4224]{2,1,0:T(8,128)(2,1)}), bf16[4,32,4224]{2,1,0:T(8,128)(2,1)S(1)}, u32[]{:S(2)}, u32[]{:S(2)}) async-start(bf16[4,32,4224]{2,1,0:T(8,128)(2,1)} %add_shards.1), calls=%async_computation.10 | async-start | bytes 2162688 | tf_op jit(solution)/shard_map/all_to_all | solution.py:1076
  264.5 9.7 %all-to-all-done.10.refs_0_ = bf16[4,32,4224]{2,1,0:T(8,128)(2,1)S(1)} async-done(((bf16[4,32,4224]{2,1,0:T(8,128)(2,1)}), bf16[4,32,4224]{2,1,0:T(8,128)(2,1)S(1)}, u32[]{:S(2)}, u32[]{:S(2)}) %all-to-all-start.10) | async-done | bytes 1081376 | tf_op jit(solution)/shard_map/all_to_all | solution.py:1076
  278.0 4.1 %place_all.1 = (f32[128,2048]{1,0:T(8,128)}, f32[512,512]{1,0:T(8,128)}, f32[128,512]{1,0:T(8,128)}, f32[128,1024]{1,0:T(8,128)}, f32[128,512]{1,0:T(8,128)}, /*...) custom-call(s32[7]{0:T(128)} %pad_add_fusion.ids, ...), custom_call_target="tpu_custom_call" | custom-call | flops 2000000000 | bytes 6360064 | tf_op jit(solution)/shard_map/place_all/pallas_call | solution.py:420
  (135 shorter events, 96.7 us)
Async XLA Ops:
  4.9 30.2 %all-to-all-start = ((bf16[4,256,1024]{2,1,0:T(8,128)(2,1)}), bf16[4,256,1024]{2,1,0:T(8,128)(2,1)S(1)}, u32[]{:S(2)}, u32[]{:S(2)}) async-start(bf16[4,256,1024]{2,1,0:T(8,128)(2,1)} %get-tuple-element.111), calls=%async_computation | async-start | bytes 4194304 | tf_op jit(solution)/shard_map/all_to_all | solution.py:1076
  10.2 24.9 %collective-permute-start.2 = (bf16[16,5632]{1,0:T(8,128)(2,1)S(1)}, bf16[16,5632]{1,0:T(8,128)(2,1)S(1)}, u32[]{:S(2)}, u32[]{:S(2)}) collective-permute-start(bf16[16,5632]{1,0:T(8,128)(2,1)S(1)} %copy-done.26), channel_id=1, source_target_pairs={{0,3},{1,2},{2,1},{3,0},{4,7},{5,6},{6,5},{7,4},{8,11},{9,10},{10,... | collective-permute-start | bytes 540680 | tf_op jit(solution)/shard_map/ppermute | solution.py:1072
  13.8 21.3 %collective-permute-start.1 = (bf16[16,5632]{1,0:T(8,128)(2,1)S(1)}, bf16[16,5632]{1,0:T(8,128)(2,1)S(1)}, u32[]{:S(2)}, u32[]{:S(2)}) collective-permute-start(bf16[16,5632]{1,0:T(8,128)(2,1)S(1)} %copy-done.26), channel_id=1, source_target_pairs={{0,2},{1,3},{2,0},{3,1},{4,6},{5,7},{6,4},{7,5},{8,10},{9,11},{10,... | collective-permute-start | bytes 540680 | tf_op jit(solution)/shard_map/ppermute | solution.py:1072
  13.8 21.3 %collective-permute-start = (bf16[16,5632]{1,0:T(8,128)(2,1)S(1)}, bf16[16,5632]{1,0:T(8,128)(2,1)S(1)}, u32[]{:S(2)}, u32[]{:S(2)}) collective-permute-start(bf16[16,5632]{1,0:T(8,128)(2,1)S(1)} %copy-done.26), channel_id=1, source_target_pairs={{0,1},{1,0},{2,3},{3,2},{4,5},{5,4},{6,7},{7,6},{8,9},{9,8},{10,11... | collective-permute-start | bytes 540680 | tf_op jit(solution)/shard_map/ppermute | solution.py:1072
  39.3 19.1 %collective-permute-start.3 = (bf16[4,256,1024]{2,1,0:T(8,128)(2,1)S(1)}, bf16[4,256,1024]{2,1,0:T(8,128)(2,1)}, u32[]{:S(2)}, u32[]{:S(2)}) collective-permute-start(bf16[4,256,1024]{2,1,0:T(8,128)(2,1)S(1)} %all-to-all-done.refs_1_.refs_2_.refs_0_), channel_id=1, source_target_pairs={{0,4},{4,0},{1,5},{5,1},{2,6},{6,2},{3,7},{7,3},{8,12},{12,8},{9,1... | collective-permute-start | bytes 6291464 | tf_op jit(solution)/shard_map/ppermute | solution.py:1062
  39.3 38.4 %all-to-all-start.1 = ((bf16[4,64,2688]{2,1,0:T(8,128)(2,1)}), bf16[4,64,2688]{2,1,0:T(8,128)(2,1)S(1)}, u32[]{:S(2)}, u32[]{:S(2)}) async-start(bf16[4,64,2688]{2,1,0:T(8,128)(2,1)} %get-tuple-element.121), calls=%async_computation.1 | async-start | bytes 2752512 | tf_op jit(solution)/shard_map/all_to_all | solution.py:1147
  45.7 10.9 %collective-permute-start.5 = (bf16[64,1536]{1,0:T(8,128)(2,1)}, bf16[64,1536]{1,0:T(8,128)(2,1)S(1)}, u32[]{:S(2)}, u32[]{:S(2)}) collective-permute-start(bf16[64,1536]{1,0:T(8,128)(2,1)} %get-tuple-element.117.refs_3_), channel_id=1, source_target_pairs={{0,16},{8,24},{16,0},{24,8},{1,17},{9,25},{17,1},{25,9},{2,18},{10... | collective-permute-start | bytes 589832 | tf_op jit(solution)/shard_map/ppermute | solution.py:1067
  47.2 9.5 %collective-permute-start.4 = (bf16[64,1536]{1,0:T(8,128)(2,1)}, bf16[64,1536]{1,0:T(8,128)(2,1)S(1)}, u32[]{:S(2)}, u32[]{:S(2)}) collective-permute-start(bf16[64,1536]{1,0:T(8,128)(2,1)} %get-tuple-element.117.refs_3_), channel_id=1, source_target_pairs={{0,8},{8,0},{16,24},{24,16},{1,9},{9,1},{17,25},{25,17},{2,10},{10... | collective-permute-start | bytes 589832 | tf_op jit(solution)/shard_map/ppermute | solution.py:1067
  78.8 28.3 %all-to-all-start.2 = ((bf16[4,64,4096]{2,1,0:T(8,128)(2,1)}), bf16[4,64,4096]{2,1,0:T(8,128)(2,1)S(1)}, u32[]{:S(2)}, u32[]{:S(2)}) async-start(bf16[4,64,4096]{2,1,0:T(8,128)(2,1)} %get-tuple-element.131), calls=%async_computation.2 | async-start | bytes 4194304 | tf_op jit(solution)/shard_map/all_to_all | solution.py:1076
  107.1 18.1 %all-to-all-start.3 = ((bf16[4,256,512]{2,1,0:T(8,128)(2,1)}), bf16[4,256,512]{2,1,0:T(8,128)(2,1)S(1)}, u32[]{:S(2)}, u32[]{:S(2)}) async-start(bf16[4,256,512]{2,1,0:T(8,128)(2,1)} %get-tuple-element.137), calls=%async_computation.3 | async-start | bytes 2097152 | tf_op jit(solution)/shard_map/all_to_all | solution.py:1076
  125.2 14.1 %collective-permute-start.13 = (bf16[256,3840]{1,0:T(8,128)(2,1)}, bf16[256,3840]{1,0:T(8,128)(2,1)S(1)}, u32[]{:S(2)}, u32[]{:S(2)}) collective-permute-start(bf16[256,3840]{1,0:T(8,128)(2,1)} %get-tuple-element.141), channel_id=1, source_target_pairs={{0,4},{4,0},{1,5},{5,1},{2,6},{6,2},{3,7},{7,3},{8,12},{12,8},{9,1... | collective-permute-start | bytes 5898248 | tf_op jit(solution)/shard_map/ppermute | solution.py:1062
  125.2 13.5 %all-to-all-start.4 = ((bf16[4,272,256]{2,1,0:T(8,128)(2,1)}), bf16[4,272,256]{2,1,0:T(8,128)(2,1)}, u32[]{:S(2)}, u32[]{:S(2)}) async-start(bf16[4,272,256]{2,1,0:T(8,128)(2,1)} %get-tuple-element.138), calls=%async_computation.4 | async-start | bytes 1114112 | tf_op jit(solution)/shard_map/all_to_all | solution.py:1076
  138.7 25.5 %collective-permute-start.15 = (bf16[4,256,512]{2,1,0:T(8,128)(2,1)S(1)}, bf16[4,256,512]{2,1,0:T(8,128)(2,1)}, u32[]{:S(2)}, u32[]{:S(2)}) collective-permute-start(bf16[4,256,512]{2,1,0:T(8,128)(2,1)S(1)} %all-to-all-done.3.refs_4_.refs_3_), channel_id=1, source_target_pairs={{0,4},{4,0},{1,5},{5,1},{2,6},{6,2},{3,7},{7,3},{8,12},{12,8},{9,1... | collective-permute-start | bytes 3145736 | tf_op jit(solution)/shard_map/ppermute | solution.py:1062
  138.7 10.6 %collective-permute-start.14 = (bf16[4,272,256]{2,1,0:T(8,128)(2,1)}, bf16[4,272,256]{2,1,0:T(8,128)(2,1)}, u32[]{:S(2)}, u32[]{:S(2)}) collective-permute-start(bf16[4,272,256]{2,1,0:T(8,128)(2,1)} %all-to-all-done.4.refs_0_), channel_id=1, source_target_pairs={{0,4},{4,0},{1,5},{5,1},{2,6},{6,2},{3,7},{7,3},{8,12},{12,8},{9,1... | collective-permute-start | bytes 1671176 | tf_op jit(solution)/shard_map/ppermute | solution.py:1062
  145.7 31.7 %all-to-all-start.5 = ((bf16[4,128,2304]{2,1,0:T(8,128)(2,1)}), bf16[4,128,2304]{2,1,0:T(8,128)(2,1)S(1)}, u32[]{:S(2)}, u32[]{:S(2)}) async-start(bf16[4,128,2304]{2,1,0:T(8,128)(2,1)} %grads_a.1), calls=%async_computation.5 | async-start | bytes 4718592 | tf_op jit(solution)/shard_map/all_to_all | solution.py:1076
  177.4 10.3 %all-to-all-start.6 = ((bf16[8,64,256]{2,1,0:T(8,128)(2,1)}), bf16[8,64,256]{2,1,0:T(8,128)(2,1)S(1)}, u32[]{:S(2)}, u32[]{:S(2)}) async-start(bf16[8,64,256]{2,1,0:T(8,128)(2,1)} %get-tuple-element.155), calls=%async_computation.6 | async-start | bytes 524288 | tf_op jit(solution)/shard_map/all_to_all | solution.py:1080
  192.1 9.7 %all-to-all-start.7 = ((bf16[4,288,128]{2,1,0:T(8,128)(2,1)}), bf16[4,288,128]{2,1,0:T(8,128)(2,1)S(1)}, u32[]{:S(2)}, u32[]{:S(2)}) async-start(bf16[4,288,128]{2,1,0:T(8,128)(2,1)} %get-tuple-element.171), calls=%async_computation.7 | async-start | bytes 589824 | tf_op jit(solution)/shard_map/all_to_all | solution.py:1076
  201.8 26.9 %collective-permute-start.17 = (bf16[32,2816]{1,0:T(8,128)(2,1)S(1)}, bf16[32,2816]{1,0:T(8,128)(2,1)S(1)}, u32[]{:S(2)}, u32[]{:S(2)}) collective-permute-start(bf16[32,2816]{1,0:T(8,128)(2,1)S(1)} %copy-done.25), channel_id=1, source_target_pairs={{0,1},{1,0},{2,3},{3,2},{4,5},{5,4},{6,7},{7,6},{8,9},{9,8},{10,11... | collective-permute-start | bytes 540680 | tf_op jit(solution)/shard_map/ppermute | solution.py:1072
  201.9 26.8 %collective-permute-start.18 = (bf16[32,2816]{1,0:T(8,128)(2,1)S(1)}, bf16[32,2816]{1,0:T(8,128)(2,1)S(1)}, u32[]{:S(2)}, u32[]{:S(2)}) collective-permute-start(bf16[32,2816]{1,0:T(8,128)(2,1)S(1)} %copy-done.23), channel_id=1, source_target_pairs={{0,2},{1,3},{2,0},{3,1},{4,6},{5,7},{6,4},{7,5},{8,10},{9,11},{10,... | collective-permute-start | bytes 540680 | tf_op jit(solution)/shard_map/ppermute | solution.py:1072
  203.9 24.8 %collective-permute-start.19 = (bf16[32,2816]{1,0:T(8,128)(2,1)S(1)}, bf16[32,2816]{1,0:T(8,128)(2,1)S(1)}, u32[]{:S(2)}, u32[]{:S(2)}) collective-permute-start(bf16[32,2816]{1,0:T(8,128)(2,1)S(1)} %copy-done.21), channel_id=1, source_target_pairs={{0,3},{1,2},{2,1},{3,0},{4,7},{5,6},{6,5},{7,4},{8,11},{9,10},{10,... | collective-permute-start | bytes 540680 | tf_op jit(solution)/shard_map/ppermute | solution.py:1072
  206.3 26.0 %all-to-all-start.8 = ((bf16[8,64,1664]{2,1,0:T(8,128)(2,1)}), bf16[8,64,1664]{2,1,0:T(8,128)(2,1)S(1)}, u32[]{:S(2)}, u32[]{:S(2)}) async-start(bf16[8,64,1664]{2,1,0:T(8,128)(2,1)} %grads_b.1), calls=%async_computation.8 | async-start | bytes 3407872 | tf_op jit(solution)/shard_map/all_to_all | solution.py:1080
  232.2 24.9 %all-to-all-start.9 = ((bf16[8,192,256]{2,1,0:T(8,128)(2,1)}), bf16[8,192,256]{2,1,0:T(8,128)(2,1)S(1)}, u32[]{:S(2)}, u32[]{:S(2)}) async-start(bf16[8,192,256]{2,1,0:T(8,128)(2,1)} %pair_back.3.refs_0_), calls=%async_computation.9 | async-start | bytes 1572864 | tf_op jit(solution)/shard_map/all_to_all | solution.py:1080
  243.0 10.4 %collective-permute-start.21 = (bf16[16,2816]{1,0:T(8,128)(2,1)}, bf16[16,2816]{1,0:T(8,128)(2,1)S(1)}, u32[]{:S(2)}, u32[]{:S(2)}) collective-permute-start(bf16[16,2816]{1,0:T(8,128)(2,1)} %get-tuple-element.194), channel_id=1, source_target_pairs={{0,2},{1,3},{2,0},{3,1},{4,6},{5,7},{6,4},{7,5},{8,10},{9,11},{10,... | collective-permute-start | bytes 270344 | tf_op jit(solution)/shard_map/ppermute | solution.py:1072
  257.2 17.1 %all-to-all-start.10 = ((bf16[4,32,4224]{2,1,0:T(8,128)(2,1)}), bf16[4,32,4224]{2,1,0:T(8,128)(2,1)S(1)}, u32[]{:S(2)}, u32[]{:S(2)}) async-start(bf16[4,32,4224]{2,1,0:T(8,128)(2,1)} %add_shards.1), calls=%async_computation.10 | async-start | bytes 2162688 | tf_op jit(solution)/shard_map/all_to_all | solution.py:1076
  (44 other events, 199.0 us)

commit v4 on v3

--- a/solution.py
+++ b/solution.py
@@ -631,25 +631,21 @@
 
 
 def feed_forward(ids, first, cross_low, cross_mixed, lse, row_data, cross_q, wco, gs, cotangent, *refs):
-    slices = refs[0:2]
-    result, dealt, second_grad, keep, send, sums, slope, wins, wouts = refs[2:]
+    slices = refs[0:8]
+    result, dealt, second_grad, keep, send, sums, slope, wins, wouts = refs[8:]
     half_ff = FF // 2
-    for n, part in enumerate(slices):
-        core = ids[1] ^ n
-        for chip in range(4):
+    for n in range(2):
+        for k in range(4):
+            chip, core, part = ids[0] ^ k, ids[1] ^ n, slices[n * 4 + k]
             for e in range(4):
                 w, here = ids[2] ^ e, slice(e * 16, (e + 1) * 16)
                 rows = at16(w * 128 + (chip * 2 + core) * 16)
                 for g in range(4):
                     row = w * 256 + ((chip % 2) * 2 + core) * 64 + g * 16
-                    wouts[(chip // 2) ^ ids[1], at16(row), :] = part[
-                        chip, here, FF + g * D : FF + (g + 1) * D
-                    ]
+                    wouts[(chip // 2) ^ ids[1], at16(row), :] = part[here, FF + g * D : FF + (g + 1) * D]
                     for h in range(2):
                         column = g * 512 + h * 256
-                        wins[h ^ ids[1], rows, g * 256 : (g + 1) * 256] = part[
-                            chip, here, column : column + 256
-                        ]
+                        wins[h ^ ids[1], rows, g * 256 : (g + 1) * 256] = part[here, column : column + 256]
     gains, shifts = gs[0:3, :].astype(wide_t), gs[3:6, :].astype(wide_t)
     second, n1, s1 = layer_norm(
         first[...] + dot_nn(cross_low[...], wco[...]), gains[1:2], shifts[1:2]
@@ -1054,8 +1050,7 @@
     for e in range(4):
         here = slice(e * 16, (e + 1) * 16)
         one[here, :] = parts[e][:, :width]
-        for k in range(4):
-            two[k, here, :] = parts[e][:, width:]
+        two[here, :] = parts[e][:, width:]
 
 
 def core_swap(value):
@@ -1136,9 +1131,9 @@
         [order, ranks, thresholds],
         [((32, rows), wide_t)],
     )
-    part1, copies3 = run(
+    part1, part3 = run(
         pack_first,
-        [((64, 3 * D), low_t), ((4, 64, 2 * FF), low_t)],
+        [((64, 3 * D), low_t), ((64, 2 * FF), low_t)],
         ids,
         [after(shards1[0], x_own, cols, copies2)] + shards1[1:],
     )
@@ -1146,6 +1141,7 @@
     slices1 = slices1 + [core_swap(part) for part in slices1]
     shards2 = lax.all_to_all(after(copies2, x_own), "wa", 0, 0, tiled=True)
     x_other = core_swap(after(x_own, part1))
+    slices3 = chip_swaps([after(part3, slices1[1])] * 4)
     stream_own, stream_other = (x_own, 0), (x_other, 0)
     source_own, source_other = (x_own, 1), (x_other, 1)
 
@@ -1167,8 +1163,9 @@
         attend_scratch,
         us=15,
     )
-    shards2_other = core_swap(after(shards2, self_low))
-    slices3 = deal(after(copies3, shards2, self_low))
+    shards2_other = core_swap(after(shards2, self_low, *slices3))
+    slices3 = slices3 + [core_swap(after(part, self_low)) for part in slices3]
+    hidden_own = deal(after(hidden_copies, shards2, self_low, *slices3[:4]))
     (
         first,
         normed,
@@ -1195,8 +1192,7 @@
         attend_scratch,
         us=15,
     )
-    slices3_other = core_swap(after(slices3, cross_low))
-    hidden_own = deal(after(hidden_copies, slices3))
+    hidden_other = core_swap(after(hidden_own, cross_low))
     width_s = 2 * FF // 2 + 3 * D + D // 2
     result, cross_dealt, second_grad, keep_a, send_a, sums = run(
         feed_forward,
@@ -1209,8 +1205,8 @@
             ((8, D), wide_t),
         ],
         ids,
-        [first, cross_low, cross_mixed, cross_lse, row_data, cross_q, wco, gs]
-        + [cotangent[0], slices3, slices3_other],
+        [after(first, hidden_own), cross_low, cross_mixed, cross_lse, row_data, cross_q, wco, gs]
+        + [cotangent[0], *slices3],
         [((rows, FF), wide_t), ((2, D, FF // 2), low_t), ((2, FF // 2, D), low_t)],
         us=8,
     )
@@ -1223,14 +1219,14 @@
         [((PAIR, rows), wide_t)],
         us=4,
     )
-    both_own = deal(after(cross_dealt, hidden_own))
+    both_own = deal(cross_dealt)
     both_other = core_swap(after(both_own, cross_head[0]))
     width_a = FF // 2 + 2 * D + D // 2
     (dealt_a,) = run(
         grads_a,
         [((4, 128, width_a), low_t)],
         ids,
-        [keep_a, core_swap(after(send_a, hidden_own))],
+        [keep_a, core_swap(send_a)],
         [((D, FF // 2), low_t), ((FF // 2, D), low_t), ((D, D // 2), low_t)],
         us=6,
     )
@@ -1250,7 +1246,6 @@
         back_scratch,
         us=16,
     )
-    hidden_other = core_swap(after(hidden_own, both_own))
     self_head = run(
         functools.partial(pair_setup, True),
         [((8, rows, PAIR), low_t)] + head_shapes,
@@ -1265,7 +1260,7 @@
         ids,
         [cross_dkv, source_own, source_other],
     )
-    cross_back = deal_all(after(cross_dq_t, rows_a, self_head[0]))
+    cross_back = deal_all(after(cross_dq_t, rows_a, self_head[0], cross_dw))
     shards_a = run(
         add_chips,
         [((32, width_a + 512), low_t)] * 4,
@@ -1311,10 +1306,10 @@
         ids,
         [self_back_t, stream_own, stream_other, hidden_own, hidden_other],
     )
-    self_back = deal_all(after(self_back_t, rows_b, *moved_a))
     end_width = 2 * D + 2 * 128 + 12 * 128
     end_parts = run(end_sums, [((16, end_width), low_t)] * 4, ids, [rows_b, self_dw])
     moved_end = shard_swaps(end_parts)
+    self_back = deal_all(after(self_back_t, end_parts[0], *moved_a))
     (source_grad,) = run(
         source_back,
         [((rows, D), wide_t)],

time: 283 us -> 272 us (0.961)
  waiting for transfers between devices: 76.4 us -> 61.1 us
  local copies, waits for them, and re-layouts: 8.31 us -> 11.2 us
    all_to_all x7 -> x6, waiting for transfers between devices: 52.5 us -> 33.8 us  [deal(): return lax.all_to_all(value, 'chip', 0, 0, tiled=True)]
    ppermute x3 -> x6, waiting for transfers between devices: 8.87 us -> 16.3 us  [chip_swaps(): lax.ppermute(parts[k], 'chip', moves[k])]
    all_to_all x1, waiting for transfers between devices: 3.98 us -> 0.01 us  [fast_shards(): shards2 = lax.all_to_all(after(copies2, x_own), 'wa', 0, 0, tiled=True)]
    all_to_all x7 -> x6, starting transfers between devices: 28.3 us -> 24.7 us  [deal(): return lax.all_to_all(value, 'chip', 0, 0, tiled=True)]
    ppermute x3 -> x6, starting transfers between devices: 3.49 us -> 6.98 us  [chip_swaps(): lax.ppermute(parts[k], 'chip', moves[k])]
    unnamed x66 -> x74, local copies, waits for them, and re-layouts: 8.31 us -> 11.2 us
  transfers between devices with their start and end apart: 35 -> 40, of which waited for: 17 -> 11; matrix products, arithmetic and copies ran while one was open for 0% -> 0% of each run, Pallas kernels for 42% -> 40%
where the time goes in v4:
time: 272 us; the launch traced here: 271 us
  Pallas kernels  133 us (49%)
  starting transfers between devices  63.5 us (23%)
  waiting for transfers between devices  61.1 us (22%)
  local copies, waits for them, and re-layouts  11.2 us (4%)
    pallas_call x22, Pallas kernels, run(): pl.pallas_call(kernel, name=getattr(body, 'func', body).__name__, out_sha...  133 us
    all_to_all x6, waiting for transfers between devices, deal(): return lax.all_to_all(value, 'chip', 0, 0, tiled=True)  33.8 us
    all_to_all x6, starting transfers between devices, deal(): return lax.all_to_all(value, 'chip', 0, 0, tiled=True)  24.7 us
    ppermute x6, waiting for transfers between devices, chip_swaps(): lax.ppermute(parts[k], 'chip', moves[k])  16.3 us
    ppermute x9, starting transfers between devices, shard_swaps(): lax.ppermute(parts[k], 'wa', moves[k])  13.2 us
    unnamed x74, local copies, waits for them, and re-layouts  11.2 us
    all_to_all x3, starting transfers between devices, deal_all(): return lax.all_to_all(value, ('chip', 'core'), 0, 0, tiled=True)  11.1 us
    ppermute x6, starting transfers between devices, chip_swaps(): lax.ppermute(parts[k], 'chip', moves[k])  6.98 us
  transfers between devices with their start and end apart: 40, of which 11 were waited for; matrix products, arithmetic and copies ran while one was open for 0% of the time, Pallas kernels for 40%

profile of v4, /device:TPU:0, one launch (start us, length us, event | category | flops | bytes accessed | tf_op | source)
XLA Modules:
  0.0 270.6 jit_solution(7001442921761790271)
XLA Ops:
  4.9 5.3 %all-to-all-start = ((bf16[4,256,1024]{2,1,0:T(8,128)(2,1)}), bf16[4,256,1024]{2,1,0:T(8,128)(2,1)S(1)}, u32[]{:S(2)}, u32[]{:S(2)}) async-start(bf16[4,256,1024]{2,1,0:T(8,128)(2,1)} %get-tuple-element.113), calls=%async_computation | async-start | bytes 4194304 | tf_op jit(solution)/shard_map/all_to_all | solution.py:1071
  19.1 16.0 %all-to-all-done.refs_1_.refs_2_.refs_0_ = bf16[4,256,1024]{2,1,0:T(8,128)(2,1)S(1)} async-done(((bf16[4,256,1024]{2,1,0:T(8,128)(2,1)}), bf16[4,256,1024]{2,1,0:T(8,128)(2,1)S(1)}, u32[]{:S(2)}, u32[]{:S(2)}) %all-to-all-start) | async-done | bytes 2097184 | tf_op jit(solution)/shard_map/all_to_all | solution.py:1071
  38.7 5.0 %all-to-all-start.1 = ((bf16[4,64,2688]{2,1,0:T(8,128)(2,1)}), bf16[4,64,2688]{2,1,0:T(8,128)(2,1)S(1)}, u32[]{:S(2)}, u32[]{:S(2)}) async-start(bf16[4,64,2688]{2,1,0:T(8,128)(2,1)} %get-tuple-element.123), calls=%async_computation.1 | async-start | bytes 2752512 | tf_op jit(solution)/shard_map/all_to_all | solution.py:1142
  47.2 5.4 %collective-permute-done.6.refs_6_ = bf16[64,1536]{1,0:T(8,128)(2,1)S(1)} collective-permute-done((bf16[64,1536]{1,0:T(8,128)(2,1)}, bf16[64,1536]{1,0:T(8,128)(2,1)S(1)}, u32[]{:S(2)}, u32[]{:S(2)}) %collective-permute-start.6) | collective-permute-done | bytes 196640 | tf_op jit(solution)/shard_map/ppermute | solution.py:1062
  60.8 14.7 %self_forward.1 = (bf16[256,512]{1,0:T(8,128)(2,1)}, f32[256,512]{1,0:T(8,128)}, f32[8,256]{1,0:T(8,128)}, bf16[512,512]{1,0:T(8,128)(2,1)}, bf16[512,1024]{1,0:T(8,128)(2,1)}) custom-call(s32[7]{0:T(128)} %pad_add_fusion.ids, bf16[256,512]{1,0:T(8,128)(2,1)} %bitcast.16, bf16[4,256,1024]{2,1,0:T(8,128)(2,1)} %copy-done.1, ...), custom_call_target="tpu_custom_call" | custom-call | flops 15000000512 | bytes 8454144 | tf_op jit(solution)/shard_map/self_forward/pallas_call | solution.py:420
  75.5 7.4 %collective-permute-done.12.refs_11_ = bf16[64,4096]{1,0:T(8,128)(2,1)S(1)} collective-permute-done((bf16[64,4096]{1,0:T(8,128)(2,1)}, bf16[64,4096]{1,0:T(8,128)(2,1)S(1)}, u32[]{:S(2)}, u32[]{:S(2)}) %collective-permute-start.12) | collective-permute-done | bytes 524320 | tf_op jit(solution)/shard_map/ppermute | solution.py:1062
  83.9 4.4 %all-to-all-start.2 = ((bf16[4,256,512]{2,1,0:T(8,128)(2,1)}), bf16[4,256,512]{2,1,0:T(8,128)(2,1)}, u32[]{:S(2)}, u32[]{:S(2)}) async-start(bf16[4,256,512]{2,1,0:T(8,128)(2,1)} %get-tuple-element.129), calls=%async_computation.2 | async-start | bytes 2097152 | tf_op jit(solution)/shard_map/all_to_all | solution.py:1071
  90.5 15.9 %cross_forward.1 = (f32[256,512]{1,0:T(8,128)}, f32[256,512]{1,0:T(8,128)}, f32[256,128]{1,0:T(8,128)}, bf16[256,512]{1,0:T(8,128)(2,1)}, bf16[256,512]{1,0:T(8,...) custom-call(s32[7]{0:T(128)} %pad_add_fusion.ids, ...), custom_call_target="tpu_custom_call" | custom-call | flops 15000000512 | bytes 12664832 | tf_op jit(solution)/shard_map/cross_forward/pallas_call | solution.py:420
  106.4 10.3 %feed_forward.1 = (bf16[256,512]{1,0:T(8,128)(2,1)}, bf16[4,272,256]{2,1,0:T(8,128)(2,1)}, f32[256,512]{1,0:T(8,128)}, bf16[256,3840]{1,0:T(8,128)(2,1)}, bf16[256,3840]{1,0:T(8,128)(2,1)}, /*index=5*/f32[8,512]{1,0:T(8,128)}) custom-call(s32[7]{0:T(128)} %pad_add_fusion.ids, f32[256,512]{1,0:T(8,128)} %get-tuple-element.130.refs_0_, ...), custom_call_target="tpu_custom_call" | custom-call | flops 8000000000 | bytes 11894784 | tf_op jit(solution)/shard_map/feed_forward/pallas_call | solution.py:420
  121.0 4.8 %pair_setup.2 = (bf16[2048,128]{1,0:T(8,128)(2,1)}, bf16[2048,128]{1,0:T(8,128)(2,1)}, bf16[64,2048]{1,0:T(8,128)(2,1)}) custom-call(s32[7]{0:T(128)} %pad_add_fusion.ids, bf16[4,256,1024]{2,1,0:T(8,128)(2,1)} %copy-done.1, bf16[4,256,1024]{2,1,0:T(8,128)(2,1)} %collective-permute-done.3.refs_2_.refs_3_.refs_1_, ...), custom_call_target="tpu_custom_call" | custom-call | flops 4000000000 | bytes 6586368 | tf_op jit(solution)/shard_map/pair_setup/pallas_call | solution.py:420
  125.8 3.9 %all-to-all-done.3.refs_0_ = bf16[4,272,256]{2,1,0:T(8,128)(2,1)S(1)} async-done(((bf16[4,272,256]{2,1,0:T(8,128)(2,1)}), bf16[4,272,256]{2,1,0:T(8,128)(2,1)S(1)}, u32[]{:S(2)}, u32[]{:S(2)}) %all-to-all-start.3) | async-done | bytes 557088 | tf_op jit(solution)/shard_map/all_to_all | solution.py:1071
  131.2 5.1 %grads_a.1 = bf16[4,128,2304]{2,1,0:T(8,128)(2,1)} custom-call(s32[7]{0:T(128)} %pad_add_fusion.ids, bf16[256,3840]{1,0:T(8,128)(2,1)} %get-tuple-element.144.refs_0_, bf16[256,3840]{1,0:T(8,128)(2,1)} %copy-done.9), custom_call_target="tpu_custom_call" | custom-call | flops 6000000000 | bytes 6291456 | tf_op jit(solution)/shard_map/grads_a/pallas_call | solution.py:420
  140.7 14.8 %pair_back.2 = (bf16[8,64,256]{2,1,0:T(8,128)(2,1)}, bf16[8,128,256]{2,1,0:T(8,128)(2,1)}) custom-call(s32[7]{0:T(128)} %pad_add_fusion.ids, bf16[4,272,256]{2,1,0:T(8,128)(2,1)} %copy-done.6, bf16[4,272,256]{2,1,0:T(8,128)(2,1)} %copy-done.12, bf16[2048,128]{1,0:T(8,128)(2,1)} %get-tuple-element.149.refs_2_, bf16[2048,128]{1,0:T(8,128)(2,1)} %get-tuple-element.151.refs_3_, ...), custom_call_target="tpu_custom_call" | custom-call | flops 16000000000 | bytes 3211264 | tf_op jit(solution)/shard_map/pair_back/pallas_call | solution.py:420
  155.5 3.9 %pair_grads.2.refs_1_ = bf16[4,128,128]{2,1,0:T(8,128)(2,1)} custom-call(s32[7]{0:T(128)} %pad_add_fusion.ids, bf16[8,128,256]{2,1,0:T(8,128)(2,1)} %get-tuple-element.159.refs_0_.refs_5_, bf16[4,256,1024]{2,1,0:T(8,128)(2,1)} %copy-done.1, bf16[4,256,1024]{2,1,0:T(8,128)(2,1)} %collective-permute-done.3.refs_2_.refs_3_.refs_1_), custom_call_target="tpu_custom_call" | custom-call | flops 2000000000 | bytes 4849664 | tf_op jit(solution)/shard_map/pair_grads/pallas_call | solution.py:420
  159.4 6.2 %pair_setup.3 = (bf16[8,256,128]{2,1,0:T(8,128)(2,1)}, bf16[2048,128]{1,0:T(8,128)(2,1)}, bf16[2048,128]{1,0:T(8,128)(2,1)}, bf16[64,2048]{1,0:T(8,128)(2,1)}) custom-call(s32[7]{0:T(128)} %pad_add_fusion.ids, bf16[4,256,1024]{2,1,0:T(8,128)(2,1)} %copy-done.1, bf16[4,256,1024]{2,1,0:T(8,128)(2,1)} %collective-permute-done.3.refs_2_.refs_3_.refs_1_, ...), custom_call_target="tpu_custom_call" | custom-call | flops 4000000000 | bytes 9732096 | tf_op jit(solution)/shard_map/pair_setup/pallas_call | solution.py:420
  174.6 4.2 %all-to-all-done.5.refs_0_ = bf16[8,64,256]{2,1,0:T(8,128)(2,1)S(1)} async-done(((bf16[8,64,256]{2,1,0:T(8,128)(2,1)}), bf16[8,64,256]{2,1,0:T(8,128)(2,1)S(1)}, u32[]{:S(2)}, u32[]{:S(2)}) %all-to-all-start.5) | async-done | bytes 262176 | tf_op jit(solution)/shard_map/all_to_all | solution.py:1075
  196.5 3.8 %all-to-all-start.7 = ((bf16[8,64,1664]{2,1,0:T(8,128)(2,1)}), bf16[8,64,1664]{2,1,0:T(8,128)(2,1)S(1)}, u32[]{:S(2)}, u32[]{:S(2)}) async-start(bf16[8,64,1664]{2,1,0:T(8,128)(2,1)} %grads_b.1), calls=%async_computation.7 | async-start | bytes 3407872 | tf_op jit(solution)/shard_map/all_to_all | solution.py:1075
  201.1 18.1 %pair_back.3.refs_0_ = bf16[8,192,256]{2,1,0:T(8,128)(2,1)} custom-call(s32[7]{0:T(128)} %pad_add_fusion.ids, bf16[8,256,128]{2,1,0:T(8,128)(2,1)} %get-tuple-element.157.refs_0_, bf16[4,288,128]{2,1,0:T(8,128)(2,1)} %copy-done.7, bf16[4,288,128]{2,1,0:T(8,128)(2,1)} %copy-done.16, bf16[2048,128]{1,0:T(8,128)(2,1)} %get-tuple-element.182.refs_3_, ...), custom_call_target="tpu_custom_call" | custom-call | flops 16000000000 | bytes 3268608 | tf_op jit(solution)/shard_map/pair_back/pallas_call | solution.py:420
  219.1 4.9 %pair_grads.3.refs_1_ = bf16[4,192,128]{2,1,0:T(8,128)(2,1)} custom-call(s32[7]{0:T(128)} %pad_add_fusion.ids, bf16[8,192,256]{2,1,0:T(8,128)(2,1)} %pair_back.3.refs_0_, bf16[4,256,1024]{2,1,0:T(8,128)(2,1)} %copy-done.1, bf16[4,256,1024]{2,1,0:T(8,128)(2,1)} %collective-permute-done.3.refs_2_.refs_3_.refs_1_, ...), custom_call_target="tpu_custom_call" | custom-call | flops 2000000000 | bytes 7274496 | tf_op jit(solution)/shard_map/pair_grads/pallas_call | solution.py:420
  227.6 3.9 %all-to-all-start.8 = ((bf16[8,192,256]{2,1,0:T(8,128)(2,1)}), bf16[8,192,256]{2,1,0:T(8,128)(2,1)S(1)}, u32[]{:S(2)}, u32[]{:S(2)}) async-start(bf16[8,192,256]{2,1,0:T(8,128)(2,1)} %pair_back.3.refs_0_), calls=%async_computation.8 | async-start | bytes 1572864 | tf_op jit(solution)/shard_map/all_to_all | solution.py:1075
  238.9 4.1 %collective-permute-done.27.refs_6_ = bf16[16,2816]{1,0:T(8,128)(2,1)S(1)} collective-permute-done((bf16[16,2816]{1,0:T(8,128)(2,1)}, bf16[16,2816]{1,0:T(8,128)(2,1)S(1)}, u32[]{:S(2)}, u32[]{:S(2)}) %collective-permute-start.27) | collective-permute-done | bytes 90144 | tf_op jit(solution)/shard_map/ppermute | solution.py:1067
  246.8 4.2 %all-to-all-start.9 = ((bf16[4,32,4224]{2,1,0:T(8,128)(2,1)}), bf16[4,32,4224]{2,1,0:T(8,128)(2,1)S(1)}, u32[]{:S(2)}, u32[]{:S(2)}) async-start(bf16[4,32,4224]{2,1,0:T(8,128)(2,1)} %add_shards.1), calls=%async_computation.9 | async-start | bytes 2162688 | tf_op jit(solution)/shard_map/all_to_all | solution.py:1071
  254.2 8.6 %all-to-all-done.9.refs_0_ = bf16[4,32,4224]{2,1,0:T(8,128)(2,1)S(1)} async-done(((bf16[4,32,4224]{2,1,0:T(8,128)(2,1)}), bf16[4,32,4224]{2,1,0:T(8,128)(2,1)S(1)}, u32[]{:S(2)}, u32[]{:S(2)}) %all-to-all-start.9) | async-done | bytes 1081376 | tf_op jit(solution)/shard_map/all_to_all | solution.py:1071
  266.6 4.1 %place_all.1 = (f32[128,2048]{1,0:T(8,128)}, f32[512,512]{1,0:T(8,128)}, f32[128,512]{1,0:T(8,128)}, f32[128,1024]{1,0:T(8,128)}, f32[128,512]{1,0:T(8,128)}, /*...) custom-call(s32[7]{0:T(128)} %pad_add_fusion.ids, ...), custom_call_target="tpu_custom_call" | custom-call | flops 2000000000 | bytes 6360064 | tf_op jit(solution)/shard_map/place_all/pallas_call | solution.py:420
  (153 shorter events, 90.6 us)
Async XLA Ops:
  4.9 30.2 %all-to-all-start = ((bf16[4,256,1024]{2,1,0:T(8,128)(2,1)}), bf16[4,256,1024]{2,1,0:T(8,128)(2,1)S(1)}, u32[]{:S(2)}, u32[]{:S(2)}) async-start(bf16[4,256,1024]{2,1,0:T(8,128)(2,1)} %get-tuple-element.113), calls=%async_computation | async-start | bytes 4194304 | tf_op jit(solution)/shard_map/all_to_all | solution.py:1071
  10.2 24.9 %collective-permute-start.2 = (bf16[16,5632]{1,0:T(8,128)(2,1)S(1)}, bf16[16,5632]{1,0:T(8,128)(2,1)S(1)}, u32[]{:S(2)}, u32[]{:S(2)}) collective-permute-start(bf16[16,5632]{1,0:T(8,128)(2,1)S(1)} %copy-done.30), channel_id=1, source_target_pairs={{0,3},{1,2},{2,1},{3,0},{4,7},{5,6},{6,5},{7,4},{8,11},{9,10},{10,... | collective-permute-start | bytes 540680 | tf_op jit(solution)/shard_map/ppermute | solution.py:1067
  13.8 21.3 %collective-permute-start.1 = (bf16[16,5632]{1,0:T(8,128)(2,1)S(1)}, bf16[16,5632]{1,0:T(8,128)(2,1)S(1)}, u32[]{:S(2)}, u32[]{:S(2)}) collective-permute-start(bf16[16,5632]{1,0:T(8,128)(2,1)S(1)} %copy-done.30), channel_id=1, source_target_pairs={{0,2},{1,3},{2,0},{3,1},{4,6},{5,7},{6,4},{7,5},{8,10},{9,11},{10,... | collective-permute-start | bytes 540680 | tf_op jit(solution)/shard_map/ppermute | solution.py:1067
  13.8 21.3 %collective-permute-start = (bf16[16,5632]{1,0:T(8,128)(2,1)S(1)}, bf16[16,5632]{1,0:T(8,128)(2,1)S(1)}, u32[]{:S(2)}, u32[]{:S(2)}) collective-permute-start(bf16[16,5632]{1,0:T(8,128)(2,1)S(1)} %copy-done.30), channel_id=1, source_target_pairs={{0,1},{1,0},{2,3},{3,2},{4,5},{5,4},{6,7},{7,6},{8,9},{9,8},{10,11... | collective-permute-start | bytes 540680 | tf_op jit(solution)/shard_map/ppermute | solution.py:1067
  38.7 21.4 %collective-permute-start.3 = (bf16[4,256,1024]{2,1,0:T(8,128)(2,1)S(1)}, bf16[4,256,1024]{2,1,0:T(8,128)(2,1)}, u32[]{:S(2)}, u32[]{:S(2)}) collective-permute-start(bf16[4,256,1024]{2,1,0:T(8,128)(2,1)S(1)} %all-to-all-done.refs_1_.refs_2_.refs_0_), channel_id=1, source_target_pairs={{0,4},{4,0},{1,5},{5,1},{2,6},{6,2},{3,7},{7,3},{8,12},{12,8},{9,1... | collective-permute-start | bytes 6291464 | tf_op jit(solution)/shard_map/ppermute | solution.py:1057
  38.7 45.0 %all-to-all-start.1 = ((bf16[4,64,2688]{2,1,0:T(8,128)(2,1)}), bf16[4,64,2688]{2,1,0:T(8,128)(2,1)S(1)}, u32[]{:S(2)}, u32[]{:S(2)}) async-start(bf16[4,64,2688]{2,1,0:T(8,128)(2,1)} %get-tuple-element.123), calls=%async_computation.1 | async-start | bytes 2752512 | tf_op jit(solution)/shard_map/all_to_all | solution.py:1142
  56.6 18.9 %collective-permute-start.13 = (bf16[64,4096]{1,0:T(8,128)(2,1)}, bf16[64,4096]{1,0:T(8,128)(2,1)S(1)}, u32[]{:S(2)}, u32[]{:S(2)}) collective-permute-start(bf16[64,4096]{1,0:T(8,128)(2,1)} %get-tuple-element.137.refs_9_), channel_id=1, source_target_pairs={{0,24},{8,16},{16,8},{24,0},{1,25},{9,17},{17,9},{25,1},{2,26},{10... | collective-permute-start | bytes 1572872 | tf_op jit(solution)/shard_map/ppermute | solution.py:1062
  58.0 24.8 %collective-permute-start.12 = (bf16[64,4096]{1,0:T(8,128)(2,1)}, bf16[64,4096]{1,0:T(8,128)(2,1)S(1)}, u32[]{:S(2)}, u32[]{:S(2)}) collective-permute-start(bf16[64,4096]{1,0:T(8,128)(2,1)} %get-tuple-element.137.refs_9_), channel_id=1, source_target_pairs={{0,16},{8,24},{16,0},{24,8},{1,17},{9,25},{17,1},{25,9},{2,18},{10... | collective-permute-start | bytes 1572872 | tf_op jit(solution)/shard_map/ppermute | solution.py:1062
  59.5 24.2 %collective-permute-start.11 = (bf16[64,4096]{1,0:T(8,128)(2,1)}, bf16[64,4096]{1,0:T(8,128)(2,1)}, u32[]{:S(2)}, u32[]{:S(2)}) collective-permute-start(bf16[64,4096]{1,0:T(8,128)(2,1)} %get-tuple-element.137.refs_9_), channel_id=1, source_target_pairs={{0,8},{8,0},{16,24},{24,16},{1,9},{9,1},{17,25},{25,17},{2,10},{10... | collective-permute-start | bytes 1572872 | tf_op jit(solution)/shard_map/ppermute | solution.py:1062
  83.9 22.5 %all-to-all-start.2 = ((bf16[4,256,512]{2,1,0:T(8,128)(2,1)}), bf16[4,256,512]{2,1,0:T(8,128)(2,1)}, u32[]{:S(2)}, u32[]{:S(2)}) async-start(bf16[4,256,512]{2,1,0:T(8,128)(2,1)} %get-tuple-element.129), calls=%async_computation.2 | async-start | bytes 2097152 | tf_op jit(solution)/shard_map/all_to_all | solution.py:1071
  88.3 18.0 %collective-permute-start.15 = (bf16[64,4096]{1,0:T(8,128)(2,1)S(1)}, bf16[64,4096]{1,0:T(8,128)(2,1)}, u32[]{:S(2)}, u32[]{:S(2)}) collective-permute-start(bf16[64,4096]{1,0:T(8,128)(2,1)S(1)} %copy-done.13), channel_id=1, source_target_pairs={{0,4},{4,0},{1,5},{5,1},{2,6},{6,2},{3,7},{7,3},{8,12},{12,8},{9,1... | collective-permute-start | bytes 1572872 | tf_op jit(solution)/shard_map/ppermute | solution.py:1057
  88.8 17.6 %collective-permute-start.16 = (bf16[64,4096]{1,0:T(8,128)(2,1)}, bf16[64,4096]{1,0:T(8,128)(2,1)}, u32[]{:S(2)}, u32[]{:S(2)}) collective-permute-start(bf16[64,4096]{1,0:T(8,128)(2,1)} %collective-permute-done.11.refs_10_), channel_id=1, source_target_pairs={{0,4},{4,0},{1,5},{5,1},{2,6},{6,2},{3,7},{7,3},{8,12},{12,8},{9,1... | collective-permute-start | bytes 1572872 | tf_op jit(solution)/shard_map/ppermute | solution.py:1057
  88.9 17.5 %collective-permute-start.17 = (bf16[64,4096]{1,0:T(8,128)(2,1)}, bf16[64,4096]{1,0:T(8,128)(2,1)}, u32[]{:S(2)}, u32[]{:S(2)}) collective-permute-start(bf16[64,4096]{1,0:T(8,128)(2,1)} %copy-done.15), channel_id=1, source_target_pairs={{0,4},{4,0},{1,5},{5,1},{2,6},{6,2},{3,7},{7,3},{8,12},{12,8},{9,1... | collective-permute-start | bytes 1572872 | tf_op jit(solution)/shard_map/ppermute | solution.py:1057
  89.3 17.1 %collective-permute-start.18 = (bf16[64,4096]{1,0:T(8,128)(2,1)}, bf16[64,4096]{1,0:T(8,128)(2,1)}, u32[]{:S(2)}, u32[]{:S(2)}) collective-permute-start(bf16[64,4096]{1,0:T(8,128)(2,1)} %copy-done.14), channel_id=1, source_target_pairs={{0,4},{4,0},{1,5},{5,1},{2,6},{6,2},{3,7},{7,3},{8,12},{12,8},{9,1... | collective-permute-start | bytes 1572872 | tf_op jit(solution)/shard_map/ppermute | solution.py:1057
  116.7 13.1 %collective-permute-start.19 = (bf16[256,3840]{1,0:T(8,128)(2,1)}, bf16[256,3840]{1,0:T(8,128)(2,1)S(1)}, u32[]{:S(2)}, u32[]{:S(2)}) collective-permute-start(bf16[256,3840]{1,0:T(8,128)(2,1)} %get-tuple-element.145), channel_id=1, source_target_pairs={{0,4},{4,0},{1,5},{5,1},{2,6},{6,2},{3,7},{7,3},{8,12},{12,8},{9,1... | collective-permute-start | bytes 5898248 | tf_op jit(solution)/shard_map/ppermute | solution.py:1057
  117.2 12.6 %all-to-all-start.3 = ((bf16[4,272,256]{2,1,0:T(8,128)(2,1)}), bf16[4,272,256]{2,1,0:T(8,128)(2,1)S(1)}, u32[]{:S(2)}, u32[]{:S(2)}) async-start(bf16[4,272,256]{2,1,0:T(8,128)(2,1)} %get-tuple-element.143), calls=%async_computation.3 | async-start | bytes 1114112 | tf_op jit(solution)/shard_map/all_to_all | solution.py:1071
  120.9 38.5 %collective-permute-start.21 = (bf16[4,256,512]{2,1,0:T(8,128)(2,1)}, bf16[4,256,512]{2,1,0:T(8,128)(2,1)}, u32[]{:S(2)}, u32[]{:S(2)}) collective-permute-start(bf16[4,256,512]{2,1,0:T(8,128)(2,1)} %all-to-all-done.2.refs_4_.refs_3_), channel_id=1, source_target_pairs={{0,4},{4,0},{1,5},{5,1},{2,6},{6,2},{3,7},{7,3},{8,12},{12,8},{9,1... | collective-permute-start | bytes 3145736 | tf_op jit(solution)/shard_map/ppermute | solution.py:1057
  136.3 32.2 %all-to-all-start.4 = ((bf16[4,128,2304]{2,1,0:T(8,128)(2,1)}), bf16[4,128,2304]{2,1,0:T(8,128)(2,1)S(1)}, u32[]{:S(2)}, u32[]{:S(2)}) async-start(bf16[4,128,2304]{2,1,0:T(8,128)(2,1)} %grads_a.1), calls=%async_computation.4 | async-start | bytes 4718592 | tf_op jit(solution)/shard_map/all_to_all | solution.py:1071
  192.0 35.5 %collective-permute-start.23 = (bf16[32,2816]{1,0:T(8,128)(2,1)S(1)}, bf16[32,2816]{1,0:T(8,128)(2,1)S(1)}, u32[]{:S(2)}, u32[]{:S(2)}) collective-permute-start(bf16[32,2816]{1,0:T(8,128)(2,1)S(1)} %copy-done.26), channel_id=1, source_target_pairs={{0,1},{1,0},{2,3},{3,2},{4,5},{5,4},{6,7},{7,6},{8,9},{9,8},{10,11... | collective-permute-start | bytes 540680 | tf_op jit(solution)/shard_map/ppermute | solution.py:1067
  193.8 33.7 %collective-permute-start.24 = (bf16[32,2816]{1,0:T(8,128)(2,1)S(1)}, bf16[32,2816]{1,0:T(8,128)(2,1)S(1)}, u32[]{:S(2)}, u32[]{:S(2)}) collective-permute-start(bf16[32,2816]{1,0:T(8,128)(2,1)S(1)} %copy-done.25), channel_id=1, source_target_pairs={{0,2},{1,3},{2,0},{3,1},{4,6},{5,7},{6,4},{7,5},{8,10},{9,11},{10,... | collective-permute-start | bytes 540680 | tf_op jit(solution)/shard_map/ppermute | solution.py:1067
  196.2 31.4 %collective-permute-start.25 = (bf16[32,2816]{1,0:T(8,128)(2,1)S(1)}, bf16[32,2816]{1,0:T(8,128)(2,1)S(1)}, u32[]{:S(2)}, u32[]{:S(2)}) collective-permute-start(bf16[32,2816]{1,0:T(8,128)(2,1)S(1)} %copy-done.24), channel_id=1, source_target_pairs={{0,3},{1,2},{2,1},{3,0},{4,7},{5,6},{6,5},{7,4},{8,11},{9,10},{10,... | collective-permute-start | bytes 540680 | tf_op jit(solution)/shard_map/ppermute | solution.py:1067
  196.5 27.6 %all-to-all-start.7 = ((bf16[8,64,1664]{2,1,0:T(8,128)(2,1)}), bf16[8,64,1664]{2,1,0:T(8,128)(2,1)S(1)}, u32[]{:S(2)}, u32[]{:S(2)}) async-start(bf16[8,64,1664]{2,1,0:T(8,128)(2,1)} %grads_b.1), calls=%async_computation.7 | async-start | bytes 3407872 | tf_op jit(solution)/shard_map/all_to_all | solution.py:1075
  227.6 19.2 %all-to-all-start.8 = ((bf16[8,192,256]{2,1,0:T(8,128)(2,1)}), bf16[8,192,256]{2,1,0:T(8,128)(2,1)S(1)}, u32[]{:S(2)}, u32[]{:S(2)}) async-start(bf16[8,192,256]{2,1,0:T(8,128)(2,1)} %pair_back.3.refs_0_), calls=%async_computation.8 | async-start | bytes 1572864 | tf_op jit(solution)/shard_map/all_to_all | solution.py:1075
  246.8 16.1 %all-to-all-start.9 = ((bf16[4,32,4224]{2,1,0:T(8,128)(2,1)}), bf16[4,32,4224]{2,1,0:T(8,128)(2,1)S(1)}, u32[]{:S(2)}, u32[]{:S(2)}) async-start(bf16[4,32,4224]{2,1,0:T(8,128)(2,1)} %add_shards.1), calls=%async_computation.9 | async-start | bytes 2162688 | tf_op jit(solution)/shard_map/all_to_all | solution.py:1071
  (53 other events, 277.5 us)
